TPU v7x, 32 devices: a whole 2x2x4 slice. The times are simulated.
32 devices in a mesh: fsdp: 8 (over z, x), ctx: 2 (over y), tp: 2 (over core).
Axes of the slice: x: 2, y: 2, z: 4, core: 2. Of those that a mesh axis runs over, the one named last changes fastest.
Arguments:
- tokens: bfloat16 [8, 2048, 768], P('fsdp', ('ctx', 'tp')), may hold values from -6 to 6
- segment_order: int32 [8, 4], P('fsdp'), may hold values from 0 to 3, each once within a row
- ln1_gain: bfloat16 [768], P('fsdp'), may hold values from 0.25 to 1.75
- ln1_bias: bfloat16 [768], P('fsdp'), may hold values from -1.75 to 1.75
- qkv_weight: bfloat16 [3, 768, 768], P(None, 'fsdp', 'tp'), may hold values from -0.21875 to 0.21875
- qv_bias: bfloat16 [2, 12, 64], P(None, 'tp', 'fsdp'), may hold values from -1.75 to 1.75
- out_weight: bfloat16 [768, 768], P('tp', 'fsdp'), may hold values from -3.5 to 3.5
- out_bias: bfloat16 [768], P('fsdp'), may hold values from -1.75 to 1.75
- ln2_gain: bfloat16 [768], P('fsdp'), may hold values from 0.25 to 1.75
- ln2_bias: bfloat16 [768], P('fsdp'), may hold values from -1.75 to 1.75
- up_weight: bfloat16 [768, 3072], P('fsdp', 'tp'), may hold values from -0.21875 to 0.21875
- up_bias: bfloat16 [48, 64], P('tp', 'fsdp'), may hold values from -1.75 to 1.75
- down_weight: bfloat16 [3072, 768], P('tp', 'fsdp'), may hold values from -0.109375 to 0.109375
- down_bias: bfloat16 [768], P('fsdp'), may hold values from -1.75 to 1.75
- cotangent: bfloat16 [8, 2048, 768], P('fsdp', ('ctx', 'tp')), may hold values from -6 to 6
Outputs:
- output: bfloat16 [8, 2048, 768], P('fsdp', ('ctx', 'tp'))
- tokens_grad: bfloat16 [8, 2048, 768], P('fsdp', ('ctx', 'tp'))
- ln1_gain_grad: float32 [768], P('fsdp')
- ln1_bias_grad: float32 [768], P('fsdp')
- qkv_weight_grad: float32 [3, 768, 768], P(None, 'fsdp', 'tp')
- qv_bias_grad: float32 [2, 12, 64], P(None, 'tp', 'fsdp')
- out_weight_grad: float32 [768, 768], P('tp', 'fsdp')
- out_bias_grad: float32 [768], P('fsdp')
- ln2_gain_grad: float32 [768], P('fsdp')
- ln2_bias_grad: float32 [768], P('fsdp')
- up_weight_grad: float32 [768, 3072], P('fsdp', 'tp')
- up_bias_grad: float32 [48, 64], P('tp', 'fsdp')
- down_weight_grad: float32 [3072, 768], P('tp', 'fsdp')
- down_bias_grad: float32 [768], P('fsdp')
Inputs may be any that keep to these rules, and one draw needn't show every extreme that they name: Each row is a permutation; stored segment c of sequence s (rows c * 512 onward) holds the tokens at places segment_order[s, c] * 512 onward.
All inputs are finite; a program needn't handle non-finite values.
Results may differ from a plain program's by a relative error of at most 0.02.
Values may be sent and summed in bfloat16 or wider, within the bound.
A program may use at most 192 MiB of HBM per device.

v0:
```python
from functools import partial

import jax
import jax.numpy as jnp
from jax import lax
from jax.sharding import PartitionSpec as P

EPSILON = 1e-05
MASKED = -1e30


def norm_rows(values, gain, shift):
    average = jnp.mean(values, axis=-1, keepdims=True)
    centred = values - average
    spread = jnp.mean(centred * centred, axis=-1, keepdims=True)
    return centred * lax.rsqrt(spread + EPSILON) * gain + shift


def norm_back(values, gain, shift, upstream):
    unused, pullback = jax.vjp(norm_rows, values, gain, shift)
    return pullback(upstream)


def split_heads(matrix, head_count):
    return matrix.reshape(matrix.shape[0], head_count, -1)


def score_rows(query_rows, key_rows, query_places, key_places, head_count):
    query_heads = split_heads(query_rows, head_count)
    key_heads = split_heads(key_rows, head_count)
    score_scale = query_heads.shape[-1] ** (-0.5)
    scores = (
        jnp.einsum("qhd,khd->hqk", query_heads, key_heads, preferred_element_type=jnp.float32)
        * score_scale
    )
    allowed = key_places[None, None, :] <= query_places[None, :, None]
    return jnp.where(allowed, scores, MASKED)


def score_grads(
    query_rows,
    grad_rows,
    lse_rows,
    key_rows,
    value_rows,
    query_places,
    key_places,
    head_count,
    delta_rows,
):
    probabilities = jnp.exp(
        score_rows(query_rows, key_rows, query_places, key_places, head_count)
        - lse_rows[:, :, None]
    )
    upstream = jnp.einsum(
        "qhd,khd->hqk",
        split_heads(grad_rows, head_count),
        split_heads(value_rows, head_count),
        preferred_element_type=jnp.float32,
    )
    delta_rows = jnp.sum(probabilities * upstream, axis=-1)
    scaled = (probabilities * (upstream - delta_rows[:, :, None])).astype(jnp.bfloat16)
    return (probabilities.astype(jnp.bfloat16), scaled, delta_rows)


def key_terms(scaled, weights_low, query_block, grad_block, head_count):
    query_heads = split_heads(query_block, head_count)
    score_scale = query_heads.shape[-1] ** (-0.5)
    key_term = (
        jnp.einsum("hqk,qhd->khd", scaled, query_heads, preferred_element_type=jnp.float32)
        * score_scale
    )
    value_term = jnp.einsum(
        "hqk,qhd->khd",
        weights_low,
        split_heads(grad_block, head_count),
        preferred_element_type=jnp.float32,
    )
    return (key_term.reshape(key_term.shape[0], -1), value_term.reshape(value_term.shape[0], -1))


def query_term(scaled, key_rows, head_count):
    key_heads = split_heads(key_rows, head_count)
    score_scale = key_heads.shape[-1] ** (-0.5)
    query_grad = (
        jnp.einsum("hqk,khd->qhd", scaled, key_heads, preferred_element_type=jnp.float32)
        * score_scale
    )
    return query_grad.reshape(query_grad.shape[0], -1)


def row_blocks(row_count):
    block_rows = min(512, row_count)
    return (block_rows, row_count // block_rows)


def sequence_forward(head_count, bundle):
    query_rows, key_rows, value_rows, query_places, key_places = bundle
    row_count, inner_width = query_rows.shape
    block_rows, block_count = row_blocks(row_count)

    def block_step(piece):
        query_block, place_block = piece
        scores = score_rows(query_block, key_rows, place_block, key_places, head_count)
        row_peak = jnp.max(scores, axis=-1, keepdims=True)
        shifted = jnp.exp(scores - row_peak)
        row_total = jnp.sum(shifted, axis=-1, keepdims=True)
        weights_low = (shifted / row_total).astype(jnp.bfloat16)
        mixed_heads = jnp.einsum(
            "hqk,khd->qhd",
            weights_low,
            split_heads(value_rows, head_count),
            preferred_element_type=jnp.float32,
        )
        return (
            mixed_heads.reshape(block_rows, inner_width).astype(jnp.bfloat16),
            (row_peak + jnp.log(row_total))[:, :, 0],
        )

    mixed_heads, lse_rows = lax.map(
        block_step,
        (
            query_rows.reshape(block_count, block_rows, inner_width),
            query_places.reshape(block_count, block_rows),
        ),
    )
    return (
        mixed_heads.reshape(row_count, inner_width),
        jnp.swapaxes(lse_rows, 0, 1).reshape(head_count, row_count),
    )


def sequence_back(head_count, bundle):
    query_rows, grad_rows, lse_rows, key_rows, value_rows, query_places, key_places = bundle
    row_count, inner_width = query_rows.shape
    block_rows, block_count = row_blocks(row_count)

    def block_step(running, piece):
        query_block, grad_block, lse_block, place_block = piece
        weights_low, scaled, unused = score_grads(
            query_block,
            grad_block,
            lse_block,
            key_rows,
            value_rows,
            place_block,
            key_places,
            head_count,
            None,
        )
        key_term, value_term = key_terms(scaled, weights_low, query_block, grad_block, head_count)
        return (
            (running[0] + key_term, running[1] + value_term),
            query_term(scaled, key_rows, head_count),
        )

    zero_sum = jnp.zeros(key_rows.shape, jnp.float32)
    pieces = (
        query_rows.reshape(block_count, block_rows, inner_width),
        grad_rows.reshape(block_count, block_rows, inner_width),
        jnp.swapaxes(lse_rows.reshape(head_count, block_count, block_rows), 0, 1),
        query_places.reshape(block_count, block_rows),
    )
    (key_sum, value_sum), query_grad = lax.scan(block_step, (zero_sum, zero_sum), pieces)
    return (query_grad.reshape(row_count, inner_width), key_sum, value_sum)


def local(
    tokens,
    segment_order,
    ln1_gain,
    ln1_bias,
    qkv_weight,
    qv_bias,
    out_weight,
    out_bias,
    ln2_gain,
    ln2_bias,
    up_weight,
    up_bias,
    down_weight,
    down_bias,
    cotangent,
):
    (
        qkv_full,
        qv_full,
        out_full,
        up_full,
        upb_full,
        down_full,
        gain_one,
        shift_one,
        outb_full,
        gain_two,
        shift_two,
        downb_full,
    ) = (
        lax.all_gather(qkv_weight, "fsdp", axis=1, tiled=True),
        lax.all_gather(qv_bias, "fsdp", axis=2, tiled=True),
        lax.all_gather(out_weight, "fsdp", axis=1, tiled=True),
        lax.all_gather(up_weight, "fsdp", axis=0, tiled=True),
        lax.all_gather(up_bias, "fsdp", axis=1, tiled=True),
        lax.all_gather(down_weight, "fsdp", axis=1, tiled=True),
        lax.all_gather(ln1_gain, "fsdp", axis=0, tiled=True),
        lax.all_gather(ln1_bias, "fsdp", axis=0, tiled=True),
        lax.all_gather(out_bias, "fsdp", axis=0, tiled=True),
        lax.all_gather(ln2_gain, "fsdp", axis=0, tiled=True),
        lax.all_gather(ln2_bias, "fsdp", axis=0, tiled=True),
        lax.all_gather(down_bias, "fsdp", axis=0, tiled=True),
    )
    seq_count, half_rows, model_width = tokens.shape
    local_rows = half_rows * lax.axis_size("tp")
    head_count = qv_full.shape[1]
    inner_width = qkv_full.shape[2]
    residual_in = tokens.astype(jnp.float32)
    normed_one = norm_rows(residual_in, gain_one, shift_one).astype(jnp.bfloat16)
    rows_one, grad_rows = (
        lax.all_gather(normed_one, "tp", axis=1, tiled=True),
        lax.all_gather(cotangent, "tp", axis=1, tiled=True),
    )
    flat_one = rows_one.reshape(-1, model_width)
    projected = jnp.einsum("rd,jde->jre", flat_one, qkv_full, preferred_element_type=jnp.float32)
    head_shape = (seq_count, local_rows, inner_width)
    queries = (projected[0] + qv_full[0].reshape(-1)).astype(jnp.bfloat16).reshape(head_shape)
    key_rows = projected[1].astype(jnp.bfloat16).reshape(head_shape)
    value_rows = (projected[2] + qv_full[1].reshape(-1)).astype(jnp.bfloat16).reshape(head_shape)
    keys_all, values_all = (
        lax.all_gather(key_rows, "ctx", axis=1, tiled=True),
        lax.all_gather(value_rows, "ctx", axis=1, tiled=True),
    )
    total_len = keys_all.shape[1]
    segment_count = segment_order.shape[1]
    segment_size = total_len // segment_count
    spread_order = jnp.broadcast_to(
        segment_order[:, :, None], (seq_count, segment_count, segment_size)
    ).reshape(seq_count, total_len)
    key_places = (
        spread_order * segment_size
        + (jnp.arange(total_len, dtype=jnp.int32) % segment_size)[None, :]
    )
    query_places = lax.dynamic_slice_in_dim(
        key_places, lax.axis_index("ctx") * local_rows, local_rows, 1
    )
    mixed_heads, lse_rows = lax.map(
        partial(sequence_forward, head_count),
        (queries, keys_all, values_all, query_places, key_places),
    )
    mixed_flat = mixed_heads.reshape(-1, inner_width)
    attn_terms = jnp.dot(mixed_flat, out_full, preferred_element_type=jnp.float32).reshape(
        seq_count, local_rows, model_width
    )
    attn_part = lax.psum_scatter(
        attn_terms.astype(jnp.bfloat16), "tp", scatter_dimension=1, tiled=True
    ).astype(jnp.float32)
    resid_mid = residual_in + attn_part + outb_full
    normed_two = norm_rows(resid_mid, gain_two, shift_two).astype(jnp.bfloat16)
    rows_two = lax.all_gather(normed_two, "tp", axis=1, tiled=True)
    flat_two = rows_two.reshape(-1, model_width)
    pre_act = jnp.dot(flat_two, up_full, preferred_element_type=jnp.float32) + upb_full.reshape(-1)
    activated = jax.nn.gelu(pre_act, approximate=True).astype(jnp.bfloat16)
    mlp_terms = jnp.dot(activated, down_full, preferred_element_type=jnp.float32).reshape(
        seq_count, local_rows, model_width
    )
    mlp_part = lax.psum_scatter(
        mlp_terms.astype(jnp.bfloat16), "tp", scatter_dimension=1, tiled=True
    ).astype(jnp.float32)
    output = (resid_mid + mlp_part + downb_full).astype(jnp.bfloat16)
    upstream = cotangent.astype(jnp.float32)
    grad_flat = grad_rows.reshape(-1, model_width)
    downb_grad = jnp.sum(upstream, axis=(0, 1))
    down_grad = jnp.einsum("rf,rd->fd", activated, grad_flat, preferred_element_type=jnp.float32)
    act_grad = jnp.einsum("rd,fd->rf", grad_flat, down_full, preferred_element_type=jnp.float32)
    unused, gelu_pull = jax.vjp(partial(jax.nn.gelu, approximate=True), pre_act)
    pre_grad = gelu_pull(act_grad)[0].astype(jnp.bfloat16)
    upb_grad = jnp.sum(pre_grad.astype(jnp.float32), axis=0).reshape(upb_full.shape)
    up_grad = jnp.einsum("rd,rf->df", flat_two, pre_grad, preferred_element_type=jnp.float32)
    norm_two_terms = jnp.einsum(
        "rf,df->rd", pre_grad, up_full, preferred_element_type=jnp.float32
    ).reshape(seq_count, local_rows, model_width)
    norm_two_grad = lax.psum_scatter(
        norm_two_terms.astype(jnp.bfloat16), "tp", scatter_dimension=1, tiled=True
    ).astype(jnp.float32)
    mid_grad, gain_two_grad, shift_two_grad = norm_back(
        resid_mid, gain_two, shift_two, norm_two_grad
    )
    resid_grad = upstream + mid_grad
    outb_grad = jnp.sum(resid_grad, axis=(0, 1))
    branch_grad = lax.all_gather(resid_grad.astype(jnp.bfloat16), "tp", axis=1, tiled=True)
    branch_flat = branch_grad.reshape(-1, model_width)
    out_grad = jnp.einsum("re,rd->ed", mixed_flat, branch_flat, preferred_element_type=jnp.float32)
    mixed_grad = (
        jnp.einsum("rd,ed->re", branch_flat, out_full, preferred_element_type=jnp.float32)
        .astype(jnp.bfloat16)
        .reshape(head_shape)
    )
    query_grad, key_partial, value_partial = lax.map(
        partial(sequence_back, head_count),
        (queries, mixed_grad, lse_rows, keys_all, values_all, query_places, key_places),
    )
    key_grad, value_grad = (
        lax.psum_scatter(
            key_partial.astype(jnp.bfloat16), "ctx", scatter_dimension=1, tiled=True
        ).astype(jnp.float32),
        lax.psum_scatter(
            value_partial.astype(jnp.bfloat16), "ctx", scatter_dimension=1, tiled=True
        ).astype(jnp.float32),
    )
    stacked = jnp.stack(
        [
            query_grad.astype(jnp.bfloat16),
            key_grad.astype(jnp.bfloat16),
            value_grad.astype(jnp.bfloat16),
        ]
    ).reshape(3, -1, inner_width)
    qkv_grad = jnp.einsum("rd,jre->jde", flat_one, stacked, preferred_element_type=jnp.float32)
    qv_grad = jnp.stack(
        [
            jnp.sum(stacked[0].astype(jnp.float32), axis=0),
            jnp.sum(stacked[2].astype(jnp.float32), axis=0),
        ]
    ).reshape(qv_full.shape)
    norm_one_terms = jnp.einsum(
        "jre,jde->rd", stacked, qkv_full, preferred_element_type=jnp.float32
    ).reshape(seq_count, local_rows, model_width)
    norm_one_grad = lax.psum_scatter(
        norm_one_terms.astype(jnp.bfloat16), "tp", scatter_dimension=1, tiled=True
    ).astype(jnp.float32)
    input_part, gain_one_grad, shift_one_grad = norm_back(
        residual_in, gain_one, shift_one, norm_one_grad
    )
    tokens_grad = (resid_grad + input_part).astype(jnp.bfloat16)
    small_grads = jnp.stack(
        [gain_one_grad, shift_one_grad, outb_grad, gain_two_grad, shift_two_grad, downb_grad]
    )
    small_total = lax.psum(small_grads, "tp")
    shards = (
        lax.psum_scatter(
            qkv_grad.astype(jnp.bfloat16), "fsdp", scatter_dimension=1, tiled=True
        ).astype(jnp.float32),
        lax.psum_scatter(
            qv_grad.astype(jnp.bfloat16), "fsdp", scatter_dimension=2, tiled=True
        ).astype(jnp.float32),
        lax.psum_scatter(
            out_grad.astype(jnp.bfloat16), "fsdp", scatter_dimension=1, tiled=True
        ).astype(jnp.float32),
        lax.psum_scatter(
            up_grad.astype(jnp.bfloat16), "fsdp", scatter_dimension=0, tiled=True
        ).astype(jnp.float32),
        lax.psum_scatter(
            upb_grad.astype(jnp.bfloat16), "fsdp", scatter_dimension=1, tiled=True
        ).astype(jnp.float32),
        lax.psum_scatter(
            down_grad.astype(jnp.bfloat16), "fsdp", scatter_dimension=1, tiled=True
        ).astype(jnp.float32),
        lax.psum_scatter(
            small_total.astype(jnp.bfloat16), "fsdp", scatter_dimension=1, tiled=True
        ).astype(jnp.float32),
    )
    qkv_total, qv_total, out_total, up_total, upb_total, down_total, small_sum = (
        lax.psum(shards[0].astype(jnp.bfloat16), "ctx").astype(jnp.float32),
        lax.psum(shards[1].astype(jnp.bfloat16), "ctx").astype(jnp.float32),
        lax.psum(shards[2].astype(jnp.bfloat16), "ctx").astype(jnp.float32),
        lax.psum(shards[3].astype(jnp.bfloat16), "ctx").astype(jnp.float32),
        lax.psum(shards[4].astype(jnp.bfloat16), "ctx").astype(jnp.float32),
        lax.psum(shards[5].astype(jnp.bfloat16), "ctx").astype(jnp.float32),
        lax.psum(shards[6].astype(jnp.bfloat16), "ctx").astype(jnp.float32),
    )
    return (
        output,
        tokens_grad,
        small_sum[0],
        small_sum[1],
        qkv_total,
        qv_total,
        out_total,
        small_sum[2],
        small_sum[3],
        small_sum[4],
        up_total,
        upb_total,
        down_total,
        small_sum[5],
    )


def solution(mesh):
    placed = (
        P("fsdp", ("ctx", "tp"), None),
        P("fsdp", None),
        P("fsdp"),
        P("fsdp"),
        P(None, "fsdp", "tp"),
        P(None, "tp", "fsdp"),
        P("tp", "fsdp"),
        P("fsdp"),
        P("fsdp"),
        P("fsdp"),
        P("fsdp", "tp"),
        P("tp", "fsdp"),
        P("tp", "fsdp"),
        P("fsdp"),
        P("fsdp", ("ctx", "tp"), None),
    )
    return jax.shard_map(
        local,
        mesh=mesh,
        in_specs=placed,
        out_specs=(
            P("fsdp", ("ctx", "tp"), None),
            P("fsdp", ("ctx", "tp"), None),
            P("fsdp"),
            P("fsdp"),
            P(None, "fsdp", "tp"),
            P(None, "tp", "fsdp"),
            P("tp", "fsdp"),
            P("fsdp"),
            P("fsdp"),
            P("fsdp"),
            P("fsdp", "tp"),
            P("tp", "fsdp"),
            P("tp", "fsdp"),
            P("fsdp"),
        ),
        check_vma=False,
    )
```

profile of v0, /device:TPU:0, one launch (start us, length us, event | category | flops | bytes accessed | tf_op | source)
XLA Modules:
  0.0 1111.0 jit_solution(8244551173031023131)
XLA Ops:
  16.8 38.8 %all-reduce.9 = (bf16[768]{0:T(1024)(128)(2,1)S(1)}, bf16[768]{0:T(1024)(128)(2,1)S(1)}, bf16[768]{0:T(1024)(128)(2,1)}, bf16[768]{0:T(1024)(128)(2,1)}, bf16[768]{0:T(1024)(128)(2,1)}) all-reduce(bf16[768]{0:T(1024)(128)(2,1)S(1)} %dynamic-update-slice.1, ...), channel_id=1, replica_groups=mesh['fsdp'=8,'ctx'=2,'tp'=2] {'fsdp'}, use_global_device_ids=true, to_apply=%add.1 | all-reduce | flops 3840 | bytes 15360
  56.3 2.4 fusion.40
  59.6 30.7 %all_gather.58 = bf16[2,6,64]{1,0,2:T(2,128)(2,1)S(1)} all-gather(bf16[2,6,8]{1,0,2:T(2,128)(2,1)S(1)} %copy.91), channel_id=1, replica_groups=mesh['fsdp'=8,'ctx'=2,'tp'=2] {'fsdp'}, dimensions={2}, use_global_device_ids=true | all-gather | bytes 1728 | tf_op jit(solution)/shard_map/all_gather | solution.py:200
  90.5 24.5 %all-gather.12.cloned.1.call-done = bf16[3,768,384]{2,1,0:T(8,128)(2,1)} async-done(((bf16[3,96,384]{2,1,0:T(8,128)(2,1)}), bf16[3,768,384]{2,1,0:T(8,128)(2,1)}) %all-gather.12.cloned.1.call-update) | async-done | bytes 1769488 | tf_op jit(solution)/shard_map/all_gather | solution.py:199
  115.0 4.2 convolution_bitcast_fusion
  121.6 2.4 slice.64
  124.5 33.7 %all_gather.61 = bf16[384,768]{0,1:T(8,128)(2,1)} all-gather(bf16[384,96]{0,1:T(8,128)(2,1)S(1)} %copy-done.30), channel_id=1, replica_groups=mesh['fsdp'=8,'ctx'=2,'tp'=2] {'fsdp'}, dimensions={1}, use_global_device_ids=true | all-gather | bytes 663552 | tf_op jit(solution)/shard_map/all_gather | solution.py:201
  161.4 15.2 %all-gather.14.cloned.1.call-done = bf16[1,2048,384]{2,1,0:T(8,128)(2,1)} async-done(((bf16[1,1024,384]{2,1,0:T(8,128)(2,1)}), bf16[1,2048,384]{2,1,0:T(8,128)(2,1)}) %all-gather.14.cloned.1.call-update) | async-done | bytes 1572880 | tf_op jit(solution)/shard_map/all_gather | solution.py:229
  178.3 78.7 %while.48 = (s32[]{:T(128)}, bf16[2,512,384]{2,1,0:T(8,128)(2,1)}, f32[2,6,512]{2,1,0:T(8,128)}, s32[2,512]{1,0:T(2,128)S(1)}, bf16[2,512,384]{1,2,0:T(8,128)(2,...) while((s32[]{:T(128)}, bf16[2,512,384]{2,1,0:T(8,128)(2,1)}, ...), condition=%wide.region_5.6_spmd.clone, body=%wide.region_2.5_spmd.clone.sunk | while | flops 1687366656 | bytes 86141056 | solution.py:120
  180.1 10.7 fusion.135
  190.8 12.0 %fusion.136 = f32[6,512]{1,0:T(8,128)S(1)} fusion(f32[6,512,2048]{2,1,0:T(8,128)} %get-tuple-element.594, f32[6,512]{1,0:T(8,128)S(1)} %get-tuple-element.595, pred[512,2048]{1,0:T(8,128)(4,1)S(1)} %broadcast_compare_fusion.4), kind=kLoop, calls=%fused_computation.6.clone.1 | loop fusion | flops 25162752 | bytes 26238976 | tf_op jit(solution)/shard_map/while/body/eval_jaxpr/while/body/eval_jaxpr/reduce_sum | solution.py:107
  202.8 12.3 %fusion.137 = bf16[6,512,64]{1,2,0:T(8,128)(2,1)} fusion(bf16[2048,6,64]{0,2,1:T(8,128)(2,1)S(1)} %bitcast.219, f32[6,512,2048]{2,1,0:T(8,128)} %get-tuple-element.594, f32[6,512]{1,0:T(8,128)S(1)} %fusion.136, f32[6,512]{1,0:T(8,128)S(1)} %get-tuple-element.595, pred[512,2048]{1,0:T(8,128)(4,1)S(1)} %broadcast_compare_fusion.4), kind=kOutput, calls=%fused_computation.9.clone.1 | convolution fusion | flops 836960256 | bytes 28205056 | tf_op jit(solution)/shard_map/while/body/eval_jaxpr/while/body/eval_jaxpr/hqk,khd->qhd/dot_general | solution.py:109
  219.4 10.7 fusion.135
  230.1 12.0 %fusion.136 = f32[6,512]{1,0:T(8,128)S(1)} fusion(f32[6,512,2048]{2,1,0:T(8,128)} %get-tuple-element.594, f32[6,512]{1,0:T(8,128)S(1)} %get-tuple-element.595, pred[512,2048]{1,0:T(8,128)(4,1)S(1)} %broadcast_compare_fusion.4), kind=kLoop, calls=%fused_computation.6.clone.1 | loop fusion | flops 25162752 | bytes 26238976 | tf_op jit(solution)/shard_map/while/body/eval_jaxpr/while/body/eval_jaxpr/reduce_sum | solution.py:107
  242.1 12.3 %fusion.137 = bf16[6,512,64]{1,2,0:T(8,128)(2,1)} fusion(bf16[2048,6,64]{0,2,1:T(8,128)(2,1)S(1)} %bitcast.219, f32[6,512,2048]{2,1,0:T(8,128)} %get-tuple-element.594, f32[6,512]{1,0:T(8,128)S(1)} %fusion.136, f32[6,512]{1,0:T(8,128)S(1)} %get-tuple-element.595, pred[512,2048]{1,0:T(8,128)(4,1)S(1)} %broadcast_compare_fusion.4), kind=kOutput, calls=%fused_computation.9.clone.1 | convolution fusion | flops 836960256 | bytes 28205056 | tf_op jit(solution)/shard_map/while/body/eval_jaxpr/while/body/eval_jaxpr/hqk,khd->qhd/dot_general | solution.py:109
  258.1 3.5 fusion.63
  262.4 8.5 reduce-scatter.18.cloned.1.call-done
  277.0 26.9 %all_gather.67 = bf16[24,64]{0,1:T(8,128)(2,1)S(1)} all-gather(bf16[24,8]{0,1:T(8,128)(2,1)S(1)} %copy-done.42), channel_id=1, replica_groups=mesh['fsdp'=8,'ctx'=2,'tp'=2] {'fsdp'}, dimensions={1}, use_global_device_ids=true | all-gather | bytes 3456 | tf_op jit(solution)/shard_map/all_gather | solution.py:203
  304.0 22.6 %all-gather.20.cloned.1.call-done = bf16[768,1536]{1,0:T(8,128)(2,1)} async-done(((bf16[96,1536]{1,0:T(8,128)(2,1)}), bf16[768,1536]{1,0:T(8,128)(2,1)}) %all-gather.20.cloned.1.call-update) | async-done | bytes 2359312 | tf_op jit(solution)/shard_map/all_gather | solution.py:202
  326.6 10.6 all-gather.18.cloned.1.call-done
  337.2 7.4 fusion.58
  344.5 5.3 all-gather.24.cloned.1.call-done
  349.8 55.7 %all-gather.22.cloned.1.call-done = bf16[1536,768]{0,1:T(8,128)(2,1)} async-done(((bf16[1536,96]{0,1:T(8,128)(2,1)}), bf16[1536,768]{0,1:T(8,128)(2,1)}) %all-gather.22.cloned.1.call-update) | async-done | bytes 2359312 | tf_op jit(solution)/shard_map/all_gather | solution.py:204
  405.5 9.4 fusion.85
  416.6 3.7 fusion.65
  420.4 7.7 reduce-scatter.22.cloned.1.call-done
  435.4 11.1 all-gather.26.cloned.1.call-done
  446.5 2.4 fusion.66
  448.8 178.0 %while.49 = (s32[]{:T(128)}, f32[2048,384]{0,1:T(8,128)}, f32[2048,384]{0,1:T(8,128)}, bf16[2,512,384]{1,2,0:T(8,128)(2,1)}, bf16[2,512,384]{1,2,0:T(8,128)(2,1)...) while((s32[]{:T(128)}, f32[2048,384]{0,1:T(8,128)}, ...), condition=%wide.region_15.16_spmd.clone, body=%wide.region_13.15_spmd.clone.sunk | while | flops 4126288896 | bytes 303573408 | solution.py:164
  451.8 10.1 fusion.148
  461.9 13.2 %fusion.150 = f32[6,64,2048]{2,1,0:T(8,128)} fusion(bf16[512,6,64]{0,2,1:T(8,128)(2,1)S(1)} %bitcast.221, f32[6,512,2048]{2,1,0:T(8,128)} %fusion.148, f32[6,512]{1,0:T(8,128)S(1)} %dynamic-slice_bitcast_fusion.2, pred[512,2048]{1,0:T(8,128)(4,1)S(1)} %broadcast_compare_fusion.5), kind=kOutput, calls=%fused_computation.27.clone.1 | convolution fusion | flops 830472192 | bytes 29765632 | tf_op jit(solution)/shard_map/while/body/eval_jaxpr/while/body/eval_jaxpr/hqk,qhd->khd/dot_general | solution.py:73
  475.1 20.0 %multiply_reduce_fusion.3 = (f32[6,512]{1,0:T(8,128)S(1)}, f32[6,512,2048]{2,1,0:T(8,128)}) fusion(f32[6,512,2048]{2,1,0:T(8,128)} %fusion.148, f32[6,512]{1,0:T(8,128)S(1)} %dynamic-slice_bitcast_fusion.2, pred[512,2048]{1,0:T(8,128)(4,1)S(1)} %broadcast_compare_fusion.5, bf16[512,6,64]{0,2,1:T(8,128)(2,1)S(1)} %bitcast.222, ...), kind=kOutput, calls=%fused_computation.24.clone.1 | convolution fusion | flops 836760576 | bytes 53370880 | tf_op jit(solution)/shard_map/while/body/eval_jaxpr/while/body/eval_jaxpr/qhd,khd->hqk/dot_general | solution.py:55
  495.1 21.2 %multiply_convert_fusion.5 = bf16[6,512,2048]{2,1,0:T(8,128)(2,1)} fusion(f32[6,512,2048]{2,1,0:T(8,128)} %get-tuple-element.607, f32[6,512,2048]{2,1,0:T(8,128)} %fusion.148, f32[6,512]{1,0:T(8,128)S(1)} %get-tuple-element.608, f32[6,512]{1,0:T(8,128)S(1)} %dynamic-slice_bitcast_fusion.2, pred[512,2048]{1,0:T(8,128)(4,1)S(1)} %broadcast_compare_fusion.5), kind=kLoop, calls=%fused_computation.23.clone.1 | loop fusion | flops 37748736 | bytes 63987712 | tf_op jit(solution)/shard_map/while/body/eval_jaxpr/while/body/eval_jaxpr/convert_element_type | solution.py:62
  516.4 8.5 convolution_multiply_fusion.5
  524.9 7.0 convolution_multiply_fusion.4
  532.2 2.2 bitcast_add_fusion.3
  540.6 10.1 fusion.148
  550.7 13.2 %fusion.150 = f32[6,64,2048]{2,1,0:T(8,128)} fusion(bf16[512,6,64]{0,2,1:T(8,128)(2,1)S(1)} %bitcast.221, f32[6,512,2048]{2,1,0:T(8,128)} %fusion.148, f32[6,512]{1,0:T(8,128)S(1)} %dynamic-slice_bitcast_fusion.2, pred[512,2048]{1,0:T(8,128)(4,1)S(1)} %broadcast_compare_fusion.5), kind=kOutput, calls=%fused_computation.27.clone.1 | convolution fusion | flops 830472192 | bytes 29765632 | tf_op jit(solution)/shard_map/while/body/eval_jaxpr/while/body/eval_jaxpr/hqk,qhd->khd/dot_general | solution.py:73
  563.9 20.0 %multiply_reduce_fusion.3 = (f32[6,512]{1,0:T(8,128)S(1)}, f32[6,512,2048]{2,1,0:T(8,128)}) fusion(f32[6,512,2048]{2,1,0:T(8,128)} %fusion.148, f32[6,512]{1,0:T(8,128)S(1)} %dynamic-slice_bitcast_fusion.2, pred[512,2048]{1,0:T(8,128)(4,1)S(1)} %broadcast_compare_fusion.5, bf16[512,6,64]{0,2,1:T(8,128)(2,1)S(1)} %bitcast.222, ...), kind=kOutput, calls=%fused_computation.24.clone.1 | convolution fusion | flops 836760576 | bytes 53370880 | tf_op jit(solution)/shard_map/while/body/eval_jaxpr/while/body/eval_jaxpr/qhd,khd->hqk/dot_general | solution.py:55
  583.9 21.2 %multiply_convert_fusion.5 = bf16[6,512,2048]{2,1,0:T(8,128)(2,1)} fusion(f32[6,512,2048]{2,1,0:T(8,128)} %get-tuple-element.607, f32[6,512,2048]{2,1,0:T(8,128)} %fusion.148, f32[6,512]{1,0:T(8,128)S(1)} %get-tuple-element.608, f32[6,512]{1,0:T(8,128)S(1)} %dynamic-slice_bitcast_fusion.2, pred[512,2048]{1,0:T(8,128)(4,1)S(1)} %broadcast_compare_fusion.5), kind=kLoop, calls=%fused_computation.23.clone.1 | loop fusion | flops 37748736 | bytes 63987712 | tf_op jit(solution)/shard_map/while/body/eval_jaxpr/while/body/eval_jaxpr/convert_element_type | solution.py:62
  605.2 8.5 convolution_multiply_fusion.5
  613.7 7.0 convolution_multiply_fusion.4
  621.0 2.2 bitcast_add_fusion.3
  626.9 3.2 copy.103
  633.5 24.0 %reduce-scatter.24.cloned.1.call-done = bf16[1,1024,384]{2,1,0:T(8,128)(2,1)} async-done(((bf16[1,2048,384]{2,1,0:T(8,128)(2,1)}), bf16[1,1024,384]{2,1,0:T(8,128)(2,1)}) %reduce-scatter.24.cloned.1.call-update) | async-done | bytes 786448 | tf_op jit(solution)/shard_map/reduce_scatter | solution.py:302
  657.5 28.4 %reduce-scatter.26.cloned.1.call-done = bf16[1,1024,384]{2,1,0:T(8,128)(2,1)} async-done(((bf16[1,2048,384]{2,1,0:T(8,128)(2,1)}), bf16[1,1024,384]{2,1,0:T(8,128)(2,1)}) %reduce-scatter.26.cloned.1.call-update) | async-done | bytes 786448 | tf_op jit(solution)/shard_map/reduce_scatter | solution.py:305
  685.9 5.6 fusion.62
  691.6 4.5 convert_bitcast_fusion
  696.1 4.0 copy.112
  701.7 7.7 convolution_convert_fusion
  710.9 5.8 convolution_convert_fusion.1
  720.5 8.7 fusion.64
  731.2 37.3 %all-reduce.8 = (bf16[2,6,64]{2,1,0:T(8,128)(2,1)S(1)}, bf16[24,64]{1,0:T(8,128)(2,1)S(1)}, bf16[768]{0:T(1024)(128)(2,1)S(1)}) all-reduce(bf16[2,6,64]{2,1,0:T(8,128)(2,1)S(1)} %pad_maximum_fusion, bf16[24,64]{1,0:T(8,128)(2,1)S(1)} %convert_element_type.407, ...), channel_id=10, replica_groups=mesh['fsdp'=8,'ctx'=2,'tp'=2] {'fsdp'}, use_global_device_ids=true, to_apply=%region_34.35.clone | all-reduce | flops 3072 | bytes 12288
  771.5 2.2 fusion.43
  773.8 3.4 psum.56
  780.2 62.9 %reduce-scatter.34.cloned.1.call-done = bf16[1536,96]{0,1:T(8,128)(2,1)} async-done(((bf16[1536,768]{0,1:T(8,128)(2,1)}), bf16[1536,96]{0,1:T(8,128)(2,1)}) %reduce-scatter.34.cloned.1.call-update) | async-done | bytes 294928 | tf_op jit(solution)/shard_map/reduce_scatter | solution.py:353
  843.0 71.4 %reduce-scatter.32.cloned.1.call-done = bf16[96,1536]{1,0:T(8,128)(2,1)} async-done(((bf16[768,1536]{1,0:T(8,128)(2,1)}), bf16[96,1536]{1,0:T(8,128)(2,1)}) %reduce-scatter.32.cloned.1.call-update) | async-done | bytes 294928 | tf_op jit(solution)/shard_map/reduce_scatter | solution.py:347
  914.5 65.0 %reduce-scatter.30.cloned.1.call-done = bf16[384,96]{0,1:T(8,128)(2,1)} async-done(((bf16[384,768]{0,1:T(8,128)(2,1)}), bf16[384,96]{0,1:T(8,128)(2,1)}) %reduce-scatter.30.cloned.1.call-update) | async-done | bytes 73744 | tf_op jit(solution)/shard_map/reduce_scatter | solution.py:344
  979.5 10.3 reduce-scatter.20.cloned.1.call-done
  989.9 3.3 add_convert_fusion
  993.2 62.6 %reduce-scatter.36.cloned.1.call-done = bf16[96,6]{1,0:T(8,128)(2,1)} async-done(((bf16[768,6]{1,0:T(8,128)(2,1)}), bf16[96,6]{1,0:T(8,128)(2,1)}) %reduce-scatter.36.cloned.1.call-update) | async-done | bytes 1168
  1056.6 8.1 all-reduce.10
  1066.5 30.1 %all-reduce.14.cloned.1.call-done = (bf16[3,96,384]{1,2,0:T(8,128)(2,1)}, bf16[384,96]{0,1:T(8,128)(2,1)}, bf16[96,1536]{1,0:T(8,128)(2,1)}, bf16[1536,96]{0,1:T(8,128)(2,1)}) async-done(((bf16[3,96,384]{1,2,0:T(8,128)(2,1)}, bf16[384,96]{0,1:T(8,128)(2,1)}, bf16[96,1536]{1,0:T(8,128)(2,1)}, bf16[1536,96]{0,1:T(8,128)(2,1)}), (bf16[3,96,384]{1,2,0:T(8,128)(2,1)}, bf16[384,96]{0,1:T(8,128)(2,1)}, ...) | async-done | bytes 884752 | tf_op jit(solution)/shard_map/psum | solution.py:361
  1096.6 1.9 copy.106
  (304 shorter events, 82.2 us)
Async XLA Ops:
  7.2 52.3 %copy-start.41 = (bf16[2,6,8]{2,0,1:T(2,128)(2,1)S(1)}, bf16[2,6,8]{2,0,1:T(2,128)(2,1)}, u32[]{:S(2)}) copy-start(bf16[2,6,8]{2,0,1:T(2,128)(2,1)} %param.24) | copy-start | bytes 580
  7.2 83.3 %all-gather.10.cloned.1.call-start = ((), (), s32[]{:S(2)}) async-start(), calls=%async_computation.11 | async-start | bytes 2359296 | tf_op jit(solution)/shard_map/all_gather | solution.py:219
  8.6 51.0 %copy-start.28 = (f32[512]{0:T(512)}, f32[512]{0:T(512)S(1)}, u32[]{:S(2)}) copy-start(f32[512]{0:T(512)S(1)} %broadcast_multiply_fusion.1) | copy-start | bytes 6148
  10.7 48.9 %copy-start.31 = (f32[512]{0:T(512)}, f32[512]{0:T(512)S(1)}, u32[]{:S(2)}) copy-start(f32[512]{0:T(512)S(1)} %fusion.77) | copy-start | bytes 6148
  58.6 56.3 %all-gather.12.cloned.1.call-start = ((), (), s32[]{:S(2)}) async-start(), calls=%async_computation.12 | async-start | bytes 1990656 | tf_op jit(solution)/shard_map/all_gather | solution.py:199
  59.4 100.3 %all-gather.16.cloned.1.call-start = ((), (), s32[]{:S(2)}) async-start(), calls=%async_computation.14 | async-start | bytes 2359296 | tf_op jit(solution)/shard_map/all_gather | solution.py:230
  119.1 2.4 copy-start.17
  121.5 2.6 copy-start.51
  121.5 3.0 copy-start.30
  121.6 55.0 %all-gather.14.cloned.1.call-start = ((), (), s32[]{:S(2)}) async-start(), calls=%async_computation.13 | async-start | bytes 2359296 | tf_op jit(solution)/shard_map/all_gather | solution.py:229
  124.1 146.8 %reduce-scatter.18.cloned.1.call-start = ((), (), s32[]{:S(2)}) async-start(), calls=%async_computation.15 | async-start | bytes 2359296 | tf_op jit(solution)/shard_map/reduce_scatter | solution.py:253
  258.1 4.2 copy-start.45
  258.1 4.2 copy-start.44
  258.1 4.2 copy-start.43
  258.1 12.8 %copy-start = (bf16[1,512,768]{2,1,0:T(8,128)(2,1)S(1)}, bf16[1,512,768]{2,1,0:T(8,128)(2,1)}, u32[]{:S(2)}) copy-start(bf16[1,512,768]{2,1,0:T(8,128)(2,1)} %param.19) | copy-start | bytes 2359300
  261.7 64.9 %all-gather.20.cloned.1.call-start = ((), (), s32[]{:S(2)}) async-start(), calls=%async_computation.17 | async-start | bytes 2654208 | tf_op jit(solution)/shard_map/all_gather | solution.py:202
  262.3 74.9 %all-gather.18.cloned.1.call-start = ((), (), s32[]{:S(2)}) async-start(), calls=%async_computation.16 | async-start | bytes 2359296 | tf_op jit(solution)/shard_map/all_gather | solution.py:258
  262.4 169.3 %copy-start.24 = (f32[768]{0:T(1024)}, f32[768]{0:T(1024)S(1)}, u32[]{:S(2)}) copy-start(f32[768]{0:T(1024)S(1)} %convert_element_type.356) | copy-start | bytes 9220
  270.9 3.1 copy-start.9
  274.1 2.9 copy-start.42
  275.4 74.3 %all-gather.24.cloned.1.call-start = ((), (), s32[]{:S(2)}) async-start(), calls=%async_computation.20 | async-start | bytes 2359296 | tf_op jit(solution)/shard_map/all_gather | solution.py:220
  276.2 129.3 %all-gather.22.cloned.1.call-start = ((), (), s32[]{:S(2)}) async-start(), calls=%async_computation.18 | async-start | bytes 2654208 | tf_op jit(solution)/shard_map/all_gather | solution.py:204
  276.9 151.2 %reduce-scatter.22.cloned.1.call-start = ((), (), s32[]{:S(2)}) async-start(), calls=%async_computation.21 | async-start | bytes 2359296 | tf_op jit(solution)/shard_map/reduce_scatter | solution.py:281
  304.0 101.5 %copy-start.37 = (f32[1536]{0:T(1024)}, f32[1536]{0:T(1024)S(1)}, u32[]{:S(2)}) copy-start(f32[1536]{0:T(1024)S(1)} %reshape.559) | copy-start | bytes 18436
  405.5 11.2 %copy-start.46 = (bf16[768,1536]{1,0:T(8,128)(2,1)S(1)}, bf16[768,1536]{1,0:T(8,128)(2,1)}, u32[]{:S(2)}) copy-start(bf16[768,1536]{1,0:T(8,128)(2,1)} %all-gather.20.cloned.1.call-done) | copy-start | bytes 7077892
  420.4 26.1 %all-gather.26.cloned.1.call-start = ((), (), s32[]{:S(2)}) async-start(), calls=%async_computation.22 | async-start | bytes 2359296 | tf_op jit(solution)/shard_map/all_gather | solution.py:289
  428.1 3.5 copy-start.18
  433.1 13.3 %copy-start.23 = (bf16[384,768]{0,1:T(8,128)(2,1)S(1)}, bf16[384,768]{0,1:T(8,128)(2,1)}, u32[]{:S(2)}) copy-start(bf16[384,768]{0,1:T(8,128)(2,1)} %all_gather.61) | copy-start | bytes 1769476
  435.3 222.2 %reduce-scatter.24.cloned.1.call-start = ((), (), s32[]{:S(2)}) async-start(), calls=%async_computation.23 | async-start | bytes 2359296 | tf_op jit(solution)/shard_map/reduce_scatter | solution.py:302
  524.9 7.1 copy-start.2
  524.9 7.1 copy-start.5
  524.9 7.3 copy-start.7
  532.2 2.2 copy-start.19
  532.2 5.6 copy-start.16
  534.4 2.6 copy-start.6
  613.7 7.1 copy-start.2
  613.7 7.1 copy-start.5
  613.7 7.3 copy-start.7
  621.0 2.2 copy-start.19
  621.0 5.6 copy-start.16
  623.2 2.6 copy-start.6
  626.8 3.3 copy-start.4
  630.1 55.8 %reduce-scatter.26.cloned.1.call-start = ((), (), s32[]{:S(2)}) async-start(), calls=%async_computation.24 | async-start | bytes 2359296 | tf_op jit(solution)/shard_map/reduce_scatter | solution.py:305
  631.9 136.6 %reduce-scatter.28.cloned.1.call-start = ((), (), s32[]{:S(2)}) async-start(), calls=%async_computation.25 | async-start | bytes 2359296 | tf_op jit(solution)/shard_map/reduce_scatter | solution.py:326
  685.9 5.7 copy-start.22
  685.9 5.7 copy-start.47
  691.6 86.6 %reduce-scatter.38.cloned.1.call-start = ((), (), s32[]{:S(2)}) async-start(), calls=%async_computation.30 | async-start | bytes 1990656
  701.7 141.4 %reduce-scatter.34.cloned.1.call-start = ((), (), s32[]{:S(2)}) async-start(), calls=%async_computation.28 | async-start | bytes 2654208 | tf_op jit(solution)/shard_map/reduce_scatter | solution.py:353
  709.5 205.0 %reduce-scatter.32.cloned.1.call-start = ((), (), s32[]{:S(2)}) async-start(), calls=%async_computation.27 | async-start | bytes 2654208 | tf_op jit(solution)/shard_map/reduce_scatter | solution.py:347
  716.7 262.8 %reduce-scatter.30.cloned.1.call-start = ((), (), s32[]{:S(2)}) async-start(), calls=%async_computation.26 | async-start | bytes 663552 | tf_op jit(solution)/shard_map/reduce_scatter | solution.py:344
  720.1 9.9 copy-start.52
  720.1 10.2 copy-start.40
  720.1 10.2 copy-start.14
  720.2 269.7 %reduce-scatter.20.cloned.1.call-start = ((), (), s32[]{:S(2)}) async-start(), calls=%async_computation.19 | async-start | bytes 2359296 | tf_op jit(solution)/shard_map/reduce_scatter | solution.py:265
  729.2 40.6 %copy-start.1 = (bf16[1,512,768]{2,1,0:T(8,128)(2,1)S(1)}, bf16[1,512,768]{2,1,0:T(8,128)(2,1)}, u32[]{:S(2)}) copy-start(bf16[1,512,768]{2,1,0:T(8,128)(2,1)} %param.19) | copy-start | bytes 2359300
  729.2 40.6 %copy-start.27 = (f32[768]{0:T(1024)S(1)}, f32[768]{0:T(1024)}, u32[]{:S(2)}) copy-start(f32[768]{0:T(1024)} %copy-done.26) | copy-start | bytes 9220
  729.2 40.6 %copy-start.29 = (f32[512]{0:T(512)S(1)}, f32[512]{0:T(512)}, u32[]{:S(2)}) copy-start(f32[512]{0:T(512)} %copy-done.28) | copy-start | bytes 6148
  729.2 326.6 %reduce-scatter.36.cloned.1.call-start = ((), (), s32[]{:S(2)}) async-start(), calls=%async_computation.29 | async-start | bytes 221184
  730.4 41.0 %copy-start.34 = (f32[512]{0:T(512)S(1)}, f32[512]{0:T(512)}, u32[]{:S(2)}) copy-start(f32[512]{0:T(512)} %copy-done.33) | copy-start | bytes 6148
  730.4 41.1 %copy-start.32 = (f32[512]{0:T(512)S(1)}, f32[512]{0:T(512)}, u32[]{:S(2)}) copy-start(f32[512]{0:T(512)} %copy-done.31) | copy-start | bytes 6148
  771.4 218.5 %copy-start.10 = (bf16[1,512,768]{2,1,0:T(8,128)(2,1)S(1)}, bf16[1,512,768]{2,1,0:T(8,128)(2,1)}, u32[]{:S(2)}) copy-start(bf16[1,512,768]{2,1,0:T(8,128)(2,1)} %reduce-scatter.18.cloned.1.call-done) | copy-start | bytes 2359300
  771.4 218.5 %copy-start.12 = (f32[1,512,768]{2,1,0:T(8,128)S(1)}, f32[1,512,768]{2,1,0:T(8,128)}, u32[]{:S(2)}) copy-start(f32[1,512,768]{2,1,0:T(8,128)} %copy-done.11) | copy-start | bytes 4718596
  771.4 218.4 %copy-start.25 = (f32[768]{0:T(1024)S(1)}, f32[768]{0:T(1024)}, u32[]{:S(2)}) copy-start(f32[768]{0:T(1024)} %copy-done.24) | copy-start | bytes 9220
  778.1 318.5 %all-reduce.14.cloned.1.call-start = ((), (), s32[]{:S(2)}) async-start(), calls=%async_computation.31 | async-start | bytes 1916928 | tf_op jit(solution)/shard_map/psum | solution.py:361
  (20 other events, 26.4 us)
Sparse Core Ops, SparseCore 0:
  58.8 7.0 all-gather.9
  68.1 46.8 all-gather.11
  121.7 26.2 all-gather.15
  149.3 27.1 all-gather.13
  261.8 9.0 reduce-scatter.17
  273.2 53.3 all-gather.19
  328.8 8.3 all-gather.17
  338.8 10.9 all-gather.23
  352.2 53.2 all-gather.21
  420.5 7.5 reduce-scatter.21
  435.4 10.9 all-gather.25
  630.2 27.2 reduce-scatter.23
  659.8 26.0 reduce-scatter.25
  691.7 9.0 reduce-scatter.27
  704.5 67.2 reduce-scatter.37
  775.2 67.7 reduce-scatter.33
  846.4 68.0 reduce-scatter.31
  918.2 61.1 reduce-scatter.29
  981.8 8.0 reduce-scatter.19
  993.6 62.2 reduce-scatter.35
  1058.9 37.6 all-reduce.13
where the time goes:
time: 1120 us; the launch traced here: 1110 us
  waiting for transfers between devices  519 us (46%)
  matrix products  228 us (20%)
  blocking collectives  179 us (16%)
  other arithmetic  107 us (10%)
  local copies, waits for them, and re-layouts  59.8 us (5%)
  between operations  16.8 us (2%)
    unnamed x2, blocking collectives  76.1 us
    reduce_scatter x1, waiting for transfers between devices, local(): lax.psum_scatter(up_grad.astype(jnp.bfloat16), 'fsdp', scatter_dimension=...  71.4 us
    unnamed x23, waiting for transfers between devices  65.5 us
    reduce_scatter x1, waiting for transfers between devices, local(): lax.psum_scatter(out_grad.astype(jnp.bfloat16), 'fsdp', scatter_dimension...  65 us
    reduce_scatter x1, waiting for transfers between devices, local(): lax.psum_scatter(down_grad.astype(jnp.bfloat16), 'fsdp', scatter_dimensio...  62.9 us
    all_gather x1, waiting for transfers between devices, local(): lax.all_gather(down_weight, 'fsdp', axis=1, tiled=True)  55.7 us
    convert_element_type x2, other arithmetic, score_grads(): (probabilities * (upstream - delta_rows[:, :, None])).astype(jnp.bfloat16)  42.5 us
    dot_general x4, matrix products, score_rows(): jnp.einsum('qhd,khd->hqk', query_heads, key_heads, preferred_element_type...  41.6 us
  transfers between devices with their start and end apart: 21, of which 17 were waited for; matrix products, arithmetic and copies ran while one was open for 6% of the time, Pallas kernels for 0%

commit v1 on v0

v1 whole, which is shorter than its diff:
```python
from functools import partial

import jax
import jax.numpy as jnp
from jax import lax
from jax.experimental import pallas as pl
from jax.experimental.pallas import tpu as pltpu
from jax.sharding import PartitionSpec as P

EPSILON = 1e-05
MASKED = -1e30
F32 = jnp.float32
BF16 = jnp.bfloat16
HEAD = 64
PAIR = 2 * HEAD


def norm_rows(values, gain, shift):
    average = jnp.mean(values, axis=-1, keepdims=True)
    centred = values - average
    spread = jnp.mean(centred * centred, axis=-1, keepdims=True)
    return centred * lax.rsqrt(spread + EPSILON) * gain + shift


def norm_back(values, gain, upstream):
    average = jnp.mean(values, axis=-1, keepdims=True)
    centred = values - average
    spread = jnp.mean(centred * centred, axis=-1, keepdims=True)
    inverse = lax.rsqrt(spread + EPSILON)
    unit = centred * inverse
    scaled = upstream * gain
    inner = jnp.mean(scaled * unit, axis=-1, keepdims=True)
    grad = (scaled - jnp.mean(scaled, axis=-1, keepdims=True) - unit * inner) * inverse
    return grad, jnp.sum(upstream * unit, axis=(0, 1)), jnp.sum(upstream, axis=(0, 1))


def swap(values, axis):
    return lax.ppermute(values, axis, [(0, 1), (1, 0)])


def dot(left, right, dims):
    return lax.dot_general(left, right, (dims, ((), ())), preferred_element_type=F32)


def head_parts(matrix):
    lane = lax.broadcasted_iota(jnp.int32, matrix.shape, 1)
    zero = jnp.zeros_like(matrix)
    return jnp.where(lane < HEAD, matrix, zero), jnp.where(lane < HEAD, zero, matrix)


def forward_kernel(
    chunk_count, q_segs, k_segs, q_ref, k_ref, v_ref, o_ref, lse_ref, peak, total, acc
):
    block = q_ref.shape[1]
    seq, qblk = pl.program_id(0), pl.program_id(2)
    q_seg = q_segs[seq, qblk]
    peak[...] = jnp.full(peak.shape, MASKED, F32)
    total[...] = jnp.zeros(total.shape, F32)
    acc[...] = jnp.zeros(acc.shape, F32)
    q_parts = head_parts(q_ref[0] * jnp.asarray(HEAD**-0.5, BF16))

    def chunk(index, diagonal):
        rows = pl.ds(index * block, block)
        keys = k_ref[0, rows, :]
        v_parts = head_parts(v_ref[0, rows, :])
        scales, terms = [], []
        for head in range(2):
            scores = dot(q_parts[head], keys, ((1,), (1,)))
            if diagonal:
                q_at = lax.broadcasted_iota(jnp.int32, scores.shape, 0)
                k_at = lax.broadcasted_iota(jnp.int32, scores.shape, 1)
                scores = jnp.where(k_at <= q_at, scores, MASKED)
            old = peak[head]
            new = jnp.maximum(old, jnp.max(scores, axis=1, keepdims=True))
            probs = jnp.exp(scores - new[:, :1])
            scale = jnp.exp(old - new)
            total[head] = total[head] * scale + jnp.sum(probs, axis=1, keepdims=True)
            peak[head] = new
            scales.append(scale)
            terms.append(dot(probs.astype(BF16), v_parts[head], ((1,), (0,))))
        lane = lax.broadcasted_iota(jnp.int32, acc.shape, 1)
        acc[...] = acc[...] * jnp.where(lane < HEAD, scales[0], scales[1]) + (terms[0] + terms[1])

    for index in range(chunk_count):
        k_seg = k_segs[seq, index]
        pl.when(k_seg == q_seg)(partial(chunk, index, True))
        pl.when(k_seg < q_seg)(partial(chunk, index, False))
    lane = lax.broadcasted_iota(jnp.int32, acc.shape, 1)
    sums = jnp.where(lane < HEAD, total[0], total[1])
    o_ref[0] = (acc[...] / sums).astype(BF16)
    lse = jnp.transpose(jnp.where(lane < HEAD, peak[0], peak[1]) + jnp.log(sums))
    lse_ref[0, 0] = jnp.concatenate([lse[0:4], lse[HEAD : HEAD + 4]], axis=0)


def backward_kernel(
    chunk_count,
    q_segs,
    k_segs,
    q_ref,
    g_ref,
    o_ref,
    lse_ref,
    k_ref,
    v_ref,
    dq_ref,
    dkv_ref,
    dq_acc,
    dk_acc,
    dv_acc,
):
    block = q_ref.shape[1]
    seq, qblk = pl.program_id(0), pl.program_id(2)
    q_seg = q_segs[seq, qblk]

    @pl.when(qblk == 0)
    def _():
        dk_acc[...] = jnp.zeros(dk_acc.shape, F32)
        dv_acc[...] = jnp.zeros(dv_acc.shape, F32)

    dq_acc[...] = jnp.zeros(dq_acc.shape, F32)
    q_parts = head_parts(q_ref[0] * jnp.asarray(HEAD**-0.5, BF16))
    g_parts = head_parts(g_ref[0])
    products = jnp.transpose(g_ref[0].astype(F32) * o_ref[0].astype(F32))
    deltas = (
        jnp.sum(products[:HEAD], axis=0, keepdims=True),
        jnp.sum(products[HEAD:], axis=0, keepdims=True),
    )
    lses = (lse_ref[0, 0, 0:1, :], lse_ref[0, 0, 4:5, :])

    def chunk(index, diagonal):
        rows = pl.ds(index * block, block)
        keys = k_ref[0, rows, :]
        values = v_ref[0, rows, :]
        k_parts = head_parts(keys)
        dk, dv, dq = dk_acc[rows, :], dv_acc[rows, :], dq_acc[...]
        for head in range(2):
            scores = dot(keys, q_parts[head], ((1,), (1,)))
            if diagonal:
                k_at = lax.broadcasted_iota(jnp.int32, scores.shape, 0)
                q_at = lax.broadcasted_iota(jnp.int32, scores.shape, 1)
                scores = jnp.where(k_at <= q_at, scores, MASKED)
            probs = jnp.exp(scores - lses[head])
            up = dot(values, g_parts[head], ((1,), (1,)))
            scaled = (probs * (up - deltas[head])).astype(BF16)
            dv = dv + dot(probs.astype(BF16), g_parts[head], ((1,), (0,)))
            dk = dk + dot(scaled, q_parts[head], ((1,), (0,)))
            dq = dq + dot(scaled, k_parts[head], ((0,), (0,)))
        dk_acc[rows, :] = dk
        dv_acc[rows, :] = dv
        dq_acc[...] = dq

    for index in range(chunk_count):
        k_seg = k_segs[seq, index]
        pl.when(k_seg == q_seg)(partial(chunk, index, True))
        pl.when(k_seg < q_seg)(partial(chunk, index, False))
    dq_ref[0] = (dq_acc[...] * HEAD**-0.5).astype(BF16)

    @pl.when(qblk == pl.num_programs(2) - 1)
    def _():
        dkv_ref[0, 0] = dk_acc[...].astype(BF16)
        dkv_ref[0, 1] = dv_acc[...].astype(BF16)


def attend(queries, kv_all, q_segs, k_segs, block):
    seqs, rows, width = queries.shape
    total_len = kv_all.shape[1]
    pairs = width // PAIR
    q_spec = pl.BlockSpec((1, block, PAIR), lambda s, p, q, *_: (s, q, p))
    return pl.pallas_call(
        partial(forward_kernel, total_len // block),
        grid_spec=pltpu.PrefetchScalarGridSpec(
            num_scalar_prefetch=2,
            grid=(seqs, pairs, rows // block),
            in_specs=[
                q_spec,
                pl.BlockSpec((1, total_len, PAIR), lambda s, p, q, *_: (s, 0, p)),
                pl.BlockSpec((1, total_len, PAIR), lambda s, p, q, *_: (s, 0, p + pairs)),
            ],
            out_specs=[
                q_spec,
                pl.BlockSpec((1, 1, 8, block), lambda s, p, q, *_: (s, p, 0, q)),
            ],
            scratch_shapes=[
                pltpu.VMEM((2, block, PAIR), F32),
                pltpu.VMEM((2, block, PAIR), F32),
                pltpu.VMEM((block, PAIR), F32),
            ],
        ),
        out_shape=[
            jax.ShapeDtypeStruct(queries.shape, BF16),
            jax.ShapeDtypeStruct((seqs, pairs, 8, rows), F32),
        ],
        compiler_params=pltpu.CompilerParams(vmem_limit_bytes=40 * 2**20),
        cost_estimate=pl.CostEstimate(
            flops=16 * seqs * rows * total_len * width,
            bytes_accessed=8 * seqs * total_len * width,
            transcendentals=seqs * rows * total_len * width // HEAD,
        ),
    )(q_segs, k_segs, queries, kv_all, kv_all)


def attend_back(queries, grads, mixed, lse, kv_all, q_segs, k_segs, block):
    seqs, rows, width = queries.shape
    total_len = kv_all.shape[1]
    pairs = width // PAIR
    q_spec = pl.BlockSpec((1, block, PAIR), lambda s, p, q, *_: (s, q, p))
    return pl.pallas_call(
        partial(backward_kernel, total_len // block),
        grid_spec=pltpu.PrefetchScalarGridSpec(
            num_scalar_prefetch=2,
            grid=(seqs, pairs, rows // block),
            in_specs=[
                q_spec,
                q_spec,
                q_spec,
                pl.BlockSpec((1, 1, 8, block), lambda s, p, q, *_: (s, p, 0, q)),
                pl.BlockSpec((1, total_len, PAIR), lambda s, p, q, *_: (s, 0, p)),
                pl.BlockSpec((1, total_len, PAIR), lambda s, p, q, *_: (s, 0, p + pairs)),
            ],
            out_specs=[
                q_spec,
                pl.BlockSpec((1, 2, total_len, PAIR), lambda s, p, q, *_: (s, 0, 0, p)),
            ],
            scratch_shapes=[
                pltpu.VMEM((block, PAIR), F32),
                pltpu.VMEM((total_len, PAIR), F32),
                pltpu.VMEM((total_len, PAIR), F32),
            ],
        ),
        out_shape=[
            jax.ShapeDtypeStruct(queries.shape, BF16),
            jax.ShapeDtypeStruct((seqs, 2, total_len, width), BF16),
        ],
        compiler_params=pltpu.CompilerParams(vmem_limit_bytes=48 * 2**20),
        cost_estimate=pl.CostEstimate(
            flops=40 * seqs * rows * total_len * width,
            bytes_accessed=16 * seqs * total_len * width,
            transcendentals=seqs * rows * total_len * width // HEAD,
        ),
    )(q_segs, k_segs, queries, grads, mixed, lse, kv_all, kv_all)


def pair_rows(values):
    return jnp.concatenate([values, swap(values, "tp")], axis=1)


def pair_sum(terms, half_rows):
    terms = terms.reshape(-1, 2 * half_rows, terms.shape[-1])
    other = swap(terms[:, half_rows:].astype(BF16), "tp")
    return terms[:, :half_rows].astype(BF16).astype(F32) + other.astype(F32)


def context_total(values):
    if lax.axis_size("ctx") == 2:
        return values.astype(F32) + swap(values, "ctx").astype(F32)
    return lax.psum(values, "ctx").astype(F32)


def local(
    tokens,
    segment_order,
    ln1_gain,
    ln1_bias,
    qkv_weight,
    qv_bias,
    out_weight,
    out_bias,
    ln2_gain,
    ln2_bias,
    up_weight,
    up_bias,
    down_weight,
    down_bias,
    cotangent,
):
    shards = lax.axis_size("fsdp")
    contexts = lax.axis_size("ctx")
    seq_count, half_rows, model_width = tokens.shape
    local_rows = half_rows * 2
    depth = model_width // shards
    inner_width = qkv_weight.shape[2]
    heads = qv_bias.shape[1]
    hidden = up_weight.shape[1]
    units = up_bias.shape[0]
    qkv_width = 3 * inner_width

    smalls = [ln1_gain, ln1_bias, out_bias, ln2_gain, ln2_bias, down_bias]
    flat = jnp.concatenate([part.reshape(-1) for part in smalls + [qv_bias, up_bias]])
    flat = jnp.pad(flat, (0, qkv_width - flat.shape[0])).reshape(1, qkv_width)
    first = jnp.concatenate(
        [jnp.swapaxes(qkv_weight, 0, 1).reshape(depth, qkv_width), flat], axis=0
    )
    first_all = lax.all_gather(first, "fsdp", axis=0, tiled=False)
    qkv_full = first_all[:, :depth].reshape(model_width, qkv_width)
    small_all = first_all[:, depth].astype(F32)
    gain_one, shift_one, outb_full, gain_two, shift_two, downb_full = [
        small_all[:, i * depth : (i + 1) * depth].reshape(model_width) for i in range(6)
    ]
    start = 6 * depth
    span = qv_bias.shape[2]
    qv_size = 2 * heads * span
    qv_full = jnp.moveaxis(
        small_all[:, start : start + qv_size].reshape(shards, 2, heads, span), 0, 2
    ).reshape(2, inner_width)
    start += qv_size
    upb_full = jnp.moveaxis(
        small_all[:, start : start + units * span].reshape(shards, units, span), 0, 1
    ).reshape(hidden)

    residual_in = tokens.astype(F32)
    normed_one = norm_rows(residual_in, gain_one, shift_one).astype(BF16)
    rows_one = pair_rows(normed_one)
    grad_flat = pair_rows(cotangent).reshape(-1, model_width)
    flat_one = rows_one.reshape(-1, model_width)
    kv = jnp.dot(flat_one, qkv_full[:, inner_width:], preferred_element_type=F32)
    kv_bias = jnp.concatenate([jnp.zeros((inner_width,), F32), qv_full[1]])
    kv = (kv + kv_bias).astype(BF16).reshape(seq_count, local_rows, 2 * inner_width)
    queries = jnp.dot(flat_one, qkv_full[:, :inner_width], preferred_element_type=F32)
    queries = (queries + qv_full[0]).astype(BF16).reshape(seq_count, local_rows, inner_width)

    second = jnp.concatenate([out_weight.T, up_weight, down_weight.T], axis=1)
    kv, second = lax.optimization_barrier((kv, second))
    second_all = lax.all_gather(second, "fsdp", axis=0, tiled=True)
    out_t = second_all[:, :inner_width]
    up_full = second_all[:, inner_width : inner_width + hidden]
    down_t = second_all[:, inner_width + hidden :]

    here, core = lax.axis_index("ctx"), lax.axis_index("tp")
    if contexts == 2:
        kv_all = jnp.concatenate([kv, swap(kv, "ctx")], axis=1)
        order = [here, 1 - here]
    else:
        kv_all = lax.all_gather(kv, "ctx", axis=1, tiled=True)
        order = list(range(contexts))
    segment_size = contexts * local_rows // segment_order.shape[1]
    block = min(segment_size, half_rows)
    per_half = half_rows // segment_size

    def half_segments(context):
        picks = []
        for turn in range(2):
            at = (context * 2 + (core + turn) % 2) * per_half
            picks.append(lax.dynamic_slice_in_dim(segment_order, at, per_half, 1))
        return jnp.concatenate(picks, axis=1)

    q_segs = half_segments(here)
    k_segs = jnp.concatenate([half_segments(context) for context in order], axis=1)
    mixed, lse = attend(queries, kv_all, q_segs, k_segs, block)
    mixed_flat = mixed.reshape(-1, inner_width)

    attn_part = pair_sum(dot(mixed_flat, out_t, ((1,), (1,))), half_rows)
    resid_mid = residual_in + attn_part + outb_full
    normed_two = norm_rows(resid_mid, gain_two, shift_two).astype(BF16)
    flat_two = pair_rows(normed_two).reshape(-1, model_width)
    pre_act = jnp.dot(flat_two, up_full, preferred_element_type=F32) + upb_full
    activated, gelu_pull = jax.vjp(partial(jax.nn.gelu, approximate=True), pre_act)
    activated = activated.astype(BF16)
    act_grad = jnp.dot(grad_flat, down_t, preferred_element_type=F32)
    pre_grad = gelu_pull(act_grad)[0].astype(BF16)
    norm_two_grad = pair_sum(dot(pre_grad, up_full, ((1,), (1,))), half_rows)
    upstream = cotangent.astype(F32)
    mid_grad, gain_two_grad, shift_two_grad = norm_back(resid_mid, gain_two, norm_two_grad)
    resid_grad = upstream + mid_grad
    branch_flat = pair_rows(resid_grad.astype(BF16)).reshape(-1, model_width)
    mixed_grad = jnp.dot(branch_flat, out_t, preferred_element_type=F32).astype(BF16)
    up_grad = dot(flat_two, pre_grad, ((0,), (0,))).astype(BF16)
    down_grad = dot(grad_flat, activated, ((0,), (0,))).astype(BF16)
    out_grad = dot(branch_flat, mixed_flat, ((0,), (0,))).astype(BF16)
    early = jnp.concatenate([out_grad, up_grad, down_grad], axis=1)
    early, mixed_grad = lax.optimization_barrier((early, mixed_grad))
    early_part = lax.psum_scatter(early, "fsdp", scatter_dimension=0, tiled=True)

    query_grad, kv_grad = attend_back(
        queries,
        mixed_grad.reshape(queries.shape),
        mixed,
        lse,
        kv_all,
        q_segs,
        k_segs,
        block,
    )
    if contexts == 2:
        kv_own = kv_grad[:, :, :local_rows].astype(F32)
        kv_own = kv_own + swap(kv_grad[:, :, local_rows:], "ctx").astype(F32)
        kv_own = kv_own.astype(BF16)
    else:
        kv_own = lax.psum_scatter(kv_grad, "ctx", scatter_dimension=2, tiled=True)
    stacked = jnp.concatenate([query_grad, kv_own[:, 0], kv_own[:, 1]], axis=2)
    stacked = stacked.reshape(-1, qkv_width)
    norm_one_grad = pair_sum(dot(stacked, qkv_full, ((1,), (1,))), half_rows)
    qkv_grad = dot(flat_one, stacked, ((0,), (0,)))

    mlp_terms = dot(activated, down_t, ((1,), (1,)))
    mlp_part = pair_sum(mlp_terms, half_rows)
    output = (resid_mid + mlp_part + downb_full).astype(BF16)

    input_part, gain_one_grad, shift_one_grad = norm_back(residual_in, gain_one, norm_one_grad)
    tokens_grad = (resid_grad + input_part).astype(BF16)
    norm_grads = jnp.stack(
        [
            gain_one_grad,
            shift_one_grad,
            jnp.sum(resid_grad, axis=(0, 1)),
            gain_two_grad,
            shift_two_grad,
            jnp.sum(upstream, axis=(0, 1)),
        ]
    )
    norm_grads = norm_grads + swap(norm_grads, "tp")
    bias_sums = jnp.sum(stacked.astype(F32), axis=0)
    qv_grad = jnp.stack([bias_sums[:inner_width], bias_sums[2 * inner_width :]])
    upb_grad = jnp.sum(pre_grad.astype(F32), axis=0)
    small_rows = jnp.concatenate(
        [
            jnp.swapaxes(norm_grads.reshape(6, shards, depth), 0, 1).reshape(shards, -1),
            jnp.moveaxis(qv_grad.reshape(2, heads, shards, span), 2, 0).reshape(shards, -1),
            jnp.moveaxis(upb_grad.reshape(units, shards, span), 1, 0).reshape(shards, -1),
        ],
        axis=1,
    )
    small_rows = jnp.pad(small_rows, ((0, 0), (0, qkv_width - small_rows.shape[1])))
    late = jnp.concatenate(
        [qkv_grad.reshape(shards, depth, qkv_width), small_rows[:, None, :]], axis=1
    ).astype(BF16)
    late_part = lax.psum_scatter(late, "fsdp", scatter_dimension=0, tiled=False)
    early_total = context_total(early_part)
    late_total = context_total(late_part)
    small = late_total[depth]
    start = 6 * depth
    return (
        output,
        tokens_grad,
        small[:depth],
        small[depth : 2 * depth],
        jnp.swapaxes(late_total[:depth].reshape(depth, 3, inner_width), 0, 1),
        small[start : start + qv_size].reshape(2, heads, span),
        early_total[:, :inner_width].T,
        small[2 * depth : 3 * depth],
        small[3 * depth : 4 * depth],
        small[4 * depth : 5 * depth],
        early_total[:, inner_width : inner_width + hidden],
        small[start + qv_size : start + qv_size + units * span].reshape(units, span),
        early_total[:, inner_width + hidden :].T,
        small[5 * depth : 6 * depth],
    )


def solution(mesh):
    placed = (
        P("fsdp", ("ctx", "tp"), None),
        P("fsdp", None),
        P("fsdp"),
        P("fsdp"),
        P(None, "fsdp", "tp"),
        P(None, "tp", "fsdp"),
        P("tp", "fsdp"),
        P("fsdp"),
        P("fsdp"),
        P("fsdp"),
        P("fsdp", "tp"),
        P("tp", "fsdp"),
        P("tp", "fsdp"),
        P("fsdp"),
        P("fsdp", ("ctx", "tp"), None),
    )
    return jax.shard_map(
        local,
        mesh=mesh,
        in_specs=placed,
        out_specs=(
            P("fsdp", ("ctx", "tp"), None),
            P("fsdp", ("ctx", "tp"), None),
            P("fsdp"),
            P("fsdp"),
            P(None, "fsdp", "tp"),
            P(None, "tp", "fsdp"),
            P("tp", "fsdp"),
            P("fsdp"),
            P("fsdp"),
            P("fsdp"),
            P("fsdp", "tp"),
            P("tp", "fsdp"),
            P("tp", "fsdp"),
            P("fsdp"),
        ),
        check_vma=False,
    )
```

time: 1120 us -> 519 us (0.46)
  waiting for transfers between devices: 519 us -> 320 us
  matrix products: 228 us -> 48.5 us
  blocking collectives: 179 us -> 0 us
  other arithmetic: 107 us -> 34 us
  Pallas kernels: 0 us -> 52.6 us
  local copies, waits for them, and re-layouts: 59.8 us -> 36.8 us
    dot_general x26 -> x13, matrix products: 228 us -> 48.5 us  [the longest x8 29 us: dot(): lax.dot_general(left, right, (dims, ((), ())), preferred_element_type=F32)]
    reduce_scatter x9 -> x1, waiting for transfers between devices: 278 us -> 102 us  [local(): lax.psum_scatter(early, 'fsdp', scatter_dimension=0, tiled=True)]
    all_gather x3 -> x0, blocking collectives: 91.2 us -> none  [the longest x1 33.7 us: local(): lax.all_gather(out_weight, 'fsdp', axis=1, tiled=True)]
    unnamed x2 -> x0, blocking collectives: 76.1 us -> none
    all_gather x9 -> x2, waiting for transfers between devices: 145 us -> 70.8 us  [the longest x1 48.1 us: local(): first_all = lax.all_gather(first, 'fsdp', axis=0, tiled=False)]
    ppermute x0 -> x13, waiting for transfers between devices: none -> 72.9 us  [swap(): return lax.ppermute(values, axis, [(0, 1), (1, 0)])]
    pallas_call x0 -> x2, Pallas kernels: none -> 52.6 us  [the longest x1 29 us: attend_back(): pl.pallas_call(partial(backward_kernel, total_len // block), grid_spec=pl...]
    convert_element_type x20 -> x6, other arithmetic: 58.1 us -> 7.9 us  [the longest x1 2.93 us: local(): tokens_grad = (resid_grad + input_part).astype(BF16)]
  transfers between devices with their start and end apart: 21 -> 17, of which waited for: 17 -> 10; matrix products, arithmetic and copies ran while one was open for 6% -> 10% of each run, Pallas kernels for 0% -> 5%
where the time goes in v1:
time: 519 us; the launch traced here: 515 us
  waiting for transfers between devices  320 us (62%)
  Pallas kernels  52.6 us (10%)
  matrix products  48.5 us (9%)
  local copies, waits for them, and re-layouts  36.8 us (7%)
  other arithmetic  34 us (7%)
  between operations  14.8 us (3%)
  starting transfers between devices  8.36 us (2%)
    reduce_scatter x1, waiting for transfers between devices, local(): lax.psum_scatter(early, 'fsdp', scatter_dimension=0, tiled=True)  102 us
    unnamed x5, waiting for transfers between devices  74.2 us
    ppermute x13, waiting for transfers between devices, swap(): return lax.ppermute(values, axis, [(0, 1), (1, 0)])  72.9 us
    all_gather x1, waiting for transfers between devices, local(): first_all = lax.all_gather(first, 'fsdp', axis=0, tiled=False)  48.1 us
    pallas_call x1, Pallas kernels, attend_back(): pl.pallas_call(partial(backward_kernel, total_len // block), grid_spec=pl...  29 us
    dot_general x8, matrix products, dot(): lax.dot_general(left, right, (dims, ((), ())), preferred_element_type=F32)  29 us
    pallas_call x1, Pallas kernels, attend(): pl.pallas_call(partial(forward_kernel, total_len // block), grid_spec=plt...  23.6 us
    all_gather x1, waiting for transfers between devices, local(): second_all = lax.all_gather(second, 'fsdp', axis=0, tiled=True)  22.7 us
  transfers between devices with their start and end apart: 17, of which 10 were waited for; matrix products, arithmetic and copies ran while one was open for 10% of the time, Pallas kernels for 5%

profile of v1, /device:TPU:0, one launch (start us, length us, event | category | flops | bytes accessed | tf_op | source)
XLA Modules:
  0.0 515.1 jit_solution(3099786233737098973)
XLA Ops:
  7.2 0.8 copy.51
  8.1 0.8 copy.52
  8.9 4.1 concatenate.51
  13.1 1.0 copy.66
  14.8 1.3 convert_reduce_fusion
  16.5 48.1 %all-gather.7.cloned.1.call-done = bf16[8,97,1152]{2,1,0:T(8,128)(2,1)} async-done(((bf16[1,97,1152]{2,1,0:T(8,128)(2,1)}), bf16[8,97,1152]{2,1,0:T(8,128)(2,1)}) %all-gather.7.cloned.1.call-update) | async-done | bytes 1787920 | tf_op jit(solution)/shard_map/all_gather | solution.py:293
  64.6 1.1 slice_convert_fusion
  67.0 2.2 pad_maximum_fusion.4
  69.2 0.8 reshape.261
  70.9 1.2 copy-done.14
  72.1 2.6 fusion.52
  75.0 1.5 collective-permute-start.1
  77.2 1.4 pad_add_fusion.q_segs
  78.5 2.7 pad_add_fusion.1.k_segs
  81.3 1.7 constant_dynamic-update-slice_fusion.1
  83.3 2.0 fusion.67.q_ref
  85.4 26.6 %collective-permute-done.1 = bf16[1,1024,768]{2,1,0:T(8,128)(2,1)} collective-permute-done((bf16[1,1024,768]{2,1,0:T(8,128)(2,1)}, bf16[1,1024,768]{2,1,0:T(8,128)(2,1)}, u32[]{:S(2)}, u32[]{:S(2)}) %collective-permute-start.1) | collective-permute-done | bytes 1572896 | tf_op jit(solution)/shard_map/ppermute | solution.py:38
  112.0 1.8 constant_dynamic-update-slice_fusion.k_ref.v_ref
  113.8 23.6 %shard_map.254 = (bf16[1,1024,384]{2,1,0:T(8,128)(2,1)S(1)}, f32[1,3,8,1024]{3,2,1,0:T(8,128)S(1)}) custom-call(s32[1,2]{1,0:T(1,128)S(1)} %pad_add_fusion.q_segs, s32[1,4]{1,0:T(1,128)S(1)} %pad_add_fusion.1.k_segs, bf16[1,1024,384]{2,1,0:T(8,128)(2,1)S(1)} %fusion.67.q_ref, bf16[1,2048,768]{2,1,0:T(8,128)(2,1)S(1)} %constant_dynamic-update-slice_fusion.k_ref.v_ref, ...), custom_call_target="tpu_custom_call" | custom-call | flops 12884901888 | bytes 6291456 | tf_op jit(solution)/shard_map/pallas_call | solution.py:169
  137.4 0.9 copy-done.1
  138.3 22.7 %all-gather.5.cloned.1.call-done = bf16[768,3456]{1,0:T(8,128)(2,1)} async-done(((bf16[96,3456]{1,0:T(8,128)(2,1)}), bf16[768,3456]{1,0:T(8,128)(2,1)}) %all-gather.5.cloned.1.call-update) | async-done | bytes 5308432 | tf_op jit(solution)/shard_map/all_gather | solution.py:323
  161.0 2.4 fusion.51
  163.8 0.8 copy-done.17
  164.5 1.4 collective-permute-done.2
  165.9 1.8 fusion.95
  168.1 1.2 add_convert_fusion.3
  169.8 0.8 slice.247
  170.9 1.0 collective-permute-done.3
  171.9 4.9 fusion.18
  176.8 7.7 %fusion.100 = (bf16[1536]{0:T(1024)(128)(2,1)S(1)}, bf16[1024,1536]{1,0:T(8,128)(2,1)S(1)}) fusion(f32[1024,1536]{1,0:T(8,128)S(1)} %fusion.18, f32[1536]{0:T(1024)S(1)} %add.212, bf16[768,3456]{1,0:T(8,128)(2,1)} %all-gather.5.cloned.1.call-done, bf16[1,512,768]{2,1,0:T(8,128)(2,1)} %collective-permute-done.5, bf16[1,512,768]{2,1,0:T(8,128)(2,1)S(1)} %copy-done.18), kind=kOutput, calls=%fused_computation.148 | convolution fusion | flops 2453666304 | bytes 13378560 | tf_op jit(solution)/shard_map/dot_general | solution.py:358
  184.5 2.6 fusion.60
  187.4 4.0 fusion.57
  191.9 5.5 %convolution_convert_fusion.1 = bf16[768,1536]{1,0:T(8,128)(2,1)} fusion(bf16[1024,1536]{1,0:T(8,128)(2,1)S(1)} %get-tuple-element.113, bf16[1,512,768]{2,1,0:T(8,128)(2,1)} %collective-permute-done.3, bf16[1,512,768]{2,1,0:T(8,128)(2,1)} %add_convert_fusion.3), kind=kOutput, calls=%fused_computation.12 | convolution fusion | flops 2420244480 | bytes 7077888 | tf_op jit(solution)/shard_map/dot_general | solution.py:42
  197.5 0.9 multiply_reduce_fusion
  198.6 2.1 fusion.94
  200.7 1.1 copy-done.7
  202.1 5.6 %convolution_convert_fusion = bf16[768,1536]{1,0:T(8,128)(2,1)} fusion(bf16[1,512,768]{2,1,0:T(8,128)(2,1)} %collective-permute-done.5, bf16[1,512,768]{2,1,0:T(8,128)(2,1)S(1)} %copy-done.19, f32[1024,1536]{1,0:T(8,128)S(1)} %fusion.18, f32[1536]{0:T(1024)S(1)} %add.212), kind=kOutput, calls=%fused_computation.11 | convolution fusion | flops 2435973120 | bytes 10229760 | tf_op jit(solution)/shard_map/dot_general | solution.py:42
  207.7 0.9 copy-done.38
  208.6 1.7 convolution_convert_fusion.5
  210.3 1.4 copy.56
  211.6 5.5 %pad_maximum_fusion = bf16[768,3456]{1,0:T(8,128)(2,1)} fusion(bf16[768,1536]{1,0:T(8,128)(2,1)} %convolution_convert_fusion, bf16[768,1536]{1,0:T(8,128)(2,1)} %convolution_convert_fusion.1, bf16[768,384]{1,0:T(8,128)(2,1)S(1)} %copy.56), kind=kLoop, calls=%fused_computation.10 | loop fusion | flops 15925248 | bytes 10616832 | tf_op jit(solution)/shard_map/concatenate | solution.py:369
  217.2 2.3 convolution_convert_fusion.4
  219.5 29.0 %shard_map.255 = (bf16[1,1024,384]{2,1,0:T(8,128)(2,1)S(1)}, bf16[1,2,2048,384]{3,2,1,0:T(8,128)(2,1)}) custom-call(s32[1,2]{1,0:T(1,128)S(1)} %pad_add_fusion.q_segs, s32[1,4]{1,0:T(1,128)S(1)} %pad_add_fusion.1.k_segs, bf16[1,1024,384]{2,1,0:T(8,128)(2,1)S(1)} %copy-done.4, bf16[1,1024,384]{2,1,0:T(8,128)(2,1)S(1)} %bitcast.108, ...), custom_call_target="tpu_custom_call" | custom-call | flops 32212254720 | bytes 12582912 | tf_op jit(solution)/shard_map/pallas_call | solution.py:207
  248.6 2.9 slice.206
  251.5 1.5 collective-permute-start.8
  252.9 1.2 fusion.78
  254.2 2.8 copy.57
  257.3 31.1 %collective-permute-done.8 = bf16[1,2,1024,384]{3,2,1,0:T(8,128)(2,1)} collective-permute-done((bf16[1,2,1024,384]{3,2,1,0:T(8,128)(2,1)}, bf16[1,2,1024,384]{3,2,1,0:T(8,128)(2,1)}, u32[]{:S(2)}, u32[]{:S(2)}) %collective-permute-start.8) | collective-permute-done | bytes 1572896 | tf_op jit(solution)/shard_map/ppermute | solution.py:38
  288.4 2.3 add_convert_fusion
  290.8 1.3 copy-done.15
  292.1 2.2 fusion.48
  294.4 1.2 copy-done.9
  295.5 0.9 slice.257
  297.1 5.0 convolution_convert_fusion.2
  302.1 2.1 fusion.42
  306.0 2.9 pad_maximum_fusion.2
  309.6 73.6 %reduce-scatter.7.cloned.1.call-done = bf16[1,97,1152]{2,1,0:T(8,128)(2,1)} async-done(((bf16[8,97,1152]{2,1,0:T(8,128)(2,1)}), bf16[1,97,1152]{2,1,0:T(8,128)(2,1)}) %reduce-scatter.7.cloned.1.call-update) | async-done | bytes 223504
  383.2 1.3 collective-permute-start.11
  384.5 2.9 fusion.41
  387.5 102.1 %reduce-scatter.5.cloned.1.call-done = bf16[96,3456]{1,0:T(8,128)(2,1)} async-done(((bf16[768,3456]{1,0:T(8,128)(2,1)}), bf16[96,3456]{1,0:T(8,128)(2,1)}) %reduce-scatter.5.cloned.1.call-update) | async-done | bytes 663568 | tf_op jit(solution)/shard_map/reduce_scatter | solution.py:371
  489.5 1.5 collective-permute-start.12
  493.4 0.8 copy.62
  494.2 12.0 %collective-permute-done.12 = bf16[96,3456]{1,0:T(8,128)(2,1)S(1)} collective-permute-done((bf16[96,3456]{1,0:T(8,128)(2,1)}, bf16[96,3456]{1,0:T(8,128)(2,1)S(1)}, u32[]{:S(2)}, u32[]{:S(2)}) %collective-permute-start.12) | collective-permute-done | bytes 663584 | tf_op jit(solution)/shard_map/ppermute | solution.py:38
  507.1 1.2 slice_bitcast_fusion.2
  (174 shorter events, 14.3 us)
Async XLA Ops:
  7.2 9.0 %copy-start.5 = (bf16[1,512,768]{2,1,0:T(8,128)(2,1)S(1)}, bf16[1,512,768]{2,1,0:T(8,128)(2,1)}, u32[]{:S(2)}) copy-start(bf16[1,512,768]{2,1,0:T(8,128)(2,1)} %param.15) | copy-start | bytes 2359300
  7.2 57.5 %all-gather.7.cloned.1.call-start = ((), (), s32[]{:S(2)}) async-start(), calls=%async_computation.4 | async-start | bytes 2156544 | tf_op jit(solution)/shard_map/all_gather | solution.py:293
  14.8 146.2 %all-gather.5.cloned.1.call-start = ((), (), s32[]{:S(2)}) async-start(), calls=%async_computation.2 | async-start | bytes 5971968 | tf_op jit(solution)/shard_map/all_gather | solution.py:323
  16.1 53.0 %copy-start.29 = (f32[512]{0:T(512)}, f32[512]{0:T(512)S(1)}, u32[]{:S(2)}) copy-start(f32[512]{0:T(512)S(1)} %broadcast_multiply_fusion.5) | copy-start | bytes 6148
  16.5 52.7 %copy-start.31 = (f32[512]{0:T(512)}, f32[512]{0:T(512)S(1)}, u32[]{:S(2)}) copy-start(f32[512]{0:T(512)S(1)} %add_rsqrt_fusion.1) | copy-start | bytes 6148
  64.6 6.1 %copy-start.16 = (bf16[8,97,1152]{2,1,0:T(8,128)(2,1)S(1)}, bf16[8,97,1152]{2,1,0:T(8,128)(2,1)}, u32[]{:S(2)}) copy-start(bf16[8,97,1152]{2,1,0:T(8,128)(2,1)} %all-gather.7.cloned.1.call-done) | copy-start | bytes 5363716
  65.7 0.8 copy-start.25
  66.5 2.7 copy-start.27
  66.9 4.0 copy-start.11
  66.9 3.9 collective-permute-start
  70.8 1.2 copy-start.14
  70.9 3.8 copy-start.20
  72.1 4.5 copy-start.37
  72.1 9.1 %copy-start.26 = (f32[1,6,8,8]{3,1,0,2:T(8,128)S(1)}, f32[1,6,8,8]{3,1,0,2:T(8,128)}, u32[]{:S(2)}) copy-start(f32[1,6,8,8]{3,1,0,2:T(8,128)} %get-tuple-element.98) | copy-start | bytes 4612
  74.7 308.5 %reduce-scatter.7.cloned.1.call-start = ((), (), s32[]{:S(2)}) async-start(), calls=%async_computation.5 | async-start | bytes 2156544
  75.0 37.0 %collective-permute-start.1 = (bf16[1,1024,768]{2,1,0:T(8,128)(2,1)}, bf16[1,1024,768]{2,1,0:T(8,128)(2,1)}, u32[]{:S(2)}, u32[]{:S(2)}) collective-permute-start(bf16[1,1024,768]{2,1,0:T(8,128)(2,1)} %fusion.52), channel_id=1, source_target_pairs={{0,2},{2,0},{1,3},{3,1},{4,6},{6,4},{5,7},{7,5},{8,10},{10,8},{9,1... | collective-permute-start | bytes 4718600 | tf_op jit(solution)/shard_map/ppermute | solution.py:38
  81.3 1.8 copy-start.12
  81.3 2.0 copy-start.21
  85.4 28.4 %copy-start.3 = (bf16[1,1024,384]{2,1,0:T(8,128)(2,1)}, bf16[1,1024,384]{2,1,0:T(8,128)(2,1)S(1)}, u32[]{:S(2)}) copy-start(bf16[1,1024,384]{2,1,0:T(8,128)(2,1)S(1)} %fusion.67.q_ref) | copy-start | bytes 2359300
  113.8 23.6 %copy-start = (bf16[1,2048,768]{2,1,0:T(8,128)(2,1)}, bf16[1,2048,768]{2,1,0:T(8,128)(2,1)S(1)}, u32[]{:S(2)}) copy-start(bf16[1,2048,768]{2,1,0:T(8,128)(2,1)S(1)} %constant_dynamic-update-slice_fusion.k_ref.v_ref) | copy-start | bytes 9437188
  137.4 0.9 copy-start.1
  161.0 2.5 copy-start.36
  161.0 2.6 copy-start.35
  161.0 2.7 copy-start.34
  161.0 4.9 copy-start.6
  163.4 1.1 copy-start.17
  163.4 2.5 collective-permute-start.2
  167.7 1.7 copy-start.18
  167.7 2.8 copy-start.33
  169.3 2.6 collective-permute-start.3
  169.4 7.4 %collective-permute-start.5 = (bf16[1,512,768]{2,1,0:T(8,128)(2,1)S(1)}, bf16[1,512,768]{2,1,0:T(8,128)(2,1)}, u32[]{:S(2)}, u32[]{:S(2)}) collective-permute-start(bf16[1,512,768]{2,1,0:T(8,128)(2,1)S(1)} %copy-done.18), channel_id=1, source_target_pairs={{0,1},{1,0},{2,3},{3,2},{4,5},{5,4},{6,7},{7,6},{8,9},{9,8},{10,11... | collective-permute-start | bytes 2359304 | tf_op jit(solution)/shard_map/ppermute | solution.py:38
  171.9 12.6 %slice-start = ((s8[5308416]{0:T(1024)(128)(4,1)}), s8[4194304]{0:T(1024)(128)(4,1)S(1)}, s32[]{:S(2)}) async-start(s8[5308416]{0:T(1024)(128)(4,1)} %bitcast.125), calls=%async_computation.6 | async-start | bytes 8388608
  176.8 7.7 %slice-start.1 = ((s8[5308416]{0:T(1024)(128)(4,1)}), s8[1114112]{0:T(1024)(128)(4,1)S(1)}, s32[]{:S(2)}) async-start(s8[5308416]{0:T(1024)(128)(4,1)} %bitcast.125), calls=%async_computation.7 | async-start | bytes 2228224
  187.2 10.2 %collective-permute-start.6 = (bf16[1,512,768]{2,1,0:T(8,128)(2,1)S(1)}, bf16[1,512,768]{2,1,0:T(8,128)(2,1)S(1)}, u32[]{:S(2)}, u32[]{:S(2)}) collective-permute-start(bf16[1,512,768]{2,1,0:T(8,128)(2,1)S(1)} %slice.253), channel_id=1, source_target_pairs={{0,1},{1,0},{2,3},{3,2},{4,5},{5,4},{6,7},{7,6},{8,9},{9,8},{10,11... | collective-permute-start | bytes 2359304 | tf_op jit(solution)/shard_map/ppermute | solution.py:38
  191.5 6.9 %collective-permute-start.4 = (bf16[1,512,768]{2,1,0:T(8,128)(2,1)S(1)}, bf16[1,512,768]{2,1,0:T(8,128)(2,1)S(1)}, u32[]{:S(2)}, u32[]{:S(2)}) collective-permute-start(bf16[1,512,768]{2,1,0:T(8,128)(2,1)S(1)} %slice.250), channel_id=1, source_target_pairs={{0,1},{1,0},{2,3},{3,2},{4,5},{5,4},{6,7},{7,6},{8,9},{9,8},{10,11... | collective-permute-start | bytes 2359304 | tf_op jit(solution)/shard_map/ppermute | solution.py:38
  197.5 1.1 copy-start.19
  200.7 1.1 copy-start.7
  201.9 6.7 %copy-start.2 = (bf16[1,1024,384]{2,1,0:T(8,128)(2,1)S(1)}, bf16[1,1024,384]{2,1,0:T(8,128)(2,1)}, u32[]{:S(2)}) copy-start(bf16[1,1024,384]{2,1,0:T(8,128)(2,1)} %copy-done.1) | copy-start | bytes 2359300
  201.9 5.8 %collective-permute-start.7 = (bf16[1,512,768]{2,1,0:T(8,128)(2,1)S(1)}, bf16[1,512,768]{2,1,0:T(8,128)(2,1)S(1)}, u32[]{:S(2)}, u32[]{:S(2)}) collective-permute-start(bf16[1,512,768]{2,1,0:T(8,128)(2,1)S(1)} %convert_element_type.132), channel_id=1, source_target_pairs={{0,1},{1,0},{2,3},{3,2},{4,5},{5,4},{6,7},{7,6},{8,9},{9,8},{10,11... | collective-permute-start | bytes 2359304 | tf_op jit(solution)/shard_map/ppermute | solution.py:38
  207.7 0.9 copy-start.38
  217.2 2.4 copy-start.4
  248.6 4.4 copy-start.13
  248.6 4.4 copy-start.22
  251.5 36.9 %collective-permute-start.8 = (bf16[1,2,1024,384]{3,2,1,0:T(8,128)(2,1)}, bf16[1,2,1024,384]{3,2,1,0:T(8,128)(2,1)}, u32[]{:S(2)}, u32[]{:S(2)}) collective-permute-start(bf16[1,2,1024,384]{3,2,1,0:T(8,128)(2,1)} %slice.206), channel_id=1, source_target_pairs={{0,2},{2,0},{1,3},{3,1},{4,6},{6,4},{5,7},{7,5},{8,10},{10,8},{9,1... | collective-permute-start | bytes 4718600 | tf_op jit(solution)/shard_map/ppermute | solution.py:38
  290.7 1.5 copy-start.15
  294.4 1.2 copy-start.9
  296.5 5.7 %collective-permute-start.9 = (bf16[1,512,768]{2,1,0:T(8,128)(2,1)}, bf16[1,512,768]{2,1,0:T(8,128)(2,1)}, u32[]{:S(2)}, u32[]{:S(2)}) collective-permute-start(bf16[1,512,768]{2,1,0:T(8,128)(2,1)} %slice.257), channel_id=1, source_target_pairs={{0,1},{1,0},{2,3},{3,2},{4,5},{5,4},{6,7},{7,6},{8,9},{9,8},{10,11... | collective-permute-start | bytes 2359304 | tf_op jit(solution)/shard_map/ppermute | solution.py:38
  297.1 5.0 copy-start.10
  297.1 5.0 copy-start.28
  297.1 5.0 copy-start.30
  297.1 5.0 copy-start.32
  304.3 1.4 collective-permute-start.10
  309.0 75.6 %copy-start.8 = (f32[1,512,768]{2,1,0:T(8,128)S(1)}, f32[1,512,768]{2,1,0:T(8,128)}, u32[]{:S(2)}) copy-start(f32[1,512,768]{2,1,0:T(8,128)} %copy-done.7) | copy-start | bytes 4718596
  309.0 180.5 %reduce-scatter.5.cloned.1.call-start = ((), (), s32[]{:S(2)}) async-start(), calls=%async_computation.3 | async-start | bytes 5971968 | tf_op jit(solution)/shard_map/reduce_scatter | solution.py:371
  383.2 107.8 %copy-start.24 = (bf16[1,97,1152]{2,1,0:T(8,128)(2,1)S(1)}, bf16[1,97,1152]{2,1,0:T(8,128)(2,1)}, u32[]{:S(2)}) copy-start(bf16[1,97,1152]{2,1,0:T(8,128)(2,1)} %reduce-scatter.7.cloned.1.call-done) | copy-start | bytes 670468
  383.2 107.8 %collective-permute-start.11 = (bf16[97,1152]{1,0:T(8,128)(2,1)}, bf16[97,1152]{1,0:T(8,128)(2,1)S(1)}, u32[]{:S(2)}, u32[]{:S(2)}) collective-permute-start(bf16[97,1152]{1,0:T(8,128)(2,1)} %bitcast.118), channel_id=1, source_target_pairs={{0,2},{2,0},{1,3},{3,1},{4,6},{6,4},{5,7},{7,5},{8,10},{10,8},{9,1... | collective-permute-start | bytes 670472 | tf_op jit(solution)/shard_map/ppermute | solution.py:38
  489.5 16.7 %copy-start.23 = (bf16[96,3456]{1,0:T(8,128)(2,1)S(1)}, bf16[96,3456]{1,0:T(8,128)(2,1)}, u32[]{:S(2)}) copy-start(bf16[96,3456]{1,0:T(8,128)(2,1)} %reduce-scatter.5.cloned.1.call-done) | copy-start | bytes 1990660
  489.5 16.7 %collective-permute-start.12 = (bf16[96,3456]{1,0:T(8,128)(2,1)}, bf16[96,3456]{1,0:T(8,128)(2,1)S(1)}, u32[]{:S(2)}, u32[]{:S(2)}) collective-permute-start(bf16[96,3456]{1,0:T(8,128)(2,1)} %reduce-scatter.5.cloned.1.call-done), channel_id=1, source_target_pairs={{0,2},{2,0},{1,3},{3,1},{4,6},{6,4},{5,7},{7,5},{8,10},{10,8},{9,1... | collective-permute-start | bytes 1990664 | tf_op jit(solution)/shard_map/ppermute | solution.py:38
Sparse Core Ops, SparseCore 0:
  14.9 49.7 all-gather.6
  74.8 86.1 all-gather.4
  309.1 74.0 reduce-scatter.6
  386.6 102.8 reduce-scatter.4

commit v2 on v1

--- a/solution.py
+++ b/solution.py
@@ -250,10 +250,59 @@
     return terms[:, :half_rows].astype(BF16).astype(F32) + other.astype(F32)
 
 
-def context_total(values):
+def axis_bits():
+    return (lax.axis_size("fsdp") - 1).bit_length()
+
+
+def halving_orders():
+    bits = axis_bits()
+    highest = list(range(bits - 1, 0, -1))
     if lax.axis_size("ctx") == 2:
-        return values.astype(F32) + swap(values, "ctx").astype(F32)
-    return lax.psum(values, "ctx").astype(F32)
+        return (
+            ["ctx", 0] + highest,
+            [0] + highest[:1] + ["ctx"] + highest[1:],
+        )
+    return [0] + highest, highest[:1] + [0] + highest[1:]
+
+
+def flip(values, bit):
+    if bit == "ctx":
+        return swap(values, "ctx")
+    count = lax.axis_size("fsdp")
+    return lax.ppermute(values, "fsdp", [(i, i ^ (1 << bit)) for i in range(count)])
+
+
+def own_bit(bit):
+    if bit == "ctx":
+        return lax.axis_index("ctx")
+    return (lax.axis_index("fsdp") >> bit) & 1
+
+
+def scatter_sum(values, order):
+    shards, rows, columns = values.shape
+    bits = axis_bits()
+    left = list(range(bits - 1, -1, -1))
+    if "ctx" in order:
+        left.append("ctx")
+        rows //= 2
+    values = values.reshape((2,) * len(left) + (rows, columns))
+    for bit in order:
+        at, mine = left.index(bit), own_bit(bit)
+        sent = lax.dynamic_index_in_dim(values, 1 - mine, at, keepdims=False)
+        kept = lax.dynamic_index_in_dim(values, mine, at, keepdims=False)
+        values = kept.astype(F32) + flip(sent, bit).astype(F32)
+        if len(left) > 1:
+            values = values.astype(sent.dtype)
+        left.remove(bit)
+    if "ctx" not in order:
+        if lax.axis_size("ctx") == 2:
+            return values + swap(values, "ctx")
+        return lax.psum(values.astype(BF16), "ctx").astype(F32)
+    values = values.astype(BF16)
+    other = swap(values, "ctx")
+    first = lax.axis_index("ctx") == 0
+    low, high = jnp.where(first, values, other), jnp.where(first, other, values)
+    return jnp.concatenate([low, high], axis=0).astype(F32)
 
 
 def local(
@@ -366,9 +415,11 @@
     up_grad = dot(flat_two, pre_grad, ((0,), (0,))).astype(BF16)
     down_grad = dot(grad_flat, activated, ((0,), (0,))).astype(BF16)
     out_grad = dot(branch_flat, mixed_flat, ((0,), (0,))).astype(BF16)
-    early = jnp.concatenate([out_grad, up_grad, down_grad], axis=1)
-    early, mixed_grad = lax.optimization_barrier((early, mixed_grad))
-    early_part = lax.psum_scatter(early, "fsdp", scatter_dimension=0, tiled=True)
+    wide = jnp.concatenate([up_grad, out_grad], axis=1)
+    wide, down_grad, mixed_grad = lax.optimization_barrier((wide, down_grad, mixed_grad))
+    order_a, order_b = halving_orders()
+    down_total = scatter_sum(down_grad.reshape(shards, depth, hidden), order_a)
+    wide_total = scatter_sum(wide.reshape(shards, depth, hidden + inner_width), order_b)
 
     query_grad, kv_grad = attend_back(
         queries,
@@ -389,7 +440,16 @@
     stacked = jnp.concatenate([query_grad, kv_own[:, 0], kv_own[:, 1]], axis=2)
     stacked = stacked.reshape(-1, qkv_width)
     norm_one_grad = pair_sum(dot(stacked, qkv_full, ((1,), (1,))), half_rows)
-    qkv_grad = dot(flat_one, stacked, ((0,), (0,)))
+    qkv_grad = dot(flat_one, stacked, ((0,), (0,))).astype(BF16)
+    cut = -(-qkv_width // 256) * 128
+    qkv_grad = qkv_grad.reshape(shards, depth, qkv_width)
+    qkv_total = jnp.concatenate(
+        [
+            scatter_sum(qkv_grad[:, :, :cut], order_a),
+            scatter_sum(qkv_grad[:, :, cut:], order_b),
+        ],
+        axis=1,
+    )
 
     mlp_terms = dot(activated, down_t, ((1,), (1,)))
     mlp_part = pair_sum(mlp_terms, half_rows)
@@ -419,29 +479,26 @@
         ],
         axis=1,
     )
-    small_rows = jnp.pad(small_rows, ((0, 0), (0, qkv_width - small_rows.shape[1])))
-    late = jnp.concatenate(
-        [qkv_grad.reshape(shards, depth, qkv_width), small_rows[:, None, :]], axis=1
-    ).astype(BF16)
-    late_part = lax.psum_scatter(late, "fsdp", scatter_dimension=0, tiled=False)
-    early_total = context_total(early_part)
-    late_total = context_total(late_part)
-    small = late_total[depth]
+    small_size = -(-small_rows.shape[1] // 1024) * 1024
+    small_rows = jnp.pad(small_rows, ((0, 0), (0, small_size - small_rows.shape[1])))
+    small = small_rows.reshape(shards, small_size // 128, 128)
+    plain = [bit for bit in order_a if bit != "ctx"]
+    small = scatter_sum(small, plain).reshape(small_size)
     start = 6 * depth
     return (
         output,
         tokens_grad,
         small[:depth],
         small[depth : 2 * depth],
-        jnp.swapaxes(late_total[:depth].reshape(depth, 3, inner_width), 0, 1),
+        jnp.swapaxes(qkv_total.reshape(depth, 3, inner_width), 0, 1),
         small[start : start + qv_size].reshape(2, heads, span),
-        early_total[:, :inner_width].T,
+        wide_total[:, hidden:].T,
         small[2 * depth : 3 * depth],
         small[3 * depth : 4 * depth],
         small[4 * depth : 5 * depth],
-        early_total[:, inner_width : inner_width + hidden],
+        wide_total[:, :hidden],
         small[start + qv_size : start + qv_size + units * span].reshape(units, span),
-        early_total[:, inner_width + hidden :].T,
+        down_total.T,
         small[5 * depth : 6 * depth],
     )
 

time: 519 us -> 418 us (0.81)
  waiting for transfers between devices: 320 us -> 170 us
  Pallas kernels: 52.6 us -> 69.8 us
  local copies, waits for them, and re-layouts: 36.8 us -> 48.1 us
  starting transfers between devices: 8.36 us -> 16 us
  other arithmetic: 34 us -> 41.4 us
    reduce_scatter x1 -> x0, waiting for transfers between devices: 102 us -> none  [local(): lax.psum_scatter(early, 'fsdp', scatter_dimension=0, tiled=True)]
    unnamed x5 -> x2, waiting for transfers between devices: 74.2 us -> 0.03 us
    ppermute x0 -> x15, waiting for transfers between devices: none -> 35.7 us  [flip(): lax.ppermute(values, 'fsdp', [(i, i ^ 1 << bit) for i in range(count)])]
    pallas_call x1, Pallas kernels: 29 us -> 38.4 us  [attend_back(): pl.pallas_call(partial(backward_kernel, total_len // block), grid_spec=pl...]
    convert_element_type x0 -> x17, other arithmetic: none -> 8.56 us  [the longest x12 7.57 us: scatter_sum(): values = values.astype(sent.dtype)]
    concatenate x2 -> x1, other arithmetic: 8.43 us -> 0.21 us  [local(): wide = jnp.concatenate([up_grad, out_grad], axis=1)]
    pallas_call x1, Pallas kernels: 23.6 us -> 31.4 us  [attend(): pl.pallas_call(partial(forward_kernel, total_len // block), grid_spec=plt...]
    all_gather x1, waiting for transfers between devices: 22.7 us -> 15.1 us  [local(): second_all = lax.all_gather(second, 'fsdp', axis=0, tiled=True)]
  transfers between devices with their start and end apart: 17 -> 37, of which waited for: 10 -> 20; matrix products, arithmetic and copies ran while one was open for 10% -> 22% of each run, Pallas kernels for 5% -> 17%
where the time goes in v2:
time: 418 us; the launch traced here: 411 us
  waiting for transfers between devices  170 us (41%)
  Pallas kernels  69.8 us (17%)
  matrix products  50.8 us (12%)
  local copies, waits for them, and re-layouts  48.1 us (12%)
  other arithmetic  41.4 us (10%)
  starting transfers between devices  16 us (4%)
  between operations  15.3 us (4%)
    ppermute x20, waiting for transfers between devices, swap(): return lax.ppermute(values, axis, [(0, 1), (1, 0)])  70.8 us
    all_gather x1, waiting for transfers between devices, local(): first_all = lax.all_gather(first, 'fsdp', axis=0, tiled=False)  48.1 us
    pallas_call x1, Pallas kernels, attend_back(): pl.pallas_call(partial(backward_kernel, total_len // block), grid_spec=pl...  38.4 us
    ppermute x15, waiting for transfers between devices, flip(): lax.ppermute(values, 'fsdp', [(i, i ^ 1 << bit) for i in range(count)])  35.7 us
    pallas_call x1, Pallas kernels, attend(): pl.pallas_call(partial(forward_kernel, total_len // block), grid_spec=plt...  31.4 us
    dot_general x8, matrix products, dot(): lax.dot_general(left, right, (dims, ((), ())), preferred_element_type=F32)  28.1 us
    all_gather x1, waiting for transfers between devices, local(): second_all = lax.all_gather(second, 'fsdp', axis=0, tiled=True)  15.1 us
    unnamed x90, local copies, waits for them, and re-layouts  12.8 us
  transfers between devices with their start and end apart: 37, of which 20 were waited for; matrix products, arithmetic and copies ran while one was open for 22% of the time, Pallas kernels for 17%

profile of v2, /device:TPU:0, one launch (start us, length us, event | category | flops | bytes accessed | tf_op | source)
XLA Modules:
  0.0 411.0 jit_solution(7838521196013413401)
XLA Ops:
  8.9 4.1 concatenate.61
  14.8 1.3 convert_reduce_fusion.2
  16.5 48.1 %all-gather.7.cloned.1.call-done = bf16[8,97,1152]{2,1,0:T(8,128)(2,1)} async-done(((bf16[1,97,1152]{2,1,0:T(8,128)(2,1)}), bf16[8,97,1152]{2,1,0:T(8,128)(2,1)}) %all-gather.7.cloned.1.call-update) | async-done | bytes 1787920 | tf_op jit(solution)/shard_map/all_gather | solution.py:342
  67.0 2.2 pad_maximum_fusion.1
  69.6 1.2 copy-done.20
  70.8 3.8 fusion.43
  74.6 1.5 collective-permute-start.1
  76.7 1.4 pad_add_fusion.q_segs
  78.1 2.7 pad_add_fusion.1.k_segs
  80.8 1.7 constant_dynamic-update-slice_fusion.1
  82.5 2.7 fusion.55.q_ref
  85.2 26.3 %collective-permute-done.1 = bf16[1,1024,768]{2,1,0:T(8,128)(2,1)} collective-permute-done((bf16[1,1024,768]{2,1,0:T(8,128)(2,1)}, bf16[1,1024,768]{2,1,0:T(8,128)(2,1)}, u32[]{:S(2)}, u32[]{:S(2)}) %collective-permute-start.1) | collective-permute-done | bytes 1572896 | tf_op jit(solution)/shard_map/ppermute | solution.py:38
  111.5 1.9 constant_dynamic-update-slice_fusion.k_ref.v_ref
  113.4 31.4 %shard_map.254 = (bf16[1,1024,384]{2,1,0:T(8,128)(2,1)S(1)}, f32[1,3,8,1024]{3,2,1,0:T(8,128)S(1)}) custom-call(s32[1,2]{1,0:T(1,128)S(1)} %pad_add_fusion.q_segs, s32[1,4]{1,0:T(1,128)S(1)} %pad_add_fusion.1.k_segs, bf16[1,1024,384]{2,1,0:T(8,128)(2,1)S(1)} %fusion.55.q_ref, bf16[1,2048,768]{2,1,0:T(8,128)(2,1)S(1)} %constant_dynamic-update-slice_fusion.k_ref.v_ref, ...), custom_call_target="tpu_custom_call" | custom-call | flops 12884901888 | bytes 6291456 | tf_op jit(solution)/shard_map/pallas_call | solution.py:169
  145.8 15.1 %all-gather.5.cloned.1.call-done = bf16[768,3456]{1,0:T(8,128)(2,1)} async-done(((bf16[96,3456]{1,0:T(8,128)(2,1)}), bf16[768,3456]{1,0:T(8,128)(2,1)}) %all-gather.5.cloned.1.call-update) | async-done | bytes 5308432 | tf_op jit(solution)/shard_map/all_gather | solution.py:372
  160.9 2.4 fusion.42
  164.4 1.4 collective-permute-done.2
  165.8 1.8 fusion.95
  167.9 1.2 add_convert_fusion.3
  170.0 1.7 collective-permute-done.3
  171.8 4.9 %fusion.17 = f32[1024,1536]{1,0:T(8,128)S(1)} fusion(bf16[768,3456]{1,0:T(8,128)(2,1)} %all-gather.5.cloned.1.call-done, bf16[1,512,768]{2,1,0:T(8,128)(2,1)} %collective-permute-done.3, bf16[1,512,768]{2,1,0:T(8,128)(2,1)} %add_convert_fusion.3), kind=kOutput, calls=%fused_computation.32 | convolution fusion | flops 2419064832 | bytes 10223616 | tf_op jit(solution)/shard_map/dot_general | solution.py:404
  176.7 9.3 %convert_reduce_fusion = (f32[1536]{0:T(1024)S(1)}, bf16[1024,1536]{1,0:T(8,128)(2,1)S(1)}) fusion(f32[1024,1536]{1,0:T(8,128)S(1)} %fusion.17, f32[1536]{0:T(1024)S(1)} %add.339, bf16[768,3456]{1,0:T(8,128)(2,1)} %all-gather.5.cloned.1.call-done, bf16[1,512,768]{2,1,0:T(8,128)(2,1)} %collective-permute-done.5, bf16[1,512,768]{2,1,0:T(8,128)(2,1)S(1)} %copy-done.25), kind=kOutput, calls=%fused_computation.9 | convolution fusion | flops 2455239168 | bytes 13381632 | tf_op jit(solution)/shard_map/dot_general | solution.py:407
  186.0 3.7 fusion.47
  189.7 2.1 slice.220
  191.9 4.0 fusion.44
  197.3 5.8 %convolution_convert_fusion.1 = bf16[768,1536]{1,0:T(8,128)(2,1)} fusion(bf16[1024,1536]{1,0:T(8,128)(2,1)S(1)} %get-tuple-element.141, bf16[1,512,768]{2,1,0:T(8,128)(2,1)} %collective-permute-done.3, bf16[1,512,768]{2,1,0:T(8,128)(2,1)} %add_convert_fusion.3), kind=kOutput, calls=%fused_computation.13 | convolution fusion | flops 2420244480 | bytes 7077888 | tf_op jit(solution)/shard_map/dot_general | solution.py:42
  203.9 2.2 multiply_reduce_fusion
  206.1 3.4 fusion.94
  210.9 4.2 %convolution_convert_fusion = bf16[768,1536]{1,0:T(8,128)(2,1)S(1)} fusion(bf16[1,512,768]{2,1,0:T(8,128)(2,1)} %collective-permute-done.5, bf16[1,512,768]{2,1,0:T(8,128)(2,1)S(1)} %copy-done.26, f32[1024,1536]{1,0:T(8,128)S(1)} %copy-done.38, f32[1536]{0:T(1024)S(1)} %add.339), kind=kOutput, calls=%fused_computation.12 | convolution fusion | flops 2435973120 | bytes 10229760 | tf_op jit(solution)/shard_map/dot_general | solution.py:42
  219.4 2.0 convolution_convert_fusion.5
  221.7 1.2 copy.110
  223.7 1.5 collective-permute-start.30
  225.3 38.4 %shard_map.255 = (bf16[1,1024,384]{2,1,0:T(8,128)(2,1)S(1)}, bf16[1,2,2048,384]{3,2,1,0:T(8,128)(2,1)}) custom-call(s32[1,2]{1,0:T(1,128)S(1)} %pad_add_fusion.q_segs, s32[1,4]{1,0:T(1,128)S(1)} %pad_add_fusion.1.k_segs, bf16[1,1024,384]{2,1,0:T(8,128)(2,1)S(1)} %copy-done.4, bf16[1,1024,384]{2,1,0:T(8,128)(2,1)S(1)} %bitcast.191, ...), custom_call_target="tpu_custom_call" | custom-call | flops 32212254720 | bytes 12582912 | tf_op jit(solution)/shard_map/pallas_call | solution.py:207
  263.7 1.6 slice.178
  266.6 1.9 fusion.7
  269.8 31.7 %collective-permute-done.8 = bf16[1,2,1024,384]{3,2,1,0:T(8,128)(2,1)S(1)} collective-permute-done((bf16[1,2,1024,384]{3,2,1,0:T(8,128)(2,1)S(1)}, bf16[1,2,1024,384]{3,2,1,0:T(8,128)(2,1)S(1)}, u32[]{:S(2)}, u32[]{:S(2)}) %collective-permute-start.8) | collective-permute-done | bytes 1572896 | tf_op jit(solution)/shard_map/ppermute | solution.py:38
  302.5 1.3 copy-done.28
  303.8 3.4 convolution_convert_fusion.2
  311.1 1.5 reshape.303
  314.3 3.7 fusion.41
  318.2 1.6 fusion.59
  319.9 2.9 collective-permute-done.20
  323.1 13.8 %collective-permute-done.32 = bf16[2,48,1536]{2,1,0:T(8,128)(2,1)S(1)} collective-permute-done((bf16[2,48,1536]{2,1,0:T(8,128)(2,1)S(1)}, bf16[2,48,1536]{2,1,0:T(8,128)(2,1)S(1)}, u32[]{:S(2)}, u32[]{:S(2)}) %collective-permute-start.32) | collective-permute-done | bytes 294944 | tf_op jit(solution)/shard_map/ppermute | solution.py:272
  338.4 2.8 collective-permute-done.21
  341.6 1.3 fusion.50
  343.7 1.7 collective-permute-start.27
  346.5 3.6 collective-permute-done.23
  351.4 1.5 fusion.38
  354.1 1.3 stack.36
  355.5 2.4 collective-permute-done.34
  357.9 1.7 broadcast_select_fusion.3
  360.2 1.4 add.354
  361.6 1.4 reshape.301
  363.0 1.4 copy.78
  364.4 1.4 reshape.302
  368.4 2.0 collective-permute-done.11
  371.0 2.9 fusion.37
  373.9 1.2 collective-permute-done.12
  376.0 2.7 collective-permute-done.13
  378.7 1.7 collective-permute-start.14
  385.4 2.2 collective-permute-done.18
  387.6 2.4 collective-permute-start.19
  392.3 4.4 %collective-permute-done.28 = bf16[48,1920]{1,0:T(8,128)(2,1)S(1)} collective-permute-done((bf16[48,1920]{1,0:T(8,128)(2,1)S(1)}, bf16[48,1920]{1,0:T(8,128)(2,1)S(1)}, u32[]{:S(2)}, u32[]{:S(2)}) %collective-permute-start.28) | collective-permute-done | bytes 184352 | tf_op jit(solution)/shard_map/ppermute | solution.py:272
  397.9 4.5 %collective-permute-done.29 = bf16[48,1920]{1,0:T(8,128)(2,1)S(1)} collective-permute-done((bf16[48,1920]{1,0:T(8,128)(2,1)S(1)}, bf16[48,1920]{1,0:T(8,128)(2,1)S(1)}, u32[]{:S(2)}, u32[]{:S(2)}) %collective-permute-start.29) | collective-permute-done | bytes 184352 | tf_op jit(solution)/shard_map/ppermute | solution.py:38
  (255 shorter events, 49.9 us)
Async XLA Ops:
  7.2 9.0 %copy-start.5 = (bf16[1,512,768]{2,1,0:T(8,128)(2,1)S(1)}, bf16[1,512,768]{2,1,0:T(8,128)(2,1)}, u32[]{:S(2)}) copy-start(bf16[1,512,768]{2,1,0:T(8,128)(2,1)} %param.15) | copy-start | bytes 2359300
  7.2 57.5 %all-gather.7.cloned.1.call-start = ((), (), s32[]{:S(2)}) async-start(), calls=%async_computation.1 | async-start | bytes 2156544 | tf_op jit(solution)/shard_map/all_gather | solution.py:342
  14.8 146.1 %all-gather.5.cloned.1.call-start = ((), (), s32[]{:S(2)}) async-start(), calls=%async_computation | async-start | bytes 5971968 | tf_op jit(solution)/shard_map/all_gather | solution.py:372
  16.5 53.0 %copy-start.31 = (f32[512]{0:T(512)}, f32[512]{0:T(512)S(1)}, u32[]{:S(2)}) copy-start(f32[512]{0:T(512)S(1)} %add_rsqrt_fusion.1) | copy-start | bytes 6148
  64.6 4.7 %copy-start.21 = (bf16[8,97,1152]{2,1,0:T(8,128)(2,1)S(1)}, bf16[8,97,1152]{2,1,0:T(8,128)(2,1)}, u32[]{:S(2)}) copy-start(bf16[8,97,1152]{2,1,0:T(8,128)(2,1)} %all-gather.7.cloned.1.call-done) | copy-start | bytes 5363716
  66.9 2.7 copy-start.27
  66.9 2.6 collective-permute-start
  70.8 5.3 %copy-start.36 = (s32[1,4]{1,0:T(1,128)S(1)}, s32[1,4]{1,0:T(1,128)}, u32[]{:S(2)}) copy-start(s32[1,4]{1,0:T(1,128)} %param.16) | copy-start | bytes 52
  74.6 37.0 %collective-permute-start.1 = (bf16[1,1024,768]{2,1,0:T(8,128)(2,1)}, bf16[1,1024,768]{2,1,0:T(8,128)(2,1)}, u32[]{:S(2)}, u32[]{:S(2)}) collective-permute-start(bf16[1,1024,768]{2,1,0:T(8,128)(2,1)} %fusion.43), channel_id=1, source_target_pairs={{0,2},{2,0},{1,3},{3,1},{4,6},{6,4},{5,7},{7,5},{8,10},{10,8},{9,1... | collective-permute-start | bytes 4718600 | tf_op jit(solution)/shard_map/ppermute | solution.py:38
  85.2 28.2 %copy-start.3 = (bf16[1,1024,384]{2,1,0:T(8,128)(2,1)}, bf16[1,1024,384]{2,1,0:T(8,128)(2,1)S(1)}, u32[]{:S(2)}) copy-start(bf16[1,1024,384]{2,1,0:T(8,128)(2,1)S(1)} %fusion.55.q_ref) | copy-start | bytes 2359300
  113.4 31.4 %copy-start = (bf16[1,2048,768]{2,1,0:T(8,128)(2,1)}, bf16[1,2048,768]{2,1,0:T(8,128)(2,1)S(1)}, u32[]{:S(2)}) copy-start(bf16[1,2048,768]{2,1,0:T(8,128)(2,1)S(1)} %constant_dynamic-update-slice_fusion.k_ref.v_ref) | copy-start | bytes 9437188
  160.9 2.5 copy-start.35
  160.9 2.6 copy-start.34
  160.9 4.9 %copy-start.6 = (bf16[1,512,768]{2,1,0:T(8,128)(2,1)S(1)}, bf16[1,512,768]{2,1,0:T(8,128)(2,1)}, u32[]{:S(2)}) copy-start(bf16[1,512,768]{2,1,0:T(8,128)(2,1)} %param.15) | copy-start | bytes 2359300
  163.3 2.5 collective-permute-start.2
  169.1 2.6 collective-permute-start.3
  169.3 7.4 %collective-permute-start.5 = (bf16[1,512,768]{2,1,0:T(8,128)(2,1)S(1)}, bf16[1,512,768]{2,1,0:T(8,128)(2,1)}, u32[]{:S(2)}, u32[]{:S(2)}) collective-permute-start(bf16[1,512,768]{2,1,0:T(8,128)(2,1)S(1)} %copy-done.25), channel_id=1, source_target_pairs={{0,1},{1,0},{2,3},{3,2},{4,5},{5,4},{6,7},{7,6},{8,9},{9,8},{10,11... | collective-permute-start | bytes 2359304 | tf_op jit(solution)/shard_map/ppermute | solution.py:38
  171.8 14.2 %slice-start = ((s8[5308416]{0:T(1024)(128)(4,1)}), s8[4194304]{0:T(1024)(128)(4,1)S(1)}, s32[]{:S(2)}) async-start(s8[5308416]{0:T(1024)(128)(4,1)} %bitcast.218), calls=%async_computation.2 | async-start | bytes 8388608
  176.7 15.3 %copy-start.37 = (f32[1024,1536]{1,0:T(8,128)}, f32[1024,1536]{1,0:T(8,128)S(1)}, u32[]{:S(2)}) copy-start(f32[1024,1536]{1,0:T(8,128)S(1)} %fusion.17) | copy-start | bytes 18874372
  176.7 9.3 %slice-start.1 = ((s8[5308416]{0:T(1024)(128)(4,1)}), s8[1114112]{0:T(1024)(128)(4,1)S(1)}, s32[]{:S(2)}) async-start(s8[5308416]{0:T(1024)(128)(4,1)} %bitcast.218), calls=%async_computation.3 | async-start | bytes 2228224
  191.8 12.1 %collective-permute-start.6 = (bf16[1,512,768]{2,1,0:T(8,128)(2,1)}, bf16[1,512,768]{2,1,0:T(8,128)(2,1)S(1)}, u32[]{:S(2)}, u32[]{:S(2)}) collective-permute-start(bf16[1,512,768]{2,1,0:T(8,128)(2,1)} %slice.220), channel_id=1, source_target_pairs={{0,1},{1,0},{2,3},{3,2},{4,5},{5,4},{6,7},{7,6},{8,9},{9,8},{10,11... | collective-permute-start | bytes 2359304 | tf_op jit(solution)/shard_map/ppermute | solution.py:38
  195.9 7.1 %copy-start.22 = (bf16[1,1024,768]{2,1,0:T(8,128)(2,1)}, bf16[1,1024,768]{2,1,0:T(8,128)(2,1)S(1)}, u32[]{:S(2)}) copy-start(bf16[1,1024,768]{2,1,0:T(8,128)(2,1)S(1)} %fusion.44) | copy-start | bytes 4718596
  196.9 9.2 %collective-permute-start.4 = (bf16[1,512,768]{2,1,0:T(8,128)(2,1)}, bf16[1,512,768]{2,1,0:T(8,128)(2,1)}, u32[]{:S(2)}, u32[]{:S(2)}) collective-permute-start(bf16[1,512,768]{2,1,0:T(8,128)(2,1)} %slice.217), channel_id=1, source_target_pairs={{0,1},{1,0},{2,3},{3,2},{4,5},{5,4},{6,7},{7,6},{8,9},{9,8},{10,11... | collective-permute-start | bytes 2359304 | tf_op jit(solution)/shard_map/ppermute | solution.py:38
  203.9 2.2 copy-start.26
  206.1 4.8 %copy-start.38 = (f32[1024,1536]{1,0:T(8,128)S(1)}, f32[1024,1536]{1,0:T(8,128)}, u32[]{:S(2)}) copy-start(f32[1024,1536]{1,0:T(8,128)} %copy-done.37) | copy-start | bytes 18874372
  210.7 6.8 %copy-start.2 = (bf16[1,1024,384]{2,1,0:T(8,128)(2,1)S(1)}, bf16[1,1024,384]{2,1,0:T(8,128)(2,1)}, u32[]{:S(2)}) copy-start(bf16[1,1024,384]{2,1,0:T(8,128)(2,1)} %copy-done.1) | copy-start | bytes 2359300
  210.7 6.8 %collective-permute-start.7 = (bf16[1,512,768]{2,1,0:T(8,128)(2,1)S(1)}, bf16[1,512,768]{2,1,0:T(8,128)(2,1)S(1)}, u32[]{:S(2)}, u32[]{:S(2)}) collective-permute-start(bf16[1,512,768]{2,1,0:T(8,128)(2,1)S(1)} %convert_element_type.321), channel_id=1, source_target_pairs={{0,1},{1,0},{2,3},{3,2},{4,5},{5,4},{6,7},{7,6},{8,9},{9,8},{10,11... | collective-permute-start | bytes 2359304 | tf_op jit(solution)/shard_map/ppermute | solution.py:38
  222.9 43.7 %collective-permute-start.25 = (bf16[2,2,2,48,1920]{4,3,1,2,0:T(8,128)(2,1)}, bf16[2,2,2,48,1920]{4,3,1,2,0:T(8,128)(2,1)}, u32[]{:S(2)}, u32[]{:S(2)}) collective-permute-start(bf16[2,2,2,48,1920]{4,3,1,2,0:T(8,128)(2,1)} %bitcast.187), channel_id=1, source_target_pairs={{0,4},{4,0},{8,12},{12,8},{16,20},{20,16},{24,28},{28,24},{1,5},{5... | collective-permute-start | bytes 4423688 | tf_op jit(solution)/shard_map/ppermute | solution.py:272
  223.7 41.6 %collective-permute-start.30 = (bf16[2,2,2,48,1536]{4,3,1,0,2:T(8,128)(2,1)S(1)}, bf16[2,2,2,48,1536]{4,3,1,0,2:T(8,128)(2,1)S(1)}, u32[]{:S(2)}, u32[]{:S(2)}) collective-permute-start(bf16[2,2,2,48,1536]{4,3,1,0,2:T(8,128)(2,1)S(1)} %bitcast.203), channel_id=1, source_target_pairs={{0,2},{2,0},{1,3},{3,1},{4,6},{6,4},{5,7},{7,5},{8,10},{10,8},{9,1... | collective-permute-start | bytes 3538952 | tf_op jit(solution)/shard_map/ppermute | solution.py:38
  265.3 36.2 %collective-permute-start.8 = (bf16[1,2,1024,384]{3,2,1,0:T(8,128)(2,1)S(1)}, bf16[1,2,1024,384]{3,2,1,0:T(8,128)(2,1)S(1)}, u32[]{:S(2)}, u32[]{:S(2)}) collective-permute-start(bf16[1,2,1024,384]{3,2,1,0:T(8,128)(2,1)S(1)} %slice.178), channel_id=1, source_target_pairs={{0,2},{2,0},{1,3},{3,1},{4,6},{6,4},{5,7},{7,5},{8,10},{10,8},{9,1... | collective-permute-start | bytes 4718600 | tf_op jit(solution)/shard_map/ppermute | solution.py:38
  266.6 51.6 %collective-permute-start.31 = (bf16[2,2,48,1536]{3,2,1,0:T(8,128)(2,1)}, bf16[2,2,48,1536]{3,2,1,0:T(8,128)(2,1)}, u32[]{:S(2)}, u32[]{:S(2)}) collective-permute-start(bf16[2,2,48,1536]{3,2,1,0:T(8,128)(2,1)} %dynamic-slice_bitcast_fusion.1), channel_id=1, source_target_pairs={{0,4},{4,0},{8,12},{12,8},{16,20},{20,16},{24,28},{28,24},{1,5},{5... | collective-permute-start | bytes 1769480 | tf_op jit(solution)/shard_map/ppermute | solution.py:272
  266.6 34.9 %copy-start.13 = (bf16[1,2,2048,384]{3,2,1,0:T(8,128)(2,1)S(1)}, bf16[1,2,2048,384]{3,2,1,0:T(8,128)(2,1)}, u32[]{:S(2)}) copy-start(bf16[1,2,2048,384]{3,2,1,0:T(8,128)(2,1)} %get-tuple-element.29) | copy-start | bytes 9437188
  269.4 72.2 %collective-permute-start.26 = (bf16[2,2,48,1920]{3,2,0,1:T(8,128)(2,1)}, bf16[2,2,48,1920]{3,2,0,1:T(8,128)(2,1)}, u32[]{:S(2)}, u32[]{:S(2)}) collective-permute-start(bf16[2,2,48,1920]{3,2,0,1:T(8,128)(2,1)} %dynamic-slice_bitcast_fusion), channel_id=1, source_target_pairs={{0,16},{4,20},{8,24},{12,28},{16,0},{20,4},{24,8},{28,12},{1,17},{... | collective-permute-start | bytes 2211848 | tf_op jit(solution)/shard_map/ppermute | solution.py:272
  302.0 5.1 %copy-start.14 = (bf16[1,1024,384]{2,1,0:T(8,128)(2,1)}, bf16[1,1024,384]{2,1,0:T(8,128)(2,1)S(1)}, u32[]{:S(2)}) copy-start(bf16[1,1024,384]{2,1,0:T(8,128)(2,1)S(1)} %get-tuple-element.104) | copy-start | bytes 2359300
  302.1 5.1 %copy-start.16 = (bf16[1,1024,384]{2,1,0:T(8,128)(2,1)}, bf16[1,1024,384]{2,1,0:T(8,128)(2,1)S(1)}, u32[]{:S(2)}) copy-start(bf16[1,1024,384]{2,1,0:T(8,128)(2,1)S(1)} %get-tuple-element.105) | copy-start | bytes 2359300
  312.8 10.1 %collective-permute-start.20 = (bf16[2,2,2,48,512]{4,3,1,2,0:T(8,128)(2,1)S(1)}, bf16[2,2,2,48,512]{4,3,1,2,0:T(8,128)(2,1)S(1)}, u32[]{:S(2)}, u32[]{:S(2)}) collective-permute-start(bf16[2,2,2,48,512]{4,3,1,2,0:T(8,128)(2,1)S(1)} %bitcast.205), channel_id=1, source_target_pairs={{0,4},{4,0},{8,12},{12,8},{16,20},{20,16},{24,28},{28,24},{1,5},{5... | collective-permute-start | bytes 1179656 | tf_op jit(solution)/shard_map/ppermute | solution.py:272
  313.9 23.2 %collective-permute-start.15 = (bf16[2,2,2,48,640]{4,3,2,1,0:T(8,128)(2,1)S(1)}, bf16[2,2,2,48,640]{4,3,2,1,0:T(8,128)(2,1)S(1)}, u32[]{:S(2)}, u32[]{:S(2)}) collective-permute-start(bf16[2,2,2,48,640]{4,3,2,1,0:T(8,128)(2,1)S(1)} %dynamic-slice_bitcast_fusion.2), channel_id=1, source_target_pairs={{0,2},{2,0},{1,3},{3,1},{4,6},{6,4},{5,7},{7,5},{8,10},{10,8},{9,1... | collective-permute-start | bytes 1474568 | tf_op jit(solution)/shard_map/ppermute | solution.py:38
  318.0 33.4 %copy-start.12 = (bf16[1,1024,768]{2,1,0:T(8,128)(2,1)}, bf16[1,1024,768]{2,1,0:T(8,128)(2,1)S(1)}, u32[]{:S(2)}) copy-start(bf16[1,1024,768]{2,1,0:T(8,128)(2,1)S(1)} %fusion.41) | copy-start | bytes 4718596
  318.1 33.3 %collective-permute-start.9 = (bf16[1,512,768]{2,1,0:T(8,128)(2,1)S(1)}, bf16[1,512,768]{2,1,0:T(8,128)(2,1)S(1)}, u32[]{:S(2)}, u32[]{:S(2)}) collective-permute-start(bf16[1,512,768]{2,1,0:T(8,128)(2,1)S(1)} %slice.224), channel_id=1, source_target_pairs={{0,1},{1,0},{2,3},{3,2},{4,5},{5,4},{6,7},{7,6},{8,9},{9,8},{10,11... | collective-permute-start | bytes 2359304 | tf_op jit(solution)/shard_map/ppermute | solution.py:38
  319.9 17.1 %collective-permute-start.32 = (bf16[2,48,1536]{2,1,0:T(8,128)(2,1)S(1)}, bf16[2,48,1536]{2,1,0:T(8,128)(2,1)S(1)}, u32[]{:S(2)}, u32[]{:S(2)}) collective-permute-start(bf16[2,48,1536]{2,1,0:T(8,128)(2,1)S(1)} %dynamic-slice_bitcast_fusion.4), channel_id=1, source_target_pairs={{0,16},{4,20},{8,24},{12,28},{16,0},{20,4},{24,8},{28,12},{1,17},{... | collective-permute-start | bytes 884744 | tf_op jit(solution)/shard_map/ppermute | solution.py:272
  323.0 18.6 %copy-start.10 = (bf16[2,2,2,48,1920]{4,3,1,2,0:T(8,128)(2,1)S(1)}, bf16[2,2,2,48,1920]{4,3,1,2,0:T(8,128)(2,1)}, u32[]{:S(2)}) copy-start(bf16[2,2,2,48,1920]{4,3,1,2,0:T(8,128)(2,1)} %copy-done.9) | copy-start | bytes 4423684
  323.0 18.2 %collective-permute-start.21 = (bf16[2,2,48,512]{3,2,0,1:T(8,128)(2,1)S(1)}, bf16[2,2,48,512]{3,2,0,1:T(8,128)(2,1)S(1)}, u32[]{:S(2)}, u32[]{:S(2)}) collective-permute-start(bf16[2,2,48,512]{3,2,0,1:T(8,128)(2,1)S(1)} %dynamic-slice_bitcast_fusion.6), channel_id=1, source_target_pairs={{0,16},{4,20},{8,24},{12,28},{16,0},{20,4},{24,8},{28,12},{1,17},{... | collective-permute-start | bytes 589832 | tf_op jit(solution)/shard_map/ppermute | solution.py:272
  337.1 9.0 %collective-permute-start.33 = (bf16[48,1536]{1,0:T(8,128)(2,1)S(1)}, bf16[48,1536]{1,0:T(8,128)(2,1)S(1)}, u32[]{:S(2)}, u32[]{:S(2)}) collective-permute-start(bf16[48,1536]{1,0:T(8,128)(2,1)S(1)} %dynamic-slice_bitcast_fusion.8), channel_id=1, source_target_pairs={{0,8},{4,12},{8,0},{12,4},{16,24},{20,28},{24,16},{28,20},{1,9},{5... | collective-permute-start | bytes 442376 | tf_op jit(solution)/shard_map/ppermute | solution.py:272
  337.3 13.2 %collective-permute-start.16 = (bf16[2,2,48,640]{3,2,1,0:T(8,128)(2,1)S(1)}, bf16[2,2,48,640]{3,2,1,0:T(8,128)(2,1)S(1)}, u32[]{:S(2)}, u32[]{:S(2)}) collective-permute-start(bf16[2,2,48,640]{3,2,1,0:T(8,128)(2,1)S(1)} %dynamic-slice_bitcast_fusion.5), channel_id=1, source_target_pairs={{0,4},{4,0},{8,12},{12,8},{16,20},{20,16},{24,28},{28,24},{1,5},{5... | collective-permute-start | bytes 737288 | tf_op jit(solution)/shard_map/ppermute | solution.py:272
  341.3 4.7 %collective-permute-start.22 = (bf16[2,48,512]{2,1,0:T(8,128)(2,1)S(1)}, bf16[2,48,512]{2,1,0:T(8,128)(2,1)S(1)}, u32[]{:S(2)}, u32[]{:S(2)}) collective-permute-start(bf16[2,48,512]{2,1,0:T(8,128)(2,1)S(1)} %dynamic-slice_bitcast_fusion.10), channel_id=1, source_target_pairs={{0,2},{2,0},{1,3},{3,1},{4,6},{6,4},{5,7},{7,5},{8,10},{10,8},{9,1... | collective-permute-start | bytes 294920 | tf_op jit(solution)/shard_map/ppermute | solution.py:38
  342.9 8.5 %copy-start.32 = (f32[512]{0:T(512)S(1)}, f32[512]{0:T(512)}, u32[]{:S(2)}) copy-start(f32[512]{0:T(512)} %copy-done.31) | copy-start | bytes 6148
  343.7 46.3 %collective-permute-start.27 = (bf16[2,48,1920]{2,1,0:T(8,128)(2,1)}, bf16[2,48,1920]{2,1,0:T(8,128)(2,1)}, u32[]{:S(2)}, u32[]{:S(2)}) collective-permute-start(bf16[2,48,1920]{2,1,0:T(8,128)(2,1)} %dynamic-slice_bitcast_fusion.3), channel_id=1, source_target_pairs={{0,2},{2,0},{1,3},{3,1},{4,6},{6,4},{5,7},{7,5},{8,10},{10,8},{9,1... | collective-permute-start | bytes 1105928 | tf_op jit(solution)/shard_map/ppermute | solution.py:38
  346.0 4.2 %collective-permute-start.23 = (bf16[48,512]{1,0:T(8,128)(2,1)S(1)}, bf16[48,512]{1,0:T(8,128)(2,1)S(1)}, u32[]{:S(2)}, u32[]{:S(2)}) collective-permute-start(bf16[48,512]{1,0:T(8,128)(2,1)S(1)} %dynamic-slice_bitcast_fusion.12), channel_id=1, source_target_pairs={{0,8},{4,12},{8,0},{12,4},{16,24},{20,28},{24,16},{28,20},{1,9},{5... | collective-permute-start | bytes 147464 | tf_op jit(solution)/shard_map/ppermute | solution.py:272
  346.2 9.3 %copy-start.30 = (bf16[48,1536]{1,0:T(8,128)(2,1)}, bf16[48,1536]{1,0:T(8,128)(2,1)S(1)}, u32[]{:S(2)}) copy-start(bf16[48,1536]{1,0:T(8,128)(2,1)S(1)} %fusion.73) | copy-start | bytes 442372
  346.2 11.7 %collective-permute-start.34 = (bf16[48,1536]{1,0:T(8,128)(2,1)S(1)}, bf16[48,1536]{1,0:T(8,128)(2,1)}, u32[]{:S(2)}, u32[]{:S(2)}) collective-permute-start(bf16[48,1536]{1,0:T(8,128)(2,1)S(1)} %fusion.73), channel_id=1, source_target_pairs={{0,2},{2,0},{1,3},{3,1},{4,6},{6,4},{5,7},{7,5},{8,10},{10,8},{9,1... | collective-permute-start | bytes 442376 | tf_op jit(solution)/shard_map/ppermute | solution.py:38
  350.2 30.2 %collective-permute-start.24 = (bf16[48,512]{1,0:T(8,128)(2,1)S(1)}, bf16[48,512]{1,0:T(8,128)(2,1)}, u32[]{:S(2)}, u32[]{:S(2)}) collective-permute-start(bf16[48,512]{1,0:T(8,128)(2,1)S(1)} %fusion.77), channel_id=1, source_target_pairs={{0,2},{2,0},{1,3},{3,1},{4,6},{6,4},{5,7},{7,5},{8,10},{10,8},{9,1... | collective-permute-start | bytes 147464 | tf_op jit(solution)/shard_map/ppermute | solution.py:38
  351.3 19.7 %copy-start.8 = (f32[1,512,768]{2,1,0:T(8,128)S(1)}, f32[1,512,768]{2,1,0:T(8,128)}, u32[]{:S(2)}) copy-start(f32[1,512,768]{2,1,0:T(8,128)} %copy-done.7) | copy-start | bytes 4718596
  351.3 19.7 %copy-start.33 = (f32[512]{0:T(512)S(1)}, f32[512]{0:T(512)}, u32[]{:S(2)}) copy-start(f32[512]{0:T(512)} %copy-done.31) | copy-start | bytes 6148
  351.3 31.0 %collective-permute-start.17 = (bf16[2,48,640]{2,1,0:T(8,128)(2,1)}, bf16[2,48,640]{2,1,0:T(8,128)(2,1)}, u32[]{:S(2)}, u32[]{:S(2)}) collective-permute-start(bf16[2,48,640]{2,1,0:T(8,128)(2,1)} %dynamic-slice_bitcast_fusion.9), channel_id=1, source_target_pairs={{0,16},{4,20},{8,24},{12,28},{16,0},{20,4},{24,8},{28,12},{1,17},{... | collective-permute-start | bytes 368648 | tf_op jit(solution)/shard_map/ppermute | solution.py:272
  355.5 4.7 %collective-permute-start.10 = (f32[6,768]{1,0:T(8,128)}, f32[6,768]{1,0:T(8,128)S(1)}, u32[]{:S(2)}, u32[]{:S(2)}) collective-permute-start(f32[6,768]{1,0:T(8,128)} %stack.36), channel_id=1, source_target_pairs={{0,1},{1,0},{2,3},{3,2},{4,5},{5,4},{6,7},{7,6},{8,9},{9,8},{10,11... | collective-permute-start | bytes 55304 | tf_op jit(solution)/shard_map/ppermute | solution.py:38
  366.7 3.8 collective-permute-start.11
  370.5 4.6 %copy-start.29 = (bf16[48,1536]{1,0:T(8,128)(2,1)S(1)}, bf16[48,1536]{1,0:T(8,128)(2,1)}, u32[]{:S(2)}) copy-start(bf16[48,1536]{1,0:T(8,128)(2,1)} %get-tuple-element.113) | copy-start | bytes 442372
  370.5 4.6 %collective-permute-start.12 = (f32[2,8,128]{2,1,0:T(8,128)S(1)}, f32[2,8,128]{2,1,0:T(8,128)S(1)}, u32[]{:S(2)}, u32[]{:S(2)}) collective-permute-start(f32[2,8,128]{2,1,0:T(8,128)S(1)} %fusion.81), channel_id=1, source_target_pairs={{0,16},{4,20},{8,24},{12,28},{16,0},{20,4},{24,8},{28,12},{1,17},{... | collective-permute-start | bytes 24584 | tf_op jit(solution)/shard_map/ppermute | solution.py:272
  375.1 3.6 collective-permute-start.13
  378.7 3.6 collective-permute-start.14
  383.3 4.3 %collective-permute-start.18 = (bf16[48,640]{1,0:T(8,128)(2,1)S(1)}, bf16[48,640]{1,0:T(8,128)(2,1)S(1)}, u32[]{:S(2)}, u32[]{:S(2)}) collective-permute-start(bf16[48,640]{1,0:T(8,128)(2,1)S(1)} %dynamic-slice_bitcast_fusion.11), channel_id=1, source_target_pairs={{0,8},{4,12},{8,0},{12,4},{16,24},{20,28},{24,16},{28,20},{1,9},{5... | collective-permute-start | bytes 184328 | tf_op jit(solution)/shard_map/ppermute | solution.py:272
  387.6 4.7 %collective-permute-start.19 = (bf16[48,640]{1,0:T(8,128)(2,1)S(1)}, bf16[48,640]{1,0:T(8,128)(2,1)S(1)}, u32[]{:S(2)}, u32[]{:S(2)}) collective-permute-start(bf16[48,640]{1,0:T(8,128)(2,1)S(1)} %fusion.76), channel_id=1, source_target_pairs={{0,2},{2,0},{1,3},{3,1},{4,6},{6,4},{5,7},{7,5},{8,10},{10,8},{9,1... | collective-permute-start | bytes 184328 | tf_op jit(solution)/shard_map/ppermute | solution.py:38
  391.1 5.6 %collective-permute-start.28 = (bf16[48,1920]{1,0:T(8,128)(2,1)S(1)}, bf16[48,1920]{1,0:T(8,128)(2,1)S(1)}, u32[]{:S(2)}, u32[]{:S(2)}) collective-permute-start(bf16[48,1920]{1,0:T(8,128)(2,1)S(1)} %dynamic-slice_bitcast_fusion.7), channel_id=1, source_target_pairs={{0,8},{4,12},{8,0},{12,4},{16,24},{20,28},{24,16},{28,20},{1,9},{5... | collective-permute-start | bytes 552968 | tf_op jit(solution)/shard_map/ppermute | solution.py:272
  396.8 5.6 %collective-permute-start.29 = (bf16[48,1920]{1,0:T(8,128)(2,1)S(1)}, bf16[48,1920]{1,0:T(8,128)(2,1)S(1)}, u32[]{:S(2)}, u32[]{:S(2)}) collective-permute-start(bf16[48,1920]{1,0:T(8,128)(2,1)S(1)} %fusion.71), channel_id=1, source_target_pairs={{0,2},{2,0},{1,3},{3,1},{4,6},{6,4},{5,7},{7,5},{8,10},{10,8},{9,1... | collective-permute-start | bytes 552968 | tf_op jit(solution)/shard_map/ppermute | solution.py:38
  (14 other events, 20.7 us)
Sparse Core Ops, SparseCore 0:
  14.9 49.7 all-gather.6
  74.7 86.1 all-gather.4

commit v3 on v2

--- a/solution.py
+++ b/solution.py
@@ -305,6 +305,23 @@
     return jnp.concatenate([low, high], axis=0).astype(F32)
 
 
+def gather(values, order):
+    rows, columns = values.shape
+    held = []
+    if "ctx" in order:
+        halves = values.reshape(2, rows // 2, columns)
+        values = lax.dynamic_index_in_dim(halves, own_bit("ctx"), 0, keepdims=False)
+    for bit in reversed(order):
+        rank = -1 if bit == "ctx" else bit
+        at = sum(1 for one in held if one > rank)
+        held.append(rank)
+        other = flip(values, bit)
+        first = own_bit(bit) == 0
+        low, high = jnp.where(first, values, other), jnp.where(first, other, values)
+        values = jnp.stack([low, high], axis=at)
+    return values.reshape(-1, rows, columns)
+
+
 def local(
     tokens,
     segment_order,
@@ -336,10 +353,15 @@
     smalls = [ln1_gain, ln1_bias, out_bias, ln2_gain, ln2_bias, down_bias]
     flat = jnp.concatenate([part.reshape(-1) for part in smalls + [qv_bias, up_bias]])
     flat = jnp.pad(flat, (0, qkv_width - flat.shape[0])).reshape(1, qkv_width)
+    flat = jnp.pad(flat, ((0, 15), (0, 0)))
+    order_a, order_b = halving_orders()
+    cut = -(-qkv_width // 256) * 128
     first = jnp.concatenate(
         [jnp.swapaxes(qkv_weight, 0, 1).reshape(depth, qkv_width), flat], axis=0
     )
-    first_all = lax.all_gather(first, "fsdp", axis=0, tiled=False)
+    first_all = jnp.concatenate(
+        [gather(first[:, :cut], order_a), gather(first[:, cut:], order_b)], axis=2
+    )
     qkv_full = first_all[:, :depth].reshape(model_width, qkv_width)
     small_all = first_all[:, depth].astype(F32)
     gain_one, shift_one, outb_full, gain_two, shift_two, downb_full = [
@@ -367,12 +389,11 @@
     queries = jnp.dot(flat_one, qkv_full[:, :inner_width], preferred_element_type=F32)
     queries = (queries + qv_full[0]).astype(BF16).reshape(seq_count, local_rows, inner_width)
 
-    second = jnp.concatenate([out_weight.T, up_weight, down_weight.T], axis=1)
-    kv, second = lax.optimization_barrier((kv, second))
-    second_all = lax.all_gather(second, "fsdp", axis=0, tiled=True)
-    out_t = second_all[:, :inner_width]
-    up_full = second_all[:, inner_width : inner_width + hidden]
-    down_t = second_all[:, inner_width + hidden :]
+    out_up = jnp.concatenate([up_weight, out_weight.T], axis=1)
+    normed_one, out_up, down_own = lax.optimization_barrier((normed_one, out_up, down_weight.T))
+    wide_all = gather(out_up, order_b).reshape(model_width, hidden + inner_width)
+    up_full, out_t = wide_all[:, :hidden], wide_all[:, hidden:]
+    down_t = gather(down_own, order_a).reshape(model_width, hidden)
 
     here, core = lax.axis_index("ctx"), lax.axis_index("tp")
     if contexts == 2:
@@ -417,7 +438,6 @@
     out_grad = dot(branch_flat, mixed_flat, ((0,), (0,))).astype(BF16)
     wide = jnp.concatenate([up_grad, out_grad], axis=1)
     wide, down_grad, mixed_grad = lax.optimization_barrier((wide, down_grad, mixed_grad))
-    order_a, order_b = halving_orders()
     down_total = scatter_sum(down_grad.reshape(shards, depth, hidden), order_a)
     wide_total = scatter_sum(wide.reshape(shards, depth, hidden + inner_width), order_b)
 
@@ -441,7 +461,6 @@
     stacked = stacked.reshape(-1, qkv_width)
     norm_one_grad = pair_sum(dot(stacked, qkv_full, ((1,), (1,))), half_rows)
     qkv_grad = dot(flat_one, stacked, ((0,), (0,))).astype(BF16)
-    cut = -(-qkv_width // 256) * 128
     qkv_grad = qkv_grad.reshape(shards, depth, qkv_width)
     qkv_total = jnp.concatenate(
         [

time: 418 us -> 417 us (level)
  starting transfers between devices: 16 us -> 71.7 us
  Pallas kernels: 69.8 us -> 44.6 us
  between operations: 15.3 us -> 2.27 us
  matrix products: 50.8 us -> 38.4 us
  local copies, waits for them, and re-layouts: 48.1 us -> 42.4 us
    ppermute x15 -> x27, waiting for transfers between devices: 35.7 us -> 105 us  [flip(): lax.ppermute(values, 'fsdp', [(i, i ^ 1 << bit) for i in range(count)])]
    all_gather x2 -> x0, waiting for transfers between devices: 63.2 us -> none  [the longest x1 48.1 us: local(): first_all = lax.all_gather(first, 'fsdp', axis=0, tiled=False)]
    ppermute x15 -> x27, starting transfers between devices: 3.91 us -> 44.8 us  [flip(): lax.ppermute(values, 'fsdp', [(i, i ^ 1 << bit) for i in range(count)])]
    ppermute x20 -> x24, starting transfers between devices: 12 us -> 26.9 us  [swap(): return lax.ppermute(values, axis, [(0, 1), (1, 0)])]
    pallas_call x1, Pallas kernels: 38.4 us -> 24.8 us  [attend_back(): pl.pallas_call(partial(backward_kernel, total_len // block), grid_spec=pl...]
    pallas_call x1, Pallas kernels: 31.4 us -> 19.8 us  [attend(): pl.pallas_call(partial(forward_kernel, total_len // block), grid_spec=plt...]
    dot_general x8, matrix products: 28.1 us -> 22.9 us  [dot(): lax.dot_general(left, right, (dims, ((), ())), preferred_element_type=F32)]
    another operation x0 -> x32, other arithmetic: none -> 4.58 us  [gather(): values = jnp.stack([low, high], axis=at)]
  transfers between devices with their start and end apart: 37 -> 51, of which waited for: 20 -> 25; matrix products, arithmetic and copies ran while one was open for 22% -> 19% of each run, Pallas kernels for 17% -> 11%
where the time goes in v3:
time: 417 us; the launch traced here: 410 us
  waiting for transfers between devices  172 us (41%)
  starting transfers between devices  71.7 us (17%)
  Pallas kernels  44.6 us (11%)
  local copies, waits for them, and re-layouts  42.4 us (10%)
  other arithmetic  39 us (9%)
  matrix products  38.4 us (9%)
    ppermute x27, waiting for transfers between devices, flip(): lax.ppermute(values, 'fsdp', [(i, i ^ 1 << bit) for i in range(count)])  105 us
    ppermute x24, waiting for transfers between devices, swap(): return lax.ppermute(values, axis, [(0, 1), (1, 0)])  67.2 us
    ppermute x27, starting transfers between devices, flip(): lax.ppermute(values, 'fsdp', [(i, i ^ 1 << bit) for i in range(count)])  44.8 us
    ppermute x24, starting transfers between devices, swap(): return lax.ppermute(values, axis, [(0, 1), (1, 0)])  26.9 us
    pallas_call x1, Pallas kernels, attend_back(): pl.pallas_call(partial(backward_kernel, total_len // block), grid_spec=pl...  24.8 us
    dot_general x8, matrix products, dot(): lax.dot_general(left, right, (dims, ((), ())), preferred_element_type=F32)  22.9 us
    pallas_call x1, Pallas kernels, attend(): pl.pallas_call(partial(forward_kernel, total_len // block), grid_spec=plt...  19.8 us
    unnamed x101, local copies, waits for them, and re-layouts  9.92 us
  transfers between devices with their start and end apart: 51, of which 25 were waited for; matrix products, arithmetic and copies ran while one was open for 19% of the time, Pallas kernels for 11%

profile of v3, /device:TPU:0, one launch (start us, length us, event | category | flops | bytes accessed | tf_op | source)
XLA Modules:
  0.0 410.4 jit_solution(4098874882774341685)
XLA Ops:
  2.4 4.1 concatenate.64
  7.6 3.1 collective-permute-start.4
  13.4 2.7 pad_add_fusion.1.k_segs
  16.1 2.0 collective-permute-start.5
  18.1 2.7 collective-permute-start.1
  21.1 3.0 collective-permute-start.6
  24.1 8.9 %collective-permute-done.1 = bf16[2,56,640]{2,1,0:T(8,128)(2,1)S(1)} collective-permute-done((bf16[2,56,640]{2,1,0:T(8,128)(2,1)S(1)}, bf16[2,56,640]{2,1,0:T(8,128)(2,1)S(1)}, u32[]{:S(2)}, u32[]{:S(2)}) %collective-permute-start.1) | collective-permute-done | bytes 143392 | tf_op jit(solution)/shard_map/ppermute | solution.py:272
  33.0 1.6 collective-permute-start.2
  34.6 2.1 collective-permute-done.6
  36.8 1.6 collective-permute-start.7
  38.3 2.7 collective-permute-done.2
  42.4 7.1 %collective-permute-done.7 = bf16[2,2,2,56,512]{4,3,2,1,0:T(8,128)(2,1)S(1)} collective-permute-done((bf16[2,2,2,56,512]{4,3,2,1,0:T(8,128)(2,1)S(1)}, bf16[2,2,2,56,512]{4,3,2,1,0:T(8,128)(2,1)S(1)}, u32[]{:S(2)}, u32[]{:S(2)}) %collective-permute-start.7) | collective-permute-done | bytes 458784 | tf_op jit(solution)/shard_map/ppermute | solution.py:272
  49.7 2.4 collective-permute-done.3
  61.2 2.2 collective-permute-start.16
  63.6 8.1 %collective-permute-done.10 = bf16[48,1920]{1,0:T(8,128)(2,1)S(1)} collective-permute-done((bf16[48,1920]{1,0:T(8,128)(2,1)S(1)}, bf16[48,1920]{1,0:T(8,128)(2,1)S(1)}, u32[]{:S(2)}, u32[]{:S(2)}) %collective-permute-start.10) | collective-permute-done | bytes 184352 | tf_op jit(solution)/shard_map/ppermute | solution.py:272
  72.5 3.4 collective-permute-start.17
  76.0 6.4 %collective-permute-done.11 = bf16[2,48,1920]{2,1,0:T(8,128)(2,1)S(1)} collective-permute-done((bf16[2,48,1920]{2,1,0:T(8,128)(2,1)S(1)}, bf16[2,48,1920]{2,1,0:T(8,128)(2,1)S(1)}, u32[]{:S(2)}, u32[]{:S(2)}) %collective-permute-start.11) | collective-permute-done | bytes 368672 | tf_op jit(solution)/shard_map/ppermute | solution.py:38
  82.5 3.4 collective-permute-start.12
  88.0 18.0 %collective-permute-done.17 = bf16[2,48,1536]{2,1,0:T(8,128)(2,1)S(1)} collective-permute-done((bf16[2,48,1536]{2,1,0:T(8,128)(2,1)S(1)}, bf16[2,48,1536]{2,1,0:T(8,128)(2,1)S(1)}, u32[]{:S(2)}, u32[]{:S(2)}) %collective-permute-start.17) | collective-permute-done | bytes 294944 | tf_op jit(solution)/shard_map/ppermute | solution.py:272
  109.4 11.3 %collective-permute-done.12 = bf16[2,2,48,1920]{3,2,1,0:T(8,128)(2,1)S(1)} collective-permute-done((bf16[2,2,48,1920]{3,2,1,0:T(8,128)(2,1)S(1)}, bf16[2,2,48,1920]{3,2,1,0:T(8,128)(2,1)S(1)}, u32[]{:S(2)}, u32[]{:S(2)}) %collective-permute-start.12) | collective-permute-done | bytes 737312 | tf_op jit(solution)/shard_map/ppermute | solution.py:272
  122.8 19.8 %shard_map.254 = (bf16[1,1024,384]{2,1,0:T(8,128)(2,1)S(1)}, f32[1,3,8,1024]{3,2,1,0:T(8,128)S(1)}) custom-call(s32[1,2]{1,0:T(1,128)S(1)} %pad_add_fusion.q_segs, s32[1,4]{1,0:T(1,128)S(1)} %pad_add_fusion.1.k_segs, bf16[1,1024,384]{2,1,0:T(8,128)(2,1)S(1)} %fusion.44.q_ref, bf16[1,2048,768]{2,1,0:T(8,128)(2,1)S(1)} %pad_maximum_fusion.k_ref.v_ref, ...), custom_call_target="tpu_custom_call" | custom-call | flops 12884901888 | bytes 6291456 | tf_op jit(solution)/shard_map/pallas_call | solution.py:169
  142.6 11.7 %collective-permute-done.13 = bf16[2,2,2,48,1920]{4,3,2,1,0:T(8,128)(2,1)S(1)} collective-permute-done((bf16[2,2,2,48,1920]{4,3,2,1,0:T(8,128)(2,1)S(1)}, bf16[2,2,2,48,1920]{4,3,2,1,0:T(8,128)(2,1)S(1)}, u32[]{:S(2)}, u32[]{:S(2)}) %collective-permute-start.13) | collective-permute-done | bytes 1474592 | tf_op jit(solution)/shard_map/ppermute | solution.py:272
  159.8 1.6 collective-permute-start.19
  161.4 1.6 fusion.87
  163.7 24.1 %collective-permute-done.19 = bf16[2,2,2,48,1536]{4,3,2,1,0:T(8,128)(2,1)S(1)} collective-permute-done((bf16[2,2,2,48,1536]{4,3,2,1,0:T(8,128)(2,1)S(1)}, bf16[2,2,2,48,1536]{4,3,2,1,0:T(8,128)(2,1)S(1)}, u32[]{:S(2)}, u32[]{:S(2)}) %collective-permute-start.19) | collective-permute-done | bytes 1179680 | tf_op jit(solution)/shard_map/ppermute | solution.py:38
  188.1 1.6 copy-done.21
  189.7 2.6 fusion.11
  192.3 8.5 %convert_reduce_fusion = (f32[1536]{0:T(1024)S(1)}, bf16[1024,1536]{1,0:T(8,128)(2,1)S(1)}) fusion(f32[1024,1536]{1,0:T(8,128)S(1)} %fusion.11, f32[1536]{0:T(1024)S(1)} %add.348, bf16[768,1536]{1,0:T(8,128)(2,1)S(1)} %bitcast.311, bf16[1,512,768]{2,1,0:T(8,128)(2,1)} %collective-permute-done.21, bf16[1,512,768]{2,1,0:T(8,128)(2,1)} %param.29), kind=kOutput, calls=%fused_computation.9 | convolution fusion | flops 2455239168 | bytes 13381632 | tf_op jit(solution)/shard_map/dot_general | solution.py:428
  200.8 2.6 fusion.36
  204.4 4.0 fusion.35
  209.9 3.9 convolution_convert_fusion.1
  214.6 2.2 multiply_reduce_fusion
  216.8 3.5 fusion.86
  221.7 4.5 %convolution_convert_fusion = bf16[768,1536]{1,0:T(8,128)(2,1)S(1)} fusion(bf16[1,512,768]{2,1,0:T(8,128)(2,1)} %collective-permute-done.21, bf16[1,512,768]{2,1,0:T(8,128)(2,1)} %param.29, f32[1024,1536]{1,0:T(8,128)S(1)} %bitcast.343, f32[1536]{0:T(1024)S(1)} %add.348), kind=kOutput, calls=%fused_computation.12 | convolution fusion | flops 2435973120 | bytes 10229760 | tf_op jit(solution)/shard_map/dot_general | solution.py:42
  230.4 2.0 convolution_convert_fusion.6
  234.6 1.6 collective-permute-start.46
  236.2 24.8 %shard_map.255 = (bf16[1,1024,384]{2,1,0:T(8,128)(2,1)S(1)}, bf16[1,2,2048,384]{3,2,1,0:T(8,128)(2,1)}) custom-call(s32[1,2]{1,0:T(1,128)S(1)} %pad_add_fusion.q_segs, s32[1,4]{1,0:T(1,128)S(1)} %pad_add_fusion.1.k_segs, bf16[1,1024,384]{2,1,0:T(8,128)(2,1)S(1)} %copy-done.4, bf16[1,1024,384]{2,1,0:T(8,128)(2,1)S(1)} %bitcast.297, ...), custom_call_target="tpu_custom_call" | custom-call | flops 32212254720 | bytes 12582912 | tf_op jit(solution)/shard_map/pallas_call | solution.py:207
  261.0 1.6 slice.182
  262.6 10.3 %collective-permute-start.24 = (bf16[1,2,1024,384]{3,2,1,0:T(8,128)(2,1)S(1)}, bf16[1,2,1024,384]{3,2,1,0:T(8,128)(2,1)S(1)}, u32[]{:S(2)}, u32[]{:S(2)}) collective-permute-start(bf16[1,2,1024,384]{3,2,1,0:T(8,128)(2,1)S(1)} %slice.182), channel_id=1, source_target_pairs={{0,2},{2,0},{1,3},{3,1},{4,6},{6,4},{5,7},{7,5},{8,10},{10,8},{9,1... | collective-permute-start | bytes 4718600 | tf_op jit(solution)/shard_map/ppermute | solution.py:38
  274.1 5.2 %collective-permute-start.47 = (bf16[2,2,48,1536]{3,2,1,0:T(8,128)(2,1)}, bf16[2,2,48,1536]{3,2,1,0:T(8,128)(2,1)}, u32[]{:S(2)}, u32[]{:S(2)}) collective-permute-start(bf16[2,2,48,1536]{3,2,1,0:T(8,128)(2,1)} %dynamic-slice_bitcast_fusion.1), channel_id=1, source_target_pairs={{0,4},{4,0},{8,12},{12,8},{16,20},{20,16},{24,28},{28,24},{1,5},{5... | collective-permute-start | bytes 1769480 | tf_op jit(solution)/shard_map/ppermute | solution.py:272
  280.5 27.1 %collective-permute-done.24 = bf16[1,2,1024,384]{3,2,1,0:T(8,128)(2,1)S(1)} collective-permute-done((bf16[1,2,1024,384]{3,2,1,0:T(8,128)(2,1)S(1)}, bf16[1,2,1024,384]{3,2,1,0:T(8,128)(2,1)S(1)}, u32[]{:S(2)}, u32[]{:S(2)}) %collective-permute-start.24) | collective-permute-done | bytes 1572896 | tf_op jit(solution)/shard_map/ppermute | solution.py:38
  310.1 2.3 convolution_convert_fusion.2
  316.1 5.2 %collective-permute-start.36 = (bf16[2,2,2,48,512]{4,3,1,2,0:T(8,128)(2,1)S(1)}, bf16[2,2,2,48,512]{4,3,1,2,0:T(8,128)(2,1)S(1)}, u32[]{:S(2)}, u32[]{:S(2)}) collective-permute-start(bf16[2,2,2,48,512]{4,3,1,2,0:T(8,128)(2,1)S(1)} %bitcast.328), channel_id=1, source_target_pairs={{0,4},{4,0},{8,12},{12,8},{16,20},{20,16},{24,28},{28,24},{1,5},{5... | collective-permute-start | bytes 1179656 | tf_op jit(solution)/shard_map/ppermute | solution.py:272
  321.4 1.8 collective-permute-start.31
  323.2 3.7 fusion.32
  327.1 1.6 fusion.48
  328.8 1.6 collective-permute-done.36
  331.9 18.2 %collective-permute-done.48 = bf16[2,48,1536]{2,1,0:T(8,128)(2,1)S(1)} collective-permute-done((bf16[2,48,1536]{2,1,0:T(8,128)(2,1)S(1)}, bf16[2,48,1536]{2,1,0:T(8,128)(2,1)S(1)}, u32[]{:S(2)}, u32[]{:S(2)}) %collective-permute-start.48) | collective-permute-done | bytes 294944 | tf_op jit(solution)/shard_map/ppermute | solution.py:272
  350.6 3.0 collective-permute-done.37
  354.0 2.6 collective-permute-done.49
  359.3 1.7 collective-permute-start.43
  361.0 1.6 collective-permute-done.39
  363.2 1.7 collective-permute-start.40
  370.4 1.8 convert_bitcast_fusion
  374.7 3.0 collective-permute-done.27
  377.8 2.9 collective-permute-start.28
  382.3 1.7 collective-permute-start.29
  384.1 2.7 fusion.28
  387.9 2.5 collective-permute-done.30
  394.3 1.6 collective-permute-done.34
  398.5 2.0 collective-permute-done.35
  400.6 2.4 collective-permute-done.44
  403.0 2.1 collective-permute-start.45
  406.1 2.5 collective-permute-done.45
  (330 shorter events, 76.8 us)
Async XLA Ops:
  0.6 10.2 %copy-start.5 = (bf16[1,512,768]{2,1,0:T(8,128)(2,1)S(1)}, bf16[1,512,768]{2,1,0:T(8,128)(2,1)}, u32[]{:S(2)}) copy-start(bf16[1,512,768]{2,1,0:T(8,128)(2,1)} %param.15) | copy-start | bytes 2359300
  7.6 8.5 %collective-permute-start.4 = (bf16[56,512]{1,0:T(8,128)(2,1)S(1)}, bf16[56,512]{1,0:T(8,128)(2,1)S(1)}, u32[]{:S(2)}, u32[]{:S(2)}) collective-permute-start(bf16[56,512]{1,0:T(8,128)(2,1)S(1)} %dynamic-slice_bitcast_fusion.15), channel_id=1, source_target_pairs={{0,8},{4,12},{8,0},{12,4},{16,24},{20,28},{24,16},{28,20},{1,9},{5... | collective-permute-start | bytes 172040 | tf_op jit(solution)/shard_map/ppermute | solution.py:272
  10.7 7.4 %collective-permute-start = (bf16[56,640]{1,0:T(8,128)(2,1)S(1)}, bf16[56,640]{1,0:T(8,128)(2,1)S(1)}, u32[]{:S(2)}, u32[]{:S(2)}) collective-permute-start(bf16[56,640]{1,0:T(8,128)(2,1)S(1)} %dynamic-slice_bitcast_fusion.13), channel_id=1, source_target_pairs={{0,8},{4,12},{8,0},{12,4},{16,24},{20,28},{24,16},{28,20},{1,9},{5... | collective-permute-start | bytes 215048 | tf_op jit(solution)/shard_map/ppermute | solution.py:272
  16.1 4.9 %collective-permute-start.5 = (bf16[2,56,512]{2,1,0:T(8,128)(2,1)S(1)}, bf16[2,56,512]{2,1,0:T(8,128)(2,1)S(1)}, u32[]{:S(2)}, u32[]{:S(2)}) collective-permute-start(bf16[2,56,512]{2,1,0:T(8,128)(2,1)S(1)} %pad_maximum_fusion.20), channel_id=1, source_target_pairs={{0,2},{2,0},{1,3},{3,1},{4,6},{6,4},{5,7},{7,5},{8,10},{10,8},{9,1... | collective-permute-start | bytes 344072 | tf_op jit(solution)/shard_map/ppermute | solution.py:38
  18.1 14.8 %collective-permute-start.1 = (bf16[2,56,640]{2,1,0:T(8,128)(2,1)S(1)}, bf16[2,56,640]{2,1,0:T(8,128)(2,1)S(1)}, u32[]{:S(2)}, u32[]{:S(2)}) collective-permute-start(bf16[2,56,640]{2,1,0:T(8,128)(2,1)S(1)} %pad_maximum_fusion.19), channel_id=1, source_target_pairs={{0,16},{4,20},{8,24},{12,28},{16,0},{20,4},{24,8},{28,12},{1,17},{... | collective-permute-start | bytes 430088 | tf_op jit(solution)/shard_map/ppermute | solution.py:272
  21.1 15.6 %collective-permute-start.6 = (bf16[2,2,56,512]{3,2,1,0:T(8,128)(2,1)S(1)}, bf16[2,2,56,512]{3,2,1,0:T(8,128)(2,1)S(1)}, u32[]{:S(2)}, u32[]{:S(2)}) collective-permute-start(bf16[2,2,56,512]{3,2,1,0:T(8,128)(2,1)S(1)} %pad_maximum_fusion.18), channel_id=1, source_target_pairs={{0,16},{4,20},{8,24},{12,28},{16,0},{20,4},{24,8},{28,12},{1,17},{... | collective-permute-start | bytes 688136 | tf_op jit(solution)/shard_map/ppermute | solution.py:272
  33.0 8.0 %collective-permute-start.2 = (bf16[2,2,56,640]{3,2,1,0:T(8,128)(2,1)S(1)}, bf16[2,2,56,640]{3,2,1,0:T(8,128)(2,1)S(1)}, u32[]{:S(2)}, u32[]{:S(2)}) collective-permute-start(bf16[2,2,56,640]{3,2,1,0:T(8,128)(2,1)S(1)} %pad_maximum_fusion.17), channel_id=1, source_target_pairs={{0,4},{4,0},{8,12},{12,8},{16,20},{20,16},{24,28},{28,24},{1,5},{5... | collective-permute-start | bytes 860168 | tf_op jit(solution)/shard_map/ppermute | solution.py:272
  36.8 12.8 %collective-permute-start.7 = (bf16[2,2,2,56,512]{4,3,2,1,0:T(8,128)(2,1)S(1)}, bf16[2,2,2,56,512]{4,3,2,1,0:T(8,128)(2,1)S(1)}, u32[]{:S(2)}, u32[]{:S(2)}) collective-permute-start(bf16[2,2,2,56,512]{4,3,2,1,0:T(8,128)(2,1)S(1)} %pad_maximum_fusion.12), channel_id=1, source_target_pairs={{0,4},{4,0},{8,12},{12,8},{16,20},{20,16},{24,28},{28,24},{1,5},{5... | collective-permute-start | bytes 1376264 | tf_op jit(solution)/shard_map/ppermute | solution.py:272
  41.2 10.9 %collective-permute-start.3 = (bf16[2,2,2,56,640]{4,3,2,1,0:T(8,128)(2,1)S(1)}, bf16[2,2,2,56,640]{4,3,2,1,0:T(8,128)(2,1)S(1)}, u32[]{:S(2)}, u32[]{:S(2)}) collective-permute-start(bf16[2,2,2,56,640]{4,3,2,1,0:T(8,128)(2,1)S(1)} %pad_maximum_fusion.11), channel_id=1, source_target_pairs={{0,2},{2,0},{1,3},{3,1},{4,6},{6,4},{5,7},{7,5},{8,10},{10,8},{9,1... | collective-permute-start | bytes 1720328 | tf_op jit(solution)/shard_map/ppermute | solution.py:38
  52.4 8.8 %copy-start.28 = (bf16[1536,96]{0,1:T(8,128)(2,1)S(1)}, bf16[1536,96]{0,1:T(8,128)(2,1)}, u32[]{:S(2)}) copy-start(bf16[1536,96]{0,1:T(8,128)(2,1)} %param.27) | copy-start | bytes 884740
  61.0 47.3 %copy-start.26 = (bf16[1,512,768]{2,1,0:T(8,128)(2,1)}, bf16[1,512,768]{2,1,0:T(8,128)(2,1)S(1)}, u32[]{:S(2)}) copy-start(bf16[1,512,768]{2,1,0:T(8,128)(2,1)S(1)} %fusion.23) | copy-start | bytes 2359300
  61.0 24.9 %collective-permute-start.8 = (bf16[1,512,768]{2,1,0:T(8,128)(2,1)S(1)}, bf16[1,512,768]{2,1,0:T(8,128)(2,1)S(1)}, u32[]{:S(2)}, u32[]{:S(2)}) collective-permute-start(bf16[1,512,768]{2,1,0:T(8,128)(2,1)S(1)} %fusion.23), channel_id=1, source_target_pairs={{0,1},{1,0},{2,3},{3,2},{4,5},{5,4},{6,7},{7,6},{8,9},{9,8},{10,11... | collective-permute-start | bytes 2359304 | tf_op jit(solution)/shard_map/ppermute | solution.py:38
  61.2 11.3 %collective-permute-start.16 = (bf16[48,1536]{1,0:T(8,128)(2,1)S(1)}, bf16[48,1536]{1,0:T(8,128)(2,1)S(1)}, u32[]{:S(2)}, u32[]{:S(2)}) collective-permute-start(bf16[48,1536]{1,0:T(8,128)(2,1)S(1)} %dynamic-slice_bitcast_fusion.10), channel_id=1, source_target_pairs={{0,8},{4,12},{8,0},{12,4},{16,24},{20,28},{24,16},{28,20},{1,9},{5... | collective-permute-start | bytes 442376 | tf_op jit(solution)/shard_map/ppermute | solution.py:272
  63.4 8.4 %collective-permute-start.10 = (bf16[48,1920]{1,0:T(8,128)(2,1)S(1)}, bf16[48,1920]{1,0:T(8,128)(2,1)S(1)}, u32[]{:S(2)}, u32[]{:S(2)}) collective-permute-start(bf16[48,1920]{1,0:T(8,128)(2,1)S(1)} %dynamic-slice_bitcast_fusion.8), channel_id=1, source_target_pairs={{0,8},{4,12},{8,0},{12,4},{16,24},{20,28},{24,16},{28,20},{1,9},{5... | collective-permute-start | bytes 552968 | tf_op jit(solution)/shard_map/ppermute | solution.py:272
  63.6 44.7 %copy-start.23 = (bf16[8,96,1152]{2,1,0:T(8,128)(2,1)}, bf16[8,96,1152]{2,1,0:T(8,128)(2,1)S(1)}, u32[]{:S(2)}) copy-start(bf16[8,96,1152]{2,1,0:T(8,128)(2,1)S(1)} %pad_maximum_fusion.4) | copy-start | bytes 5308420
  71.9 10.5 %collective-permute-start.11 = (bf16[2,48,1920]{2,1,0:T(8,128)(2,1)S(1)}, bf16[2,48,1920]{2,1,0:T(8,128)(2,1)S(1)}, u32[]{:S(2)}, u32[]{:S(2)}) collective-permute-start(bf16[2,48,1920]{2,1,0:T(8,128)(2,1)S(1)} %pad_maximum_fusion.14), channel_id=1, source_target_pairs={{0,2},{2,0},{1,3},{3,1},{4,6},{6,4},{5,7},{7,5},{8,10},{10,8},{9,1... | collective-permute-start | bytes 1105928 | tf_op jit(solution)/shard_map/ppermute | solution.py:38
  72.5 33.4 %collective-permute-start.17 = (bf16[2,48,1536]{2,1,0:T(8,128)(2,1)S(1)}, bf16[2,48,1536]{2,1,0:T(8,128)(2,1)S(1)}, u32[]{:S(2)}, u32[]{:S(2)}) collective-permute-start(bf16[2,48,1536]{2,1,0:T(8,128)(2,1)S(1)} %pad_maximum_fusion.16), channel_id=1, source_target_pairs={{0,16},{4,20},{8,24},{12,28},{16,0},{20,4},{24,8},{28,12},{1,17},{... | collective-permute-start | bytes 884744 | tf_op jit(solution)/shard_map/ppermute | solution.py:272
  82.5 38.2 %collective-permute-start.12 = (bf16[2,2,48,1920]{3,2,1,0:T(8,128)(2,1)S(1)}, bf16[2,2,48,1920]{3,2,1,0:T(8,128)(2,1)S(1)}, u32[]{:S(2)}, u32[]{:S(2)}) collective-permute-start(bf16[2,2,48,1920]{3,2,1,0:T(8,128)(2,1)S(1)} %pad_maximum_fusion.9), channel_id=1, source_target_pairs={{0,16},{4,20},{8,24},{12,28},{16,0},{20,4},{24,8},{28,12},{1,17},{... | collective-permute-start | bytes 2211848 | tf_op jit(solution)/shard_map/ppermute | solution.py:272
  86.0 22.4 %copy-start.42 = (bf16[1,512,768]{2,1,0:T(8,128)(2,1)}, bf16[1,512,768]{2,1,0:T(8,128)(2,1)S(1)}, u32[]{:S(2)}) copy-start(bf16[1,512,768]{2,1,0:T(8,128)(2,1)S(1)} %collective-permute-done.8) | copy-start | bytes 2359300
  87.4 35.2 %collective-permute-start.9 = (bf16[1,1024,768]{2,1,0:T(8,128)(2,1)S(1)}, bf16[1,1024,768]{2,1,0:T(8,128)(2,1)S(1)}, u32[]{:S(2)}, u32[]{:S(2)}) collective-permute-start(bf16[1,1024,768]{2,1,0:T(8,128)(2,1)S(1)} %fusion.34), channel_id=1, source_target_pairs={{0,2},{2,0},{1,3},{3,1},{4,6},{6,4},{5,7},{7,5},{8,10},{10,8},{9,1... | collective-permute-start | bytes 4718600 | tf_op jit(solution)/shard_map/ppermute | solution.py:38
  106.9 51.6 %collective-permute-start.18 = (bf16[2,2,48,1536]{3,2,1,0:T(8,128)(2,1)}, bf16[2,2,48,1536]{3,2,1,0:T(8,128)(2,1)}, u32[]{:S(2)}, u32[]{:S(2)}) collective-permute-start(bf16[2,2,48,1536]{3,2,1,0:T(8,128)(2,1)} %pad_maximum_fusion.10), channel_id=1, source_target_pairs={{0,4},{4,0},{8,12},{12,8},{16,20},{20,16},{24,28},{28,24},{1,5},{5... | collective-permute-start | bytes 1769480 | tf_op jit(solution)/shard_map/ppermute | solution.py:272
  109.4 13.4 %copy-start.3 = (bf16[1,1024,384]{2,1,0:T(8,128)(2,1)}, bf16[1,1024,384]{2,1,0:T(8,128)(2,1)S(1)}, u32[]{:S(2)}) copy-start(bf16[1,1024,384]{2,1,0:T(8,128)(2,1)S(1)} %fusion.44.q_ref) | copy-start | bytes 2359300
  121.0 33.3 %collective-permute-start.13 = (bf16[2,2,2,48,1920]{4,3,2,1,0:T(8,128)(2,1)S(1)}, bf16[2,2,2,48,1920]{4,3,2,1,0:T(8,128)(2,1)S(1)}, u32[]{:S(2)}, u32[]{:S(2)}) collective-permute-start(bf16[2,2,2,48,1920]{4,3,2,1,0:T(8,128)(2,1)S(1)} %pad_maximum_fusion.5), channel_id=1, source_target_pairs={{0,4},{4,0},{8,12},{12,8},{16,20},{20,16},{24,28},{28,24},{1,5},{5... | collective-permute-start | bytes 4423688 | tf_op jit(solution)/shard_map/ppermute | solution.py:272
  122.8 19.8 %copy-start = (bf16[1,2048,768]{2,1,0:T(8,128)(2,1)}, bf16[1,2048,768]{2,1,0:T(8,128)(2,1)S(1)}, u32[]{:S(2)}) copy-start(bf16[1,2048,768]{2,1,0:T(8,128)(2,1)S(1)} %pad_maximum_fusion.k_ref.v_ref) | copy-start | bytes 9437188
  142.6 12.4 %copy-start.1 = (bf16[1,1024,384]{2,1,0:T(8,128)(2,1)}, bf16[1,1024,384]{2,1,0:T(8,128)(2,1)S(1)}, u32[]{:S(2)}) copy-start(bf16[1,1024,384]{2,1,0:T(8,128)(2,1)S(1)} %get-tuple-element.23.o_ref) | copy-start | bytes 2359300
  156.6 4.7 %collective-permute-start.14 = (bf16[1,512,768]{2,1,0:T(8,128)(2,1)S(1)}, bf16[1,512,768]{2,1,0:T(8,128)(2,1)}, u32[]{:S(2)}, u32[]{:S(2)}) collective-permute-start(bf16[1,512,768]{2,1,0:T(8,128)(2,1)S(1)} %slice.213), channel_id=1, source_target_pairs={{0,1},{1,0},{2,3},{3,2},{4,5},{5,4},{6,7},{7,6},{8,9},{9,8},{10,11... | collective-permute-start | bytes 2359304 | tf_op jit(solution)/shard_map/ppermute | solution.py:38
  156.7 35.7 %collective-permute-start.21 = (bf16[1,512,768]{2,1,0:T(8,128)(2,1)}, bf16[1,512,768]{2,1,0:T(8,128)(2,1)}, u32[]{:S(2)}, u32[]{:S(2)}) collective-permute-start(bf16[1,512,768]{2,1,0:T(8,128)(2,1)} %param.29), channel_id=1, source_target_pairs={{0,1},{1,0},{2,3},{3,2},{4,5},{5,4},{6,7},{7,6},{8,9},{9,8},{10,11... | collective-permute-start | bytes 2359304 | tf_op jit(solution)/shard_map/ppermute | solution.py:38
  159.8 27.9 %collective-permute-start.19 = (bf16[2,2,2,48,1536]{4,3,2,1,0:T(8,128)(2,1)S(1)}, bf16[2,2,2,48,1536]{4,3,2,1,0:T(8,128)(2,1)S(1)}, u32[]{:S(2)}, u32[]{:S(2)}) collective-permute-start(bf16[2,2,2,48,1536]{4,3,2,1,0:T(8,128)(2,1)S(1)} %pad_maximum_fusion.6), channel_id=1, source_target_pairs={{0,2},{2,0},{1,3},{3,1},{4,6},{6,4},{5,7},{7,5},{8,10},{10,8},{9,1... | collective-permute-start | bytes 3538952 | tf_op jit(solution)/shard_map/ppermute | solution.py:38
  163.6 24.5 %collective-permute-start.15 = (bf16[1,512,768]{2,1,0:T(8,128)(2,1)S(1)}, bf16[1,512,768]{2,1,0:T(8,128)(2,1)S(1)}, u32[]{:S(2)}, u32[]{:S(2)}) collective-permute-start(bf16[1,512,768]{2,1,0:T(8,128)(2,1)S(1)} %add_convert_fusion.3), channel_id=1, source_target_pairs={{0,1},{1,0},{2,3},{3,2},{4,5},{5,4},{6,7},{7,6},{8,9},{9,8},{10,11... | collective-permute-start | bytes 2359304 | tf_op jit(solution)/shard_map/ppermute | solution.py:38
  192.3 12.1 %copy-start.44 = (f32[1024,1536]{1,0:T(8,128)}, f32[1024,1536]{1,0:T(8,128)S(1)}, u32[]{:S(2)}) copy-start(f32[1024,1536]{1,0:T(8,128)S(1)} %fusion.11) | copy-start | bytes 18874372
  204.4 10.3 %collective-permute-start.22 = (bf16[1,512,768]{2,1,0:T(8,128)(2,1)}, bf16[1,512,768]{2,1,0:T(8,128)(2,1)}, u32[]{:S(2)}, u32[]{:S(2)}) collective-permute-start(bf16[1,512,768]{2,1,0:T(8,128)(2,1)} %slice.223), channel_id=1, source_target_pairs={{0,1},{1,0},{2,3},{3,2},{4,5},{5,4},{6,7},{7,6},{8,9},{9,8},{10,11... | collective-permute-start | bytes 2359304 | tf_op jit(solution)/shard_map/ppermute | solution.py:38
  209.4 7.4 %collective-permute-start.20 = (bf16[1,512,768]{2,1,0:T(8,128)(2,1)}, bf16[1,512,768]{2,1,0:T(8,128)(2,1)}, u32[]{:S(2)}, u32[]{:S(2)}) collective-permute-start(bf16[1,512,768]{2,1,0:T(8,128)(2,1)} %slice.220), channel_id=1, source_target_pairs={{0,1},{1,0},{2,3},{3,2},{4,5},{5,4},{6,7},{7,6},{8,9},{9,8},{10,11... | collective-permute-start | bytes 2359304 | tf_op jit(solution)/shard_map/ppermute | solution.py:38
  221.6 6.9 %collective-permute-start.23 = (bf16[1,512,768]{2,1,0:T(8,128)(2,1)S(1)}, bf16[1,512,768]{2,1,0:T(8,128)(2,1)S(1)}, u32[]{:S(2)}, u32[]{:S(2)}) collective-permute-start(bf16[1,512,768]{2,1,0:T(8,128)(2,1)S(1)} %convert_element_type.323), channel_id=1, source_target_pairs={{0,1},{1,0},{2,3},{3,2},{4,5},{5,4},{6,7},{7,6},{8,9},{9,8},{10,11... | collective-permute-start | bytes 2359304 | tf_op jit(solution)/shard_map/ppermute | solution.py:38
  232.8 46.4 %collective-permute-start.41 = (bf16[2,2,2,48,1920]{4,3,1,2,0:T(8,128)(2,1)S(1)}, bf16[2,2,2,48,1920]{4,3,1,2,0:T(8,128)(2,1)S(1)}, u32[]{:S(2)}, u32[]{:S(2)}) collective-permute-start(bf16[2,2,2,48,1920]{4,3,1,2,0:T(8,128)(2,1)S(1)} %bitcast.319), channel_id=1, source_target_pairs={{0,4},{4,0},{8,12},{12,8},{16,20},{20,16},{24,28},{28,24},{1,5},{5... | collective-permute-start | bytes 4423688 | tf_op jit(solution)/shard_map/ppermute | solution.py:272
  234.6 38.2 %collective-permute-start.46 = (bf16[2,2,2,48,1536]{4,3,1,0,2:T(8,128)(2,1)S(1)}, bf16[2,2,2,48,1536]{4,3,1,0,2:T(8,128)(2,1)S(1)}, u32[]{:S(2)}, u32[]{:S(2)}) collective-permute-start(bf16[2,2,2,48,1536]{4,3,1,0,2:T(8,128)(2,1)S(1)} %bitcast.322), channel_id=1, source_target_pairs={{0,2},{2,0},{1,3},{3,1},{4,6},{6,4},{5,7},{7,5},{8,10},{10,8},{9,1... | collective-permute-start | bytes 3538952 | tf_op jit(solution)/shard_map/ppermute | solution.py:38
  262.6 45.0 %collective-permute-start.24 = (bf16[1,2,1024,384]{3,2,1,0:T(8,128)(2,1)S(1)}, bf16[1,2,1024,384]{3,2,1,0:T(8,128)(2,1)S(1)}, u32[]{:S(2)}, u32[]{:S(2)}) collective-permute-start(bf16[1,2,1024,384]{3,2,1,0:T(8,128)(2,1)S(1)} %slice.182), channel_id=1, source_target_pairs={{0,2},{2,0},{1,3},{3,1},{4,6},{6,4},{5,7},{7,5},{8,10},{10,8},{9,1... | collective-permute-start | bytes 4718600 | tf_op jit(solution)/shard_map/ppermute | solution.py:38
  274.1 53.0 %collective-permute-start.47 = (bf16[2,2,48,1536]{3,2,1,0:T(8,128)(2,1)}, bf16[2,2,48,1536]{3,2,1,0:T(8,128)(2,1)}, u32[]{:S(2)}, u32[]{:S(2)}) collective-permute-start(bf16[2,2,48,1536]{3,2,1,0:T(8,128)(2,1)} %dynamic-slice_bitcast_fusion.1), channel_id=1, source_target_pairs={{0,4},{4,0},{8,12},{12,8},{16,20},{20,16},{24,28},{28,24},{1,5},{5... | collective-permute-start | bytes 1769480 | tf_op jit(solution)/shard_map/ppermute | solution.py:272
  279.2 28.4 %copy-start.12 = (bf16[1,2,2048,384]{3,2,1,0:T(8,128)(2,1)S(1)}, bf16[1,2,2048,384]{3,2,1,0:T(8,128)(2,1)}, u32[]{:S(2)}) copy-start(bf16[1,2,2048,384]{3,2,1,0:T(8,128)(2,1)} %get-tuple-element.29) | copy-start | bytes 9437188
  280.5 76.5 %collective-permute-start.42 = (bf16[2,2,48,1920]{3,2,0,1:T(8,128)(2,1)}, bf16[2,2,48,1920]{3,2,0,1:T(8,128)(2,1)}, u32[]{:S(2)}, u32[]{:S(2)}) collective-permute-start(bf16[2,2,48,1920]{3,2,0,1:T(8,128)(2,1)} %dynamic-slice_bitcast_fusion), channel_id=1, source_target_pairs={{0,16},{4,20},{8,24},{12,28},{16,0},{20,4},{24,8},{28,12},{1,17},{... | collective-permute-start | bytes 2211848 | tf_op jit(solution)/shard_map/ppermute | solution.py:272
  316.1 14.3 %collective-permute-start.36 = (bf16[2,2,2,48,512]{4,3,1,2,0:T(8,128)(2,1)S(1)}, bf16[2,2,2,48,512]{4,3,1,2,0:T(8,128)(2,1)S(1)}, u32[]{:S(2)}, u32[]{:S(2)}) collective-permute-start(bf16[2,2,2,48,512]{4,3,1,2,0:T(8,128)(2,1)S(1)} %bitcast.328), channel_id=1, source_target_pairs={{0,4},{4,0},{8,12},{12,8},{16,20},{20,16},{24,28},{28,24},{1,5},{5... | collective-permute-start | bytes 1179656 | tf_op jit(solution)/shard_map/ppermute | solution.py:272
  321.4 28.9 %collective-permute-start.31 = (bf16[2,2,2,48,640]{4,3,2,1,0:T(8,128)(2,1)S(1)}, bf16[2,2,2,48,640]{4,3,2,1,0:T(8,128)(2,1)S(1)}, u32[]{:S(2)}, u32[]{:S(2)}) collective-permute-start(bf16[2,2,2,48,640]{4,3,2,1,0:T(8,128)(2,1)S(1)} %dynamic-slice_bitcast_fusion.2), channel_id=1, source_target_pairs={{0,2},{2,0},{1,3},{3,1},{4,6},{6,4},{5,7},{7,5},{8,10},{10,8},{9,1... | collective-permute-start | bytes 1474568 | tf_op jit(solution)/shard_map/ppermute | solution.py:38
  326.9 39.5 %copy-start.11 = (bf16[1,1024,768]{2,1,0:T(8,128)(2,1)}, bf16[1,1024,768]{2,1,0:T(8,128)(2,1)S(1)}, u32[]{:S(2)}) copy-start(bf16[1,1024,768]{2,1,0:T(8,128)(2,1)S(1)} %fusion.32) | copy-start | bytes 4718596
  327.0 39.4 %collective-permute-start.25 = (bf16[1,512,768]{2,1,0:T(8,128)(2,1)S(1)}, bf16[1,512,768]{2,1,0:T(8,128)(2,1)S(1)}, u32[]{:S(2)}, u32[]{:S(2)}) collective-permute-start(bf16[1,512,768]{2,1,0:T(8,128)(2,1)S(1)} %slice.227), channel_id=1, source_target_pairs={{0,1},{1,0},{2,3},{3,2},{4,5},{5,4},{6,7},{7,6},{8,9},{9,8},{10,11... | collective-permute-start | bytes 2359304 | tf_op jit(solution)/shard_map/ppermute | solution.py:38
  328.7 21.4 %collective-permute-start.48 = (bf16[2,48,1536]{2,1,0:T(8,128)(2,1)S(1)}, bf16[2,48,1536]{2,1,0:T(8,128)(2,1)S(1)}, u32[]{:S(2)}, u32[]{:S(2)}) collective-permute-start(bf16[2,48,1536]{2,1,0:T(8,128)(2,1)S(1)} %dynamic-slice_bitcast_fusion.4), channel_id=1, source_target_pairs={{0,16},{4,20},{8,24},{12,28},{16,0},{20,4},{24,8},{28,12},{1,17},{... | collective-permute-start | bytes 884744 | tf_op jit(solution)/shard_map/ppermute | solution.py:272
  330.5 23.0 %collective-permute-start.37 = (bf16[2,2,48,512]{3,2,0,1:T(8,128)(2,1)S(1)}, bf16[2,2,48,512]{3,2,0,1:T(8,128)(2,1)S(1)}, u32[]{:S(2)}, u32[]{:S(2)}) collective-permute-start(bf16[2,2,48,512]{3,2,0,1:T(8,128)(2,1)S(1)} %dynamic-slice_bitcast_fusion.6), channel_id=1, source_target_pairs={{0,16},{4,20},{8,24},{12,28},{16,0},{20,4},{24,8},{28,12},{1,17},{... | collective-permute-start | bytes 589832 | tf_op jit(solution)/shard_map/ppermute | solution.py:272
  350.2 6.4 %collective-permute-start.49 = (bf16[48,1536]{1,0:T(8,128)(2,1)S(1)}, bf16[48,1536]{1,0:T(8,128)(2,1)S(1)}, u32[]{:S(2)}, u32[]{:S(2)}) collective-permute-start(bf16[48,1536]{1,0:T(8,128)(2,1)S(1)} %dynamic-slice_bitcast_fusion.9), channel_id=1, source_target_pairs={{0,8},{4,12},{8,0},{12,4},{16,24},{20,28},{24,16},{28,20},{1,9},{5... | collective-permute-start | bytes 442376 | tf_op jit(solution)/shard_map/ppermute | solution.py:272
  350.5 14.5 %collective-permute-start.32 = (bf16[2,2,48,640]{3,2,1,0:T(8,128)(2,1)S(1)}, bf16[2,2,48,640]{3,2,1,0:T(8,128)(2,1)S(1)}, u32[]{:S(2)}, u32[]{:S(2)}) collective-permute-start(bf16[2,2,48,640]{3,2,1,0:T(8,128)(2,1)S(1)} %dynamic-slice_bitcast_fusion.5), channel_id=1, source_target_pairs={{0,4},{4,0},{8,12},{12,8},{16,20},{20,16},{24,28},{28,24},{1,5},{5... | collective-permute-start | bytes 737288 | tf_op jit(solution)/shard_map/ppermute | solution.py:272
  353.6 4.7 %collective-permute-start.38 = (bf16[2,48,512]{2,1,0:T(8,128)(2,1)S(1)}, bf16[2,48,512]{2,1,0:T(8,128)(2,1)S(1)}, u32[]{:S(2)}, u32[]{:S(2)}) collective-permute-start(bf16[2,48,512]{2,1,0:T(8,128)(2,1)S(1)} %dynamic-slice_bitcast_fusion.12), channel_id=1, source_target_pairs={{0,2},{2,0},{1,3},{3,1},{4,6},{6,4},{5,7},{7,5},{8,10},{10,8},{9,1... | collective-permute-start | bytes 294920 | tf_op jit(solution)/shard_map/ppermute | solution.py:38
  356.6 9.1 %collective-permute-start.50 = (bf16[48,1536]{1,0:T(8,128)(2,1)S(1)}, bf16[48,1536]{1,0:T(8,128)(2,1)S(1)}, u32[]{:S(2)}, u32[]{:S(2)}) collective-permute-start(bf16[48,1536]{1,0:T(8,128)(2,1)S(1)} %fusion.64), channel_id=1, source_target_pairs={{0,2},{2,0},{1,3},{3,1},{4,6},{6,4},{5,7},{7,5},{8,10},{10,8},{9,1... | collective-permute-start | bytes 442376 | tf_op jit(solution)/shard_map/ppermute | solution.py:38
  358.4 4.2 %collective-permute-start.39 = (bf16[48,512]{1,0:T(8,128)(2,1)S(1)}, bf16[48,512]{1,0:T(8,128)(2,1)S(1)}, u32[]{:S(2)}, u32[]{:S(2)}) collective-permute-start(bf16[48,512]{1,0:T(8,128)(2,1)S(1)} %dynamic-slice_bitcast_fusion.16), channel_id=1, source_target_pairs={{0,8},{4,12},{8,0},{12,4},{16,24},{20,28},{24,16},{28,20},{1,9},{5... | collective-permute-start | bytes 147464 | tf_op jit(solution)/shard_map/ppermute | solution.py:272
  359.3 36.8 %collective-permute-start.43 = (bf16[2,48,1920]{2,1,0:T(8,128)(2,1)}, bf16[2,48,1920]{2,1,0:T(8,128)(2,1)}, u32[]{:S(2)}, u32[]{:S(2)}) collective-permute-start(bf16[2,48,1920]{2,1,0:T(8,128)(2,1)} %dynamic-slice_bitcast_fusion.3), channel_id=1, source_target_pairs={{0,2},{2,0},{1,3},{3,1},{4,6},{6,4},{5,7},{7,5},{8,10},{10,8},{9,1... | collective-permute-start | bytes 1105928 | tf_op jit(solution)/shard_map/ppermute | solution.py:38
  363.2 23.9 %collective-permute-start.40 = (bf16[48,512]{1,0:T(8,128)(2,1)}, bf16[48,512]{1,0:T(8,128)(2,1)}, u32[]{:S(2)}, u32[]{:S(2)}) collective-permute-start(bf16[48,512]{1,0:T(8,128)(2,1)} %fusion.69), channel_id=1, source_target_pairs={{0,2},{2,0},{1,3},{3,1},{4,6},{6,4},{5,7},{7,5},{8,10},{10,8},{9,1... | collective-permute-start | bytes 147464 | tf_op jit(solution)/shard_map/ppermute | solution.py:38
  365.7 24.7 %collective-permute-start.33 = (bf16[2,48,640]{2,1,0:T(8,128)(2,1)}, bf16[2,48,640]{2,1,0:T(8,128)(2,1)}, u32[]{:S(2)}, u32[]{:S(2)}) collective-permute-start(bf16[2,48,640]{2,1,0:T(8,128)(2,1)} %dynamic-slice_bitcast_fusion.11), channel_id=1, source_target_pairs={{0,16},{4,20},{8,24},{12,28},{16,0},{20,4},{24,8},{28,12},{1,17},{... | collective-permute-start | bytes 368648 | tf_op jit(solution)/shard_map/ppermute | solution.py:272
  366.4 17.7 %copy-start.9 = (f32[1,512,768]{2,1,0:T(8,128)S(1)}, f32[1,512,768]{2,1,0:T(8,128)}, u32[]{:S(2)}) copy-start(f32[1,512,768]{2,1,0:T(8,128)} %copy-done.8) | copy-start | bytes 4718596
  367.9 16.1 %copy-start.18 = (bf16[1,512,768]{2,1,0:T(8,128)(2,1)S(1)}, bf16[1,512,768]{2,1,0:T(8,128)(2,1)}, u32[]{:S(2)}) copy-start(bf16[1,512,768]{2,1,0:T(8,128)(2,1)} %copy-done.17) | copy-start | bytes 2359300
  370.4 1.8 collective-permute-start.26
  373.9 3.8 collective-permute-start.27
  377.8 4.5 %collective-permute-start.28 = (f32[2,8,128]{2,1,0:T(8,128)S(1)}, f32[2,8,128]{2,1,0:T(8,128)S(1)}, u32[]{:S(2)}, u32[]{:S(2)}) collective-permute-start(f32[2,8,128]{2,1,0:T(8,128)S(1)} %fusion.73), channel_id=1, source_target_pairs={{0,16},{4,20},{8,24},{12,28},{16,0},{20,4},{24,8},{28,12},{1,17},{... | collective-permute-start | bytes 24584 | tf_op jit(solution)/shard_map/ppermute | solution.py:272
  382.3 4.4 %collective-permute-start.29 = (f32[8,128]{1,0:T(8,128)S(1)}, f32[8,128]{1,0:T(8,128)S(1)}, u32[]{:S(2)}, u32[]{:S(2)}) collective-permute-start(f32[8,128]{1,0:T(8,128)S(1)} %fusion.76), channel_id=1, source_target_pairs={{0,8},{4,12},{8,0},{12,4},{16,24},{20,28},{24,16},{28,20},{1,9},{5... | collective-permute-start | bytes 12296 | tf_op jit(solution)/shard_map/ppermute | solution.py:272
  386.8 3.6 collective-permute-start.30
  391.3 4.7 %collective-permute-start.34 = (bf16[48,640]{1,0:T(8,128)(2,1)S(1)}, bf16[48,640]{1,0:T(8,128)(2,1)S(1)}, u32[]{:S(2)}, u32[]{:S(2)}) collective-permute-start(bf16[48,640]{1,0:T(8,128)(2,1)S(1)} %dynamic-slice_bitcast_fusion.14), channel_id=1, source_target_pairs={{0,8},{4,12},{8,0},{12,4},{16,24},{20,28},{24,16},{28,20},{1,9},{5... | collective-permute-start | bytes 184328 | tf_op jit(solution)/shard_map/ppermute | solution.py:272
  396.0 4.5 %collective-permute-start.35 = (bf16[48,640]{1,0:T(8,128)(2,1)S(1)}, bf16[48,640]{1,0:T(8,128)(2,1)S(1)}, u32[]{:S(2)}, u32[]{:S(2)}) collective-permute-start(bf16[48,640]{1,0:T(8,128)(2,1)S(1)} %fusion.68), channel_id=1, source_target_pairs={{0,2},{2,0},{1,3},{3,1},{4,6},{6,4},{5,7},{7,5},{8,10},{10,8},{9,1... | collective-permute-start | bytes 184328 | tf_op jit(solution)/shard_map/ppermute | solution.py:38
  397.3 5.6 %collective-permute-start.44 = (bf16[48,1920]{1,0:T(8,128)(2,1)S(1)}, bf16[48,1920]{1,0:T(8,128)(2,1)S(1)}, u32[]{:S(2)}, u32[]{:S(2)}) collective-permute-start(bf16[48,1920]{1,0:T(8,128)(2,1)S(1)} %dynamic-slice_bitcast_fusion.7), channel_id=1, source_target_pairs={{0,8},{4,12},{8,0},{12,4},{16,24},{20,28},{24,16},{28,20},{1,9},{5... | collective-permute-start | bytes 552968 | tf_op jit(solution)/shard_map/ppermute | solution.py:272
  403.0 5.6 %collective-permute-start.45 = (bf16[48,1920]{1,0:T(8,128)(2,1)S(1)}, bf16[48,1920]{1,0:T(8,128)(2,1)S(1)}, u32[]{:S(2)}, u32[]{:S(2)}) collective-permute-start(bf16[48,1920]{1,0:T(8,128)(2,1)S(1)} %fusion.62), channel_id=1, source_target_pairs={{0,2},{2,0},{1,3},{3,1},{4,6},{6,4},{5,7},{7,5},{8,10},{10,8},{9,1... | collective-permute-start | bytes 552968 | tf_op jit(solution)/shard_map/ppermute | solution.py:38
  (34 other events, 149.3 us)
